TPU v7x, 32 devices: a whole 2x2x4 slice. The times are simulated.
32 devices in a mesh: groups: 2 (over y), ctx: 4 (over z), tp: 2 (over x), kv: 2 (over core).
Axes of the slice: x: 2, y: 2, z: 4, core: 2. Of those that a mesh axis runs over, the one named last changes fastest.
Arguments:
- queries: bfloat16 [2048, 8192], P(('groups', 'ctx'), ('tp', 'kv')), parts along dimension 0, may hold values from -8 to 8
- key_matrix: bfloat16 [2048, 1024], P(('groups', 'ctx'), 'tp'), parts along dimension 0, may hold values from -8 to 8
- value_matrix: bfloat16 [2048, 1024], P(('groups', 'ctx'), 'tp'), parts along dimension 0, may hold values from -6 to 6
- out_grad: bfloat16 [2048, 8192], P(('groups', 'ctx'), ('tp', 'kv')), parts along dimension 0, may hold values from -6 to 6
- segments: int32 [2048], P(('groups', 'ctx')), parts along dimension 0, may hold values from 0 to 15, never falling along the last dimension, each value on 1 to 512 neighbouring positions
Outputs:
- query_grad: bfloat16 [2048, 8192], P(('groups', 'ctx'), ('tp', 'kv')), parts along dimension 0
- key_gradient: bfloat16 [2048, 1024], P(('groups', 'ctx'), 'tp'), parts along dimension 0
- value_gradient: bfloat16 [2048, 1024], P(('groups', 'ctx'), 'tp'), parts along dimension 0
There are 2 independent parts, one for each index of `groups`. A program takes and returns all parts, laid end to end along the dimension named above; each array names one. Nothing has to cross between parts.
Inputs may be any that keep to these rules, and one draw needn't show every extreme that they name: `segments`: document numbers never fall along the sequence; each of the 16 documents has 1 or more positions and one document holds exactly half of the 1024 positions.
All inputs are finite; a program needn't handle non-finite values.
Results may differ from a plain program's by a relative error of at most 0.011.
Values may be sent and summed in bfloat16 or wider, within the bound.
No kernel may reach another device: no remote copies, remote signals or barrier semaphores. Data moves between devices by JAX's collectives and lax.ppermute only.
A program may use at most 64 MiB of HBM per device.

v0:
```python
import jax
import jax.numpy as jnp
from jax import lax
from jax.sharding import PartitionSpec as P

QUERY_HEADS = 64
KEY_VALUE_HEADS = 8
HEAD_SIZE = 128
BLOCK = 128


FILL_LOW = -1e30


def from_behind(array, axis, by):
    count = lax.axis_size(axis)
    return lax.ppermute(array, axis, [(i, (i + by) % count) for i in range(count)])


def swapped(block, axis, apart):
    count = lax.axis_size(axis)
    route = []
    for low in range(count):
        high = low | 1 << apart
        if high != low and high < count:
            route += [(low, high), (high, low)]
    return lax.ppermute(block, axis, route)


def block_scores(row_block, key_block, groups):
    row_count = row_block.shape[0]
    key_count = key_block.shape[0]
    row_view = row_block.reshape(row_count, groups, -1, HEAD_SIZE)
    key_view = key_block.reshape(key_count, groups, HEAD_SIZE)
    scores = jnp.einsum("qgpd,kgd->gpqk", row_view, key_view, preferred_element_type=jnp.float32)
    return scores.reshape(-1, row_count, key_count)


def key_mask(seg_all, q_pos, q_seg, k_first, key_count):
    k_pos = k_first + jnp.arange(key_count, dtype=jnp.int32)
    k_seg = lax.dynamic_slice_in_dim(seg_all, k_first, key_count)
    allowed = (q_seg[:, None] == k_seg[None, :]) & (k_pos[None, :] <= q_pos[:, None])
    active = k_first <= jnp.max(q_pos)
    return (allowed, active)


def stats_update(state_now, query_rows, grad_rows, key_value, allowed, groups, logit_scale):
    peak_old, total_old, weighted_old = state_now
    logits = block_scores(query_rows, key_value[0], groups) * logit_scale
    dprobs = block_scores(grad_rows, key_value[1], groups)
    masked = jnp.where(allowed[None], logits, FILL_LOW)
    peak_new = jnp.maximum(peak_old, jnp.max(masked, axis=-1))
    weights = jnp.where(allowed[None], jnp.exp(masked - peak_new[:, :, None]), 0.0)
    fade = jnp.exp(peak_old - peak_new)
    return (
        peak_new,
        total_old * fade + jnp.sum(weights, axis=-1),
        weighted_old * fade + jnp.sum(weights * dprobs, axis=-1),
    )


def grads_update(query_rows, grad_rows, key_value, allowed, log_total, deltas, groups, logit_scale):
    row_count = query_rows.shape[0]
    key_count = key_value.shape[1]
    logits = block_scores(query_rows, key_value[0], groups) * logit_scale
    dprobs = block_scores(grad_rows, key_value[1], groups)
    shifted = jnp.where(allowed[None], logits - log_total[:, :, None], FILL_LOW)
    probs = jnp.where(allowed[None], jnp.exp(shifted), 0.0)
    dlogits = probs * (dprobs - deltas[:, :, None])
    probs_low = probs.astype(jnp.bfloat16).reshape(groups, -1, row_count, key_count)
    dlogits_low = dlogits.astype(jnp.bfloat16).reshape(groups, -1, row_count, key_count)
    query_view = query_rows.reshape(row_count, groups, -1, HEAD_SIZE)
    grad_view = grad_rows.reshape(row_count, groups, -1, HEAD_SIZE)
    key_view = key_value[0].reshape(key_count, groups, HEAD_SIZE)
    query_term = jnp.einsum(
        "gpqk,kgd->gpqd", dlogits_low, key_view, preferred_element_type=jnp.float32
    )
    key_term = jnp.einsum(
        "gpqk,qgpd->kgd", dlogits_low, query_view, preferred_element_type=jnp.float32
    )
    value_term = jnp.einsum(
        "gpqk,qgpd->kgd", probs_low, grad_view, preferred_element_type=jnp.float32
    )
    return (
        query_term.reshape(-1, row_count, HEAD_SIZE),
        jnp.stack([key_term.reshape(key_count, -1), value_term.reshape(key_count, -1)]),
    )


def visit_stats(
    stats_now, query_rows, grad_rows, q_pos, q_seg, key_value, k_first, seg_all, groups, logit_scale
):
    allowed, active = key_mask(seg_all, q_pos, q_seg, k_first, key_value.shape[1])

    def advance(state_in):
        return stats_update(
            state_in, query_rows, grad_rows, key_value, allowed, groups, logit_scale
        )

    def remain(state_in):
        return state_in

    return lax.cond(active, advance, remain, stats_now)


def visit_grads(
    acc_now,
    kv_grad,
    query_rows,
    grad_rows,
    q_pos,
    q_seg,
    log_total,
    deltas,
    key_value,
    k_first,
    seg_all,
    groups,
    logit_scale,
):
    allowed, active = key_mask(seg_all, q_pos, q_seg, k_first, key_value.shape[1])

    def advance(state_in):
        query_term, kv_term = grads_update(
            query_rows, grad_rows, key_value, allowed, log_total, deltas, groups, logit_scale
        )
        return (state_in[0] + query_term, state_in[1] + kv_term)

    def remain(state_in):
        return state_in

    return lax.cond(active, advance, remain, (acc_now, kv_grad))


def pass_forward(kv_grad):
    return from_behind(kv_grad, "ctx", 1)


def mirror_inputs(stacked, level_list):
    for bit_number in range(level_list):
        stacked = swapped(stacked, "ctx", bit_number)
    return stacked


def mirror_result(block_grad, level_list):
    for bit_number in range(level_list):
        block_grad = swapped(block_grad, "ctx", bit_number)
    return block_grad


def finish_stats(stats_end):
    return (stats_end[0] + jnp.log(stats_end[1]), stats_end[2] / stats_end[1])


def shards(queries, key_matrix, value_matrix, out_grad, segments):
    cycle_size = lax.axis_size("ctx")
    rank_self = lax.axis_index("ctx")
    level_list = cycle_size.bit_length() - 1
    block_count = queries.shape[0] // BLOCK
    head_count = queries.shape[1] // HEAD_SIZE
    group_width = QUERY_HEADS // KEY_VALUE_HEADS
    kv_count = max(head_count // group_width, 1)
    kv_first = lax.axis_index("kv") * head_count // group_width
    logit_scale = HEAD_SIZE ** (-0.5)
    rows_here = block_count * BLOCK
    kept_rows = rows_here - BLOCK
    seg_all = lax.all_gather(segments, "ctx", axis=0, tiled=True)
    arrived = mirror_inputs(jnp.stack([queries[kept_rows:], out_grad[kept_rows:]]), level_list)
    query_rows = jnp.concatenate([queries[:kept_rows], arrived[0]], axis=0)
    grad_rows = jnp.concatenate([out_grad[:kept_rows], arrived[1]], axis=0)
    offsets = jnp.arange(BLOCK, dtype=jnp.int32)
    moved_first = ((cycle_size - 1 - rank_self) * block_count + block_count - 1) * BLOCK
    q_pos = jnp.concatenate(
        [rank_self * rows_here + jnp.arange(kept_rows, dtype=jnp.int32), moved_first + offsets]
    )
    q_seg = jnp.concatenate(
        [
            lax.dynamic_slice_in_dim(seg_all, rank_self * rows_here, kept_rows),
            lax.dynamic_slice_in_dim(seg_all, moved_first, BLOCK),
        ]
    )
    key_value = jnp.stack(
        [
            lax.dynamic_slice_in_dim(key_matrix, kv_first * HEAD_SIZE, kv_count * HEAD_SIZE, 1),
            lax.dynamic_slice_in_dim(value_matrix, kv_first * HEAD_SIZE, kv_count * HEAD_SIZE, 1),
        ]
    )
    start_stats = (
        jnp.full((head_count, rows_here), FILL_LOW, jnp.float32),
        jnp.zeros((head_count, rows_here), jnp.float32),
        jnp.zeros((head_count, rows_here), jnp.float32),
    )
    start_acc = jnp.zeros((head_count, rows_here, HEAD_SIZE), jnp.float32)

    def see_stats(stats_now, part_kv, k_first):
        return visit_stats(
            stats_now,
            query_rows,
            grad_rows,
            q_pos,
            q_seg,
            part_kv,
            k_first,
            seg_all,
            kv_count,
            logit_scale,
        )

    def see_grads(acc_now, kv_grad, part_kv, k_first, log_total, deltas):
        return visit_grads(
            acc_now,
            kv_grad,
            query_rows,
            grad_rows,
            q_pos,
            q_seg,
            log_total,
            deltas,
            part_kv,
            k_first,
            seg_all,
            kv_count,
            logit_scale,
        )

    stats_now = see_stats(start_stats, key_value, rank_self * rows_here)

    def fwd_turn(turn_index, state_now):
        moving, stats_in = state_now
        moving = from_behind(moving, "ctx", 1)
        anchor = (rank_self - turn_index) % cycle_size
        return (moving, see_stats(stats_in, moving, anchor * rows_here))

    log_total, deltas = finish_stats(
        lax.fori_loop(1, cycle_size, fwd_turn, (key_value, stats_now))[1]
    )
    empty_grad = jnp.zeros((2, rows_here, kv_count * HEAD_SIZE), jnp.float32)
    grad_acc, kv_grad = see_grads(
        start_acc, empty_grad, key_value, rank_self * rows_here, log_total, deltas
    )

    def back_turn(turn_index, state_now):
        moving, kv_now, acc_now = state_now
        moving = from_behind(moving, "ctx", 1)
        kv_now = pass_forward(kv_now)
        anchor = (rank_self - turn_index) % cycle_size
        acc_now, kv_now = see_grads(acc_now, kv_now, moving, anchor * rows_here, log_total, deltas)
        return (moving, kv_now, acc_now)

    loop_end = lax.fori_loop(1, cycle_size, back_turn, (key_value, kv_grad, grad_acc))
    grad_acc = loop_end[2]
    key_value_grad = pass_forward(loop_end[1])
    grad_full = jnp.zeros((2, rows_here, key_matrix.shape[1]), jnp.float32)
    grad_full = lax.dynamic_update_slice_in_dim(grad_full, key_value_grad, kv_first * HEAD_SIZE, 2)
    summed = lax.psum(grad_full.astype(jnp.bfloat16), "kv").astype(jnp.float32)
    key_gradient = (summed[0] * logit_scale).astype(jnp.bfloat16)
    value_gradient = summed[1].astype(jnp.bfloat16)
    query_all = (
        (grad_acc * logit_scale)
        .astype(jnp.bfloat16)
        .transpose(1, 0, 2)
        .reshape(rows_here, head_count * HEAD_SIZE)
    )
    returned = mirror_result(query_all[kept_rows:], level_list)
    return (
        jnp.concatenate([query_all[:kept_rows], returned], axis=0),
        key_gradient,
        value_gradient,
    )


def solution(mesh):
    return jax.shard_map(
        shards,
        mesh=mesh,
        in_specs=(
            P(("groups", "ctx"), ("tp", "kv")),
            P(("groups", "ctx"), "tp"),
            P(("groups", "ctx"), "tp"),
            P(("groups", "ctx"), ("tp", "kv")),
            P(("groups", "ctx")),
        ),
        out_specs=(
            P(("groups", "ctx"), ("tp", "kv")),
            P(("groups", "ctx"), "tp"),
            P(("groups", "ctx"), "tp"),
        ),
        check_vma=False,
    )
```

profile of v0, /device:TPU:0, one launch (start us, length us, event | category | flops | bytes accessed | tf_op | source)
XLA Modules:
  0.0 299.9 jit_solution(5921494750152145410)
XLA Ops:
  11.4 3.0 %collective-permute-start.3 = (bf16[2,128,2048]{1,2,0:T(8,128)(2,1)}, bf16[2,128,2048]{1,2,0:T(8,128)(2,1)}, u32[]{:S(2)}, u32[]{:S(2)}) collective-permute-start(bf16[2,128,2048]{1,2,0:T(8,128)(2,1)} %pad_maximum_fusion.1), channel_id=1, source_target_pairs={{0,4},{4,0},{8,12},{12,8},{1,5},{5,1},{9,13},{13,9},{2,6},{6,2},{1... | collective-permute-start | bytes 3145736 | tf_op jit(solution)/shard_map/ppermute | solution.py:27
  14.4 23.5 %collective-permute-done.3 = bf16[2,128,2048]{1,2,0:T(8,128)(2,1)} collective-permute-done((bf16[2,128,2048]{1,2,0:T(8,128)(2,1)}, bf16[2,128,2048]{1,2,0:T(8,128)(2,1)}, u32[]{:S(2)}, u32[]{:S(2)}) %collective-permute-start.3) | collective-permute-done | bytes 1048608 | tf_op jit(solution)/shard_map/ppermute | solution.py:27
  37.9 2.8 collective-permute-start.4
  44.9 23.5 %all-gather = s32[4,1,256]{2,1,0:T(1,128)S(1)} all-gather(s32[1,1,256]{2,1,0:T(1,128)S(1)} %bitcast.244), channel_id=1, replica_groups=mesh['groups'=2,'ctx'=4,'tp'=2,'kv'=2] {'ctx'}, dimensions={0}, use_global_device_ids=true | all-gather | bytes 5120 | tf_op jit(solution)/shard_map/all_gather | solution.py:167
  69.6 16.4 %collective-permute-done.4 = bf16[2,128,2048]{1,2,0:T(8,128)(2,1)} collective-permute-done((bf16[2,128,2048]{1,2,0:T(8,128)(2,1)}, bf16[2,128,2048]{1,2,0:T(8,128)(2,1)}, u32[]{:S(2)}, u32[]{:S(2)}) %collective-permute-start.4) | collective-permute-done | bytes 1048608 | tf_op jit(solution)/shard_map/ppermute | solution.py:27
  90.6 11.5 %conditional.4 = (f32[16,256]{1,0:T(8,128)}, f32[16,256]{1,0:T(8,128)S(1)}, f32[16,256]{1,0:T(8,128)}) conditional(s32[]{:T(128)} %convert_element_type.59, () %tuple.93, (pred[256,256]{0,1:T(8,128)(4,1)S(1)}, bf16[256,256]{1,0:T(8,128)(2,1)S(1)}, bf16[256,2048]{0,1:T(8,128)(2,1)S(1)}, bf16[256,256]{1,0:T(8,128)(2,1)S(1)}, ...), branch_computations={%region_2.3_spmd, %region_3.7_spmd} | conditional | flops 551571456 | bytes 32669748 | solution.py:103
  91.3 3.7 %fusion.1 = (f32[2,8,256]{2,1,0:T(8,128)S(1)}, f32[2,256,256,8]{2,1,3,0:T(8,128)}) fusion(pred[256,256]{0,1:T(8,128)(4,1)S(1)} %get-tuple-element.740, bf16[256,2,8,128]{0,3,2,1:T(8,128)(2,1)S(1)} %bitcast.196, bf16[256,2,128,1]{2,1,0,3:T(2,128)(2,1)} %bitcast.226), kind=kOutput, calls=%fused_computation.4 | convolution fusion | flops 271577088 | bytes 5455872 | tf_op jit(solution)/shard_map/cond/branch_1_fun/qgpd,kgd->gpqk/dot_general | solution.py:35
  95.7 4.1 %fusion = f32[2,8,256]{2,1,0:T(8,128)S(1)} fusion(f32[2,256,256,8]{2,1,3,0:T(8,128)} %get-tuple-element.942, bf16[256,2,8,128]{0,3,2,1:T(8,128)(2,1)} %bitcast.213, f32[2,8,256]{2,1,0:T(8,128)S(1)} %broadcast_maximum_fusion, pred[256,256]{0,1:T(8,128)(4,1)S(1)} %get-tuple-element.740, bf16[256,2,128,1]{2,1,0,3:T(2,128)(2,1)} %bitcast.231), kind=kOutput, calls=%fused_computation.1 | convolution fusion | flops 274722816 | bytes 5472256 | tf_op jit(solution)/shard_map/cond/branch_1_fun/qgpd,kgd->gpqk/dot_general | solution.py:35
  102.2 60.1 %while.40 = (s32[]{:T(128)}, bf16[2,256,256]{1,2,0:T(8,128)(2,1)}, f32[16,256]{1,0:T(8,128)}, f32[16,256]{1,0:T(8,128)S(1)}, f32[16,256]{1,0:T(8,128)}, /*index=...) while((s32[]{:T(128)}, bf16[2,256,256]{1,2,0:T(8,128)(2,1)}, ...), condition=%wide.region_13.14_spmd, body=%wide.region_7.13_spmd.sunk | while | flops 551760128 | bytes 21800464 | solution.py:235
  102.2 3.0 %collective-permute-start = (bf16[2,256,256]{1,2,0:T(8,128)(2,1)}, bf16[2,256,256]{1,2,0:T(8,128)(2,1)S(1)}, u32[]{:S(2)}, u32[]{:S(2)}) collective-permute-start(bf16[2,256,256]{1,2,0:T(8,128)(2,1)} %get-tuple-element.1159), channel_id=1, source_target_pairs={{0,4},{4,8},{8,12},{12,0},{1,5},{5,9},{9,13},{13,1},{2,6},{6,10},{... | collective-permute-start | bytes 786440 | tf_op jit(solution)/shard_map/while/body/eval_jaxpr/ppermute | solution.py:17
  105.2 9.1 %collective-permute-done = bf16[2,256,256]{1,2,0:T(8,128)(2,1)S(1)} collective-permute-done((bf16[2,256,256]{1,2,0:T(8,128)(2,1)}, bf16[2,256,256]{1,2,0:T(8,128)(2,1)S(1)}, u32[]{:S(2)}, u32[]{:S(2)}) %collective-permute-start) | collective-permute-done | bytes 262176 | tf_op jit(solution)/shard_map/while/body/eval_jaxpr/ppermute | solution.py:17
  114.9 9.1 %conditional.8 = ((f32[16,256]{1,0:T(8,128)}, f32[16,256]{1,0:T(8,128)S(1)}, f32[16,256]{1,0:T(8,128)})) conditional(s32[]{:T(128)} %convert_element_type.79, (f32[16,256]{1,0:T(8,128)}, f32[16,256]{1,0:T(8,128)S(1)}, f32[16,256]{1,0:T(8,128)}) %tuple.140, (s32[256]{0:T(256)}, s32[]{:T(128)}, s32[1024]{0:T(1024)}, s32[1,256]{1,0:T(1,128)}, ...), branch_computations={%region_8.8_spmd, %region_9.12_spmd} | conditional | flops 551760128 | bytes 20226122 | solution.py:103
  124.7 8.4 %collective-permute-done = bf16[2,256,256]{1,2,0:T(8,128)(2,1)S(1)} collective-permute-done((bf16[2,256,256]{1,2,0:T(8,128)(2,1)}, bf16[2,256,256]{1,2,0:T(8,128)(2,1)S(1)}, u32[]{:S(2)}, u32[]{:S(2)}) %collective-permute-start) | collective-permute-done | bytes 262176 | tf_op jit(solution)/shard_map/while/body/eval_jaxpr/ppermute | solution.py:17
  133.7 9.1 %conditional.8 = ((f32[16,256]{1,0:T(8,128)}, f32[16,256]{1,0:T(8,128)S(1)}, f32[16,256]{1,0:T(8,128)})) conditional(s32[]{:T(128)} %convert_element_type.79, (f32[16,256]{1,0:T(8,128)}, f32[16,256]{1,0:T(8,128)S(1)}, f32[16,256]{1,0:T(8,128)}) %tuple.140, (s32[256]{0:T(256)}, s32[]{:T(128)}, s32[1024]{0:T(1024)}, s32[1,256]{1,0:T(1,128)}, ...), branch_computations={%region_8.8_spmd, %region_9.12_spmd} | conditional | flops 551760128 | bytes 20226122 | solution.py:103
  143.5 8.4 %collective-permute-done = bf16[2,256,256]{1,2,0:T(8,128)(2,1)S(1)} collective-permute-done((bf16[2,256,256]{1,2,0:T(8,128)(2,1)}, bf16[2,256,256]{1,2,0:T(8,128)(2,1)S(1)}, u32[]{:S(2)}, u32[]{:S(2)}) %collective-permute-start) | collective-permute-done | bytes 262176 | tf_op jit(solution)/shard_map/while/body/eval_jaxpr/ppermute | solution.py:17
  152.4 9.1 %conditional.8 = ((f32[16,256]{1,0:T(8,128)}, f32[16,256]{1,0:T(8,128)S(1)}, f32[16,256]{1,0:T(8,128)})) conditional(s32[]{:T(128)} %convert_element_type.79, (f32[16,256]{1,0:T(8,128)}, f32[16,256]{1,0:T(8,128)S(1)}, f32[16,256]{1,0:T(8,128)}) %tuple.140, (s32[256]{0:T(256)}, s32[]{:T(128)}, s32[1024]{0:T(1024)}, s32[1,256]{1,0:T(1,128)}, ...), branch_computations={%region_8.8_spmd, %region_9.12_spmd} | conditional | flops 551760128 | bytes 20226122 | solution.py:103
  163.0 11.5 %conditional.5 = (f32[16,256,128]{2,1,0:T(8,128)S(1)}, f32[2,256,256]{1,2,0:T(8,128)}) conditional(s32[]{:T(128)} %convert_element_type.59, () %tuple.92, (pred[256,256]{0,1:T(8,128)(4,1)}, bf16[256,256]{1,0:T(8,128)(2,1)}, bf16[256,2048]{0,1:T(8,128)(2,1)S(1)}, f32[16,256]{1,0:T(8,128)S(1)}, bf16[256,256]{1,0:T(8,128)(2,1)S(1)}, ...), branch_computations={%region_14.15_spmd, %region_15.16_spmd} | conditional | flops 1354891264 | bytes 49070180 | solution.py:132
  164.3 2.7 fusion.25
  167.0 3.8 %fusion.14 = bf16[2,8,256,256]{2,3,1,0:T(8,128)(2,1)S(1)} fusion(f32[2,256,256,8]{2,1,3,0:T(8,128)} %fusion.25, bf16[256,2,8,128]{0,3,2,1:T(8,128)(2,1)S(1)} %bitcast.214, f32[2,8,256]{2,1,0:T(8,128)S(1)} %bitcast.238, f32[2,8,256]{2,1,0:T(8,128)S(1)} %bitcast.240, pred[256,256]{0,1:T(8,128)(4,1)S(1)} %copy-done.7, bf16[256,2,128,1]{2,1,0,3:T(2,128)(2,1)S(1)} %bitcast.232), kind=kOutput, calls=%fused_computation.31 | convolution fusion | flops 275775488 | bytes 7569408 | tf_op jit(solution)/shard_map/cond/branch_1_fun/qgpd,kgd->gpqk/dot_general | solution.py:35
  174.6 83.3 %while.41 = (s32[]{:T(128)}, bf16[2,256,256]{1,2,0:T(8,128)(2,1)}, f32[2,256,256]{1,2,0:T(8,128)}, f32[16,256,128]{2,1,0:T(8,128)S(1)}, s32[]{:T(128)}, /*index=...) while((s32[]{:T(128)}, bf16[2,256,256]{1,2,0:T(8,128)(2,1)}, ...), condition=%wide.region_19.20_spmd, body=%wide.region_16.19_spmd.sunk | while | flops 1355743488 | bytes 43640408 | solution.py:250
  174.8 17.2 %collective-permute-done.1 = bf16[2,256,256]{1,2,0:T(8,128)(2,1)S(1)} collective-permute-done((bf16[2,256,256]{1,2,0:T(8,128)(2,1)}, bf16[2,256,256]{1,2,0:T(8,128)(2,1)S(1)}, u32[]{:S(2)}, u32[]{:S(2)}) %collective-permute-start.1) | collective-permute-done | bytes 262176 | tf_op jit(solution)/shard_map/while/body/eval_jaxpr/ppermute | solution.py:17
  192.7 8.6 %conditional.9 = ((f32[16,256,128]{2,1,0:T(8,128)S(1)}, f32[2,256,256]{1,2,0:T(8,128)})) conditional(s32[]{:T(128)} %convert_element_type.80, (f32[16,256,128]{2,1,0:T(8,128)S(1)}, f32[2,256,256]{1,2,0:T(8,128)}) %tuple.143, (s32[256]{0:T(256)S(1)}, s32[]{:T(128)}, s32[1024]{0:T(1024)}, s32[1,256]{1,0:T(1,128)S(1)}, s32[256]{0:T(256)S(1)}, ...), branch_computations={%region_17.17_spmd, %region_18.18_spmd} | conditional | flops 1355743488 | bytes 38920288 | solution.py:132
  203.2 16.5 %collective-permute-done.1 = bf16[2,256,256]{1,2,0:T(8,128)(2,1)S(1)} collective-permute-done((bf16[2,256,256]{1,2,0:T(8,128)(2,1)}, bf16[2,256,256]{1,2,0:T(8,128)(2,1)S(1)}, u32[]{:S(2)}, u32[]{:S(2)}) %collective-permute-start.1) | collective-permute-done | bytes 262176 | tf_op jit(solution)/shard_map/while/body/eval_jaxpr/ppermute | solution.py:17
  220.4 8.6 %conditional.9 = ((f32[16,256,128]{2,1,0:T(8,128)S(1)}, f32[2,256,256]{1,2,0:T(8,128)})) conditional(s32[]{:T(128)} %convert_element_type.80, (f32[16,256,128]{2,1,0:T(8,128)S(1)}, f32[2,256,256]{1,2,0:T(8,128)}) %tuple.143, (s32[256]{0:T(256)S(1)}, s32[]{:T(128)}, s32[1024]{0:T(1024)}, s32[1,256]{1,0:T(1,128)S(1)}, s32[256]{0:T(256)S(1)}, ...), branch_computations={%region_17.17_spmd, %region_18.18_spmd} | conditional | flops 1355743488 | bytes 38920288 | solution.py:132
  225.7 1.9 maximum_add_fusion
  230.9 15.7 %collective-permute-done.1 = bf16[2,256,256]{1,2,0:T(8,128)(2,1)S(1)} collective-permute-done((bf16[2,256,256]{1,2,0:T(8,128)(2,1)}, bf16[2,256,256]{1,2,0:T(8,128)(2,1)S(1)}, u32[]{:S(2)}, u32[]{:S(2)}) %collective-permute-start.1) | collective-permute-done | bytes 262176 | tf_op jit(solution)/shard_map/while/body/eval_jaxpr/ppermute | solution.py:17
  247.3 8.6 %conditional.9 = ((f32[16,256,128]{2,1,0:T(8,128)S(1)}, f32[2,256,256]{1,2,0:T(8,128)})) conditional(s32[]{:T(128)} %convert_element_type.80, (f32[16,256,128]{2,1,0:T(8,128)S(1)}, f32[2,256,256]{1,2,0:T(8,128)}) %tuple.143, (s32[256]{0:T(256)S(1)}, s32[]{:T(128)}, s32[1024]{0:T(1024)}, s32[1,256]{1,0:T(1,128)S(1)}, s32[256]{0:T(256)S(1)}, ...), branch_computations={%region_17.17_spmd, %region_18.18_spmd} | conditional | flops 1355743488 | bytes 38920288 | solution.py:132
  259.7 8.9 %collective-permute-done.7 = bf16[2,256,256]{2,1,0:T(8,128)(2,1)S(1)} collective-permute-done((bf16[2,256,256]{2,1,0:T(8,128)(2,1)S(1)}, bf16[2,256,256]{2,1,0:T(8,128)(2,1)S(1)}, u32[]{:S(2)}, u32[]{:S(2)}) %collective-permute-start.7) | collective-permute-done | bytes 262176 | tf_op jit(solution)/shard_map/ppermute | solution.py:17
  269.5 7.0 %collective-permute-done.5 = bf16[128,2048]{1,0:T(8,128)(2,1)S(1)} collective-permute-done((bf16[128,2048]{1,0:T(8,128)(2,1)S(1)}, bf16[128,2048]{1,0:T(8,128)(2,1)S(1)}, u32[]{:S(2)}, u32[]{:S(2)}) %collective-permute-start.5) | collective-permute-done | bytes 524320 | tf_op jit(solution)/shard_map/ppermute | solution.py:27
  276.4 3.8 %collective-permute-start.6 = (bf16[128,2048]{1,0:T(8,128)(2,1)S(1)}, bf16[128,2048]{1,0:T(8,128)(2,1)S(1)}, u32[]{:S(2)}, u32[]{:S(2)}) collective-permute-start(bf16[128,2048]{1,0:T(8,128)(2,1)S(1)} %collective-permute-done.5), channel_id=1, source_target_pairs={{0,8},{8,0},{4,12},{12,4},{1,9},{9,1},{5,13},{13,5},{2,10},{10,2},... | collective-permute-start | bytes 1572872 | tf_op jit(solution)/shard_map/ppermute | solution.py:27
  280.3 6.3 %all-reduce.2.cloned.1.call-done = bf16[2,256,512]{2,1,0:T(8,128)(2,1)} async-done(((bf16[2,256,512]{2,1,0:T(8,128)(2,1)}), bf16[2,256,512]{2,1,0:T(8,128)(2,1)}) %all-reduce.2.cloned.1.call-update) | async-done | bytes 524304 | tf_op jit(solution)/shard_map/psum | solution.py:255
  290.0 2.0 collective-permute-done.6
  (183 shorter events, 92.0 us)
Async XLA Ops:
  7.2 279.5 %all-reduce.2.cloned.1.call-start = ((), (), s32[]{:S(2)}) async-start(), calls=%async_computation | async-start | bytes 1048576 | tf_op jit(solution)/shard_map/psum | solution.py:255
  8.5 35.3 %copy-start.13 = (bf16[256,512]{1,0:T(8,128)(2,1)S(1)}, bf16[256,512]{1,0:T(8,128)(2,1)}, u32[]{:S(2)}) copy-start(bf16[256,512]{1,0:T(8,128)(2,1)} %param.19) | copy-start | bytes 786436
  8.5 35.3 %copy-start.14 = (bf16[256,512]{1,0:T(8,128)(2,1)S(1)}, bf16[256,512]{1,0:T(8,128)(2,1)}, u32[]{:S(2)}) copy-start(bf16[256,512]{1,0:T(8,128)(2,1)} %param.18) | copy-start | bytes 786436
  10.1 34.8 %copy-start.16 = (s32[256]{0:T(256)S(1)}, s32[256]{0:T(256)}, u32[]{:S(2)}) copy-start(s32[256]{0:T(256)} %param.21) | copy-start | bytes 3076
  11.4 26.5 %collective-permute-start.3 = (bf16[2,128,2048]{1,2,0:T(8,128)(2,1)}, bf16[2,128,2048]{1,2,0:T(8,128)(2,1)}, u32[]{:S(2)}, u32[]{:S(2)}) collective-permute-start(bf16[2,128,2048]{1,2,0:T(8,128)(2,1)} %pad_maximum_fusion.1), channel_id=1, source_target_pairs={{0,4},{4,0},{8,12},{12,8},{1,5},{5,1},{9,13},{13,9},{2,6},{6,2},{1... | collective-permute-start | bytes 3145736 | tf_op jit(solution)/shard_map/ppermute | solution.py:27
  37.9 48.1 %collective-permute-start.4 = (bf16[2,128,2048]{1,2,0:T(8,128)(2,1)}, bf16[2,128,2048]{1,2,0:T(8,128)(2,1)}, u32[]{:S(2)}, u32[]{:S(2)}) collective-permute-start(bf16[2,128,2048]{1,2,0:T(8,128)(2,1)} %collective-permute-done.3), channel_id=1, source_target_pairs={{0,8},{8,0},{4,12},{12,4},{1,9},{9,1},{5,13},{13,5},{2,10},{10,2},... | collective-permute-start | bytes 3145736 | tf_op jit(solution)/shard_map/ppermute | solution.py:27
  43.9 46.8 %copy-start.4 = (bf16[256,256]{1,0:T(8,128)(2,1)}, bf16[256,256]{1,0:T(8,128)(2,1)S(1)}, u32[]{:S(2)}) copy-start(bf16[256,256]{1,0:T(8,128)(2,1)S(1)} %get-tuple-element.956) | copy-start | bytes 393220
  44.1 25.0 %copy-start.8 = (bf16[2,256,256]{1,2,0:T(8,128)(2,1)}, bf16[2,256,256]{1,2,0:T(8,128)(2,1)S(1)}, u32[]{:S(2)}) copy-start(bf16[2,256,256]{1,2,0:T(8,128)(2,1)S(1)} %pad_maximum_fusion.5) | copy-start | bytes 786436
  68.4 0.6 copy-start.15
  69.6 21.0 %copy-start.6 = (pred[256,256]{0,1:T(8,128)(4,1)}, pred[256,256]{0,1:T(8,128)(4,1)S(1)}, u32[]{:S(2)}) copy-start(pred[256,256]{0,1:T(8,128)(4,1)S(1)} %compare_and_fusion.2) | copy-start | bytes 196612
  95.7 4.7 %copy-start = (f32[2,256,256,8]{2,1,3,0:T(8,128)S(1)}, f32[2,256,256,8]{2,1,3,0:T(8,128)}, u32[]{:S(2)}) copy-start(f32[2,256,256,8]{2,1,3,0:T(8,128)} %get-tuple-element.942) | copy-start | bytes 12582916 | tf_op jit(solution)/shard_map/cond
  102.2 12.1 %collective-permute-start = (bf16[2,256,256]{1,2,0:T(8,128)(2,1)}, bf16[2,256,256]{1,2,0:T(8,128)(2,1)S(1)}, u32[]{:S(2)}, u32[]{:S(2)}) collective-permute-start(bf16[2,256,256]{1,2,0:T(8,128)(2,1)} %get-tuple-element.1159), channel_id=1, source_target_pairs={{0,4},{4,8},{8,12},{12,0},{1,5},{5,9},{9,13},{13,1},{2,6},{6,10},{... | collective-permute-start | bytes 786440 | tf_op jit(solution)/shard_map/while/body/eval_jaxpr/ppermute | solution.py:17
  124.7 8.4 %collective-permute-start = (bf16[2,256,256]{1,2,0:T(8,128)(2,1)}, bf16[2,256,256]{1,2,0:T(8,128)(2,1)S(1)}, u32[]{:S(2)}, u32[]{:S(2)}) collective-permute-start(bf16[2,256,256]{1,2,0:T(8,128)(2,1)} %get-tuple-element.1159), channel_id=1, source_target_pairs={{0,4},{4,8},{8,12},{12,0},{1,5},{5,9},{9,13},{13,1},{2,6},{6,10},{... | collective-permute-start | bytes 786440 | tf_op jit(solution)/shard_map/while/body/eval_jaxpr/ppermute | solution.py:17
  143.5 8.4 %collective-permute-start = (bf16[2,256,256]{1,2,0:T(8,128)(2,1)}, bf16[2,256,256]{1,2,0:T(8,128)(2,1)S(1)}, u32[]{:S(2)}, u32[]{:S(2)}) collective-permute-start(bf16[2,256,256]{1,2,0:T(8,128)(2,1)} %get-tuple-element.1159), channel_id=1, source_target_pairs={{0,4},{4,8},{8,12},{12,0},{1,5},{5,9},{9,13},{13,1},{2,6},{6,10},{... | collective-permute-start | bytes 786440 | tf_op jit(solution)/shard_map/while/body/eval_jaxpr/ppermute | solution.py:17
  163.0 11.6 %copy-start.10 = (s32[256]{0:T(256)S(1)}, s32[256]{0:T(256)}, u32[]{:S(2)}) copy-start(s32[256]{0:T(256)} %get-tuple-element.1266) | copy-start | bytes 3076
  163.0 11.6 %copy-start.12 = (s32[256]{0:T(256)S(1)}, s32[256]{0:T(256)}, u32[]{:S(2)}) copy-start(s32[256]{0:T(256)} %get-tuple-element.1267) | copy-start | bytes 3076
  163.2 3.7 %copy-start.2 = (bf16[256,2048]{0,1:T(8,128)(2,1)S(1)}, bf16[256,2048]{0,1:T(8,128)(2,1)}, u32[]{:S(2)}) copy-start(bf16[256,2048]{0,1:T(8,128)(2,1)} %get-tuple-element.777) | copy-start | bytes 3145732 | tf_op jit(solution)/shard_map/cond
  163.2 3.7 %copy-start.7 = (pred[256,256]{0,1:T(8,128)(4,1)S(1)}, pred[256,256]{0,1:T(8,128)(4,1)}, u32[]{:S(2)}) copy-start(pred[256,256]{0,1:T(8,128)(4,1)} %get-tuple-element.772) | copy-start | bytes 196612 | tf_op jit(solution)/shard_map/cond
  167.0 4.6 %copy-start.1 = (f32[2,256,256,8]{2,1,3,0:T(8,128)S(1)}, f32[2,256,256,8]{2,1,3,0:T(8,128)}, u32[]{:S(2)}) copy-start(f32[2,256,256,8]{2,1,3,0:T(8,128)} %fusion.25) | copy-start | bytes 12582916 | tf_op jit(solution)/shard_map/cond
  174.6 18.1 %collective-permute-start.2 = (f32[2,256,256]{1,2,0:T(8,128)}, f32[2,256,256]{1,2,0:T(8,128)}, u32[]{:S(2)}, u32[]{:S(2)}) collective-permute-start(f32[2,256,256]{1,2,0:T(8,128)} %get-tuple-element.1216), channel_id=1, source_target_pairs={{0,4},{4,8},{8,12},{12,0},{1,5},{5,9},{9,13},{13,1},{2,6},{6,10},{... | collective-permute-start | bytes 1572872 | tf_op jit(solution)/shard_map/while/body/eval_jaxpr/ppermute | solution.py:17
  174.7 17.3 %collective-permute-start.1 = (bf16[2,256,256]{1,2,0:T(8,128)(2,1)}, bf16[2,256,256]{1,2,0:T(8,128)(2,1)S(1)}, u32[]{:S(2)}, u32[]{:S(2)}) collective-permute-start(bf16[2,256,256]{1,2,0:T(8,128)(2,1)} %get-tuple-element.1215), channel_id=1, source_target_pairs={{0,4},{4,8},{8,12},{12,0},{1,5},{5,9},{9,13},{13,1},{2,6},{6,10},{... | collective-permute-start | bytes 786440 | tf_op jit(solution)/shard_map/while/body/eval_jaxpr/ppermute | solution.py:17
  192.7 1.8 copy-start.3
  203.2 17.2 %collective-permute-start.2 = (f32[2,256,256]{1,2,0:T(8,128)}, f32[2,256,256]{1,2,0:T(8,128)}, u32[]{:S(2)}, u32[]{:S(2)}) collective-permute-start(f32[2,256,256]{1,2,0:T(8,128)} %get-tuple-element.1216), channel_id=1, source_target_pairs={{0,4},{4,8},{8,12},{12,0},{1,5},{5,9},{9,13},{13,1},{2,6},{6,10},{... | collective-permute-start | bytes 1572872 | tf_op jit(solution)/shard_map/while/body/eval_jaxpr/ppermute | solution.py:17
  203.2 16.5 %collective-permute-start.1 = (bf16[2,256,256]{1,2,0:T(8,128)(2,1)}, bf16[2,256,256]{1,2,0:T(8,128)(2,1)S(1)}, u32[]{:S(2)}, u32[]{:S(2)}) collective-permute-start(bf16[2,256,256]{1,2,0:T(8,128)(2,1)} %get-tuple-element.1215), channel_id=1, source_target_pairs={{0,4},{4,8},{8,12},{12,0},{1,5},{5,9},{9,13},{13,1},{2,6},{6,10},{... | collective-permute-start | bytes 786440 | tf_op jit(solution)/shard_map/while/body/eval_jaxpr/ppermute | solution.py:17
  220.4 1.8 copy-start.3
  230.9 16.4 %collective-permute-start.2 = (f32[2,256,256]{1,2,0:T(8,128)}, f32[2,256,256]{1,2,0:T(8,128)}, u32[]{:S(2)}, u32[]{:S(2)}) collective-permute-start(f32[2,256,256]{1,2,0:T(8,128)} %get-tuple-element.1216), channel_id=1, source_target_pairs={{0,4},{4,8},{8,12},{12,0},{1,5},{5,9},{9,13},{13,1},{2,6},{6,10},{... | collective-permute-start | bytes 1572872 | tf_op jit(solution)/shard_map/while/body/eval_jaxpr/ppermute | solution.py:17
  230.9 15.7 %collective-permute-start.1 = (bf16[2,256,256]{1,2,0:T(8,128)(2,1)}, bf16[2,256,256]{1,2,0:T(8,128)(2,1)S(1)}, u32[]{:S(2)}, u32[]{:S(2)}) collective-permute-start(bf16[2,256,256]{1,2,0:T(8,128)(2,1)} %get-tuple-element.1215), channel_id=1, source_target_pairs={{0,4},{4,8},{8,12},{12,0},{1,5},{5,9},{9,13},{13,1},{2,6},{6,10},{... | collective-permute-start | bytes 786440 | tf_op jit(solution)/shard_map/while/body/eval_jaxpr/ppermute | solution.py:17
  247.3 1.8 copy-start.3
  259.3 9.3 %collective-permute-start.7 = (bf16[2,256,256]{2,1,0:T(8,128)(2,1)S(1)}, bf16[2,256,256]{2,1,0:T(8,128)(2,1)S(1)}, u32[]{:S(2)}, u32[]{:S(2)}) collective-permute-start(bf16[2,256,256]{2,1,0:T(8,128)(2,1)S(1)} %copy.111), channel_id=1, source_target_pairs={{0,4},{4,8},{8,12},{12,0},{1,5},{5,9},{9,13},{13,1},{2,6},{6,10},{... | collective-permute-start | bytes 786440 | tf_op jit(solution)/shard_map/ppermute | solution.py:17
  259.6 16.8 %collective-permute-start.5 = (bf16[128,2048]{1,0:T(8,128)(2,1)S(1)}, bf16[128,2048]{1,0:T(8,128)(2,1)S(1)}, u32[]{:S(2)}, u32[]{:S(2)}) collective-permute-start(bf16[128,2048]{1,0:T(8,128)(2,1)S(1)} %bitcast.227), channel_id=1, source_target_pairs={{0,4},{4,0},{8,12},{12,8},{1,5},{5,1},{9,13},{13,9},{2,6},{6,2},{1... | collective-permute-start | bytes 1572872 | tf_op jit(solution)/shard_map/ppermute | solution.py:27
  268.7 0.8 copy-start.5
  276.4 15.5 %collective-permute-start.6 = (bf16[128,2048]{1,0:T(8,128)(2,1)S(1)}, bf16[128,2048]{1,0:T(8,128)(2,1)S(1)}, u32[]{:S(2)}, u32[]{:S(2)}) collective-permute-start(bf16[128,2048]{1,0:T(8,128)(2,1)S(1)} %collective-permute-done.5), channel_id=1, source_target_pairs={{0,8},{8,0},{4,12},{12,4},{1,9},{9,1},{5,13},{13,5},{2,10},{10,2},... | collective-permute-start | bytes 1572872 | tf_op jit(solution)/shard_map/ppermute | solution.py:27
  (2 other events, 1.2 us)
Sparse Core Ops, SparseCore 0:
  269.6 16.9 all-reduce.1
where the time goes:
time: 301 us; the launch traced here: 300 us
  waiting for transfers between devices  139 us (46%)
  matrix products  40.5 us (13%)
  local copies, waits for them, and re-layouts  35.2 us (12%)
  other arithmetic  32.1 us (11%)
  blocking collectives  23.5 us (8%)
  between operations  15.7 us (5%)
  starting transfers between devices  12.9 us (4%)
    ppermute x10, waiting for transfers between devices, from_behind(): lax.ppermute(array, axis, [(i, (i + by) % count) for i in range(count)])  84.1 us
    ppermute x4, waiting for transfers between devices, swapped(): return lax.ppermute(block, axis, route)  48.8 us
    dot_general x16, matrix products, block_scores(): jnp.einsum('qgpd,kgd->gpqk', row_view, key_view, preferred_element_type=j...  29 us
    all_gather x1, blocking collectives, shards(): seg_all = lax.all_gather(segments, 'ctx', axis=0, tiled=True)  23.5 us
    while x9, local copies, waits for them, and re-layouts  9.88 us
    ppermute x4, starting transfers between devices, swapped(): return lax.ppermute(block, axis, route)  9.63 us
    add x6, other arithmetic, advance(): return (state_in[0] + query_term, state_in[1] + kv_term)  7.14 us
    psum x1, waiting for transfers between devices, shards(): summed = lax.psum(grad_full.astype(jnp.bfloat16), 'kv').astype(jnp.float32)  6.28 us
  transfers between devices with their start and end apart: 15, of which 12 were waited for; matrix products, arithmetic and copies ran while one was open for 3% of the time, Pallas kernels for 0%

commit v1 on v0

v1 whole, which is shorter than its diff:
```python
import functools
import jax
import jax.numpy as jnp
from jax import lax
from jax.experimental import pallas as pl
from jax.experimental.pallas import tpu as pltpu
from jax.sharding import PartitionSpec as P

QUERY_HEADS = 64
KEY_VALUE_HEADS = 8
HEAD_SIZE = 128
SEGMENT_ROWS = 16
TILE = 32
HINT = 0.2
AHEAD = 3
FILL_LOW = -1e30
LOG2_E = 1.4426950408889634
VMEM_LIMIT = 40 * 1024 * 1024
PACK_VMEM_LIMIT = 53 * 1024 * 1024 + 512 * 1024
LOAD_VMEM_LIMIT = 51 * 1024 * 1024
NUMBER_VMEM_LIMIT = 50 * 1024 * 1024
LOAD_PIECES = 8

WHOLE = pl.BlockSpec(memory_space=pltpu.VMEM)
ANYWHERE = pl.BlockSpec(memory_space=pl.ANY)


def across(a, b):
    return lax.dot_general(a, b, (((1,), (1,)), ((), ())), preferred_element_type=jnp.float32)


def times(a, b):
    return jnp.dot(a, b, preferred_element_type=jnp.float32)


def joined(pieces, axis):
    return pieces[0] if len(pieces) == 1 else jnp.concatenate(pieces, axis=axis)


def pack_kernel(k_ref, v_ref, *refs, first_of):
    *out_refs, sems = refs
    rows = k_ref.shape[0]
    first = first_of(lax.axis_index("kv"))
    copies = []
    for chunk, out_ref in enumerate(out_refs):
        columns = pl.ds(pl.multiple_of((first + chunk) * HEAD_SIZE, HEAD_SIZE), HEAD_SIZE)
        for part, ref in enumerate((k_ref, v_ref)):
            copies.append(
                pltpu.make_async_copy(
                    ref.at[:, columns],
                    out_ref.at[pl.ds(part * rows, rows), :],
                    sems.at[2 * chunk + part],
                )
            )
    for copy in copies:
        copy.start()
    for copy in copies:
        copy.wait()


def number_kernel(seg_ref, own_ref, out_ref):
    rows = seg_ref.shape[1]
    numbers = jnp.broadcast_to(seg_ref[...].astype(jnp.float32) + 1.0, (number_rows(rows), rows))
    pieces = [numbers[:, at : at + HEAD_SIZE] for at in range(0, rows, HEAD_SIZE)]
    tail = joined(pieces, 0).astype(jnp.bfloat16)
    out_ref[: 2 * rows, :] = own_ref[: 2 * rows, :]
    out_ref[pl.ds(2 * rows, tail.shape[0]), :] = tail


def load_kernel(q_ref, g_ref, own_ref, q_out_ref, g_out_ref, sems):
    pieces = sems.shape[1]
    count = q_ref.shape[0] // pieces
    copies = []
    for piece in range(pieces):
        here = slice(piece * count, (piece + 1) * count)
        for part, (ref, out_ref) in enumerate(((q_ref, q_out_ref), (g_ref, g_out_ref))):
            copies.append(
                pltpu.make_async_copy(
                    ref.at[here, :], out_ref.at[here, :], sems.at[part, piece]
                )
            )
    for copy in copies:
        copy.start()
    for copy in copies:
        copy.wait()


def number_rows(rows):
    return max(SEGMENT_ROWS * HEAD_SIZE // rows, 1)


def segment_row(ref, rows):
    repeat = number_rows(rows)
    count = repeat * rows // HEAD_SIZE
    tail = ref[pl.ds(ref.shape[0] - count, count), :].astype(jnp.float32)
    return joined([tail[at : at + 1] for at in range(0, tail.shape[0], repeat)], 1)


def fill_bias(bias_ref, own_ref, kv_ref, step):
    rows = bias_ref.shape[0]
    q_seg = segment_row(own_ref, rows)
    k_seg = segment_row(kv_ref, rows)
    k_col = jnp.broadcast_to(k_seg, (8, rows)).T[:, :1]
    allowed = k_col == q_seg
    if step == 0:
        k_pos = lax.broadcasted_iota(jnp.int32, (rows, rows), 0)
        q_pos = lax.broadcasted_iota(jnp.int32, (rows, rows), 1)
        allowed = allowed & (k_pos <= q_pos)
    bias_ref[...] = jnp.where(allowed, 0.0, FILL_LOW)


def activity(own_ref, kv_ref, step, rows):
    q_seg = segment_row(own_ref, rows)
    k_seg = segment_row(kv_ref, rows)
    reached = lax.axis_index("ctx") >= step
    active = reached & (k_seg[0, rows - 1] >= q_seg[0, 0]) & (k_seg[0, 0] <= q_seg[0, rows - 1])
    return active, k_seg[0, rows // 2 - 1] >= q_seg[0, 0]


def full_units(per_kv, rows):
    return [(slice(0, rows), [(head, slice(0, rows))]) for head in range(per_kv)]


def own_units(per_kv, rows):
    half = rows // 2
    units = []
    for head in range(0, per_kv, 2):
        units += [(slice(0, half), [(head + i, slice(0, rows))]) for i in range(2)]
        units.append((slice(half, rows), [(head + i, slice(half, rows)) for i in range(2)]))
    return units


def late_units(per_kv, rows):
    return [(slice(rows // 2, rows), [(head, slice(0, rows))]) for head in range(per_kv)]


def early_units(per_kv, rows):
    early = slice(0, rows // 2)
    return [(slice(0, rows), [(head, early), (head + 1, early)]) for head in range(0, per_kv, 2)]


class Unit:
    def __init__(self, unit, base, q_ref, g_ref, kv_ref, bias_ref):
        self.keys, self.parts = unit
        self.rows = kv_ref.shape[0] // 2
        self.bias_ref = bias_ref
        rows = bias_ref.shape[0]
        self.q = self.gather(q_ref, base)
        self.g = self.gather(g_ref, base)
        k = kv_ref[self.keys, :]
        v = kv_ref[slice(rows + self.keys.start, rows + self.keys.stop), :]
        self.raw = across(k, self.q)
        self.dprobs = across(v, self.g)

    def gather(self, ref, base):
        return joined(
            [ref[span, (base + head) * HEAD_SIZE : (base + head + 1) * HEAD_SIZE] for head, span in self.parts],
            0,
        )

    def row(self, ref, part):
        return joined([ref[part, head : head + 1, span] for head, span in self.parts], 1)

    def put_row(self, ref, part, value):
        for (head, span), piece in zip(self.parts, self.split(value)):
            ref[part, head : head + 1, span] = piece

    def split(self, value):
        at, pieces = 0, []
        for _, span in self.parts:
            width = span.stop - span.start
            pieces.append(value[:, at : at + width])
            at += width
        return pieces

    def tiles(self):
        for first in range(0, self.keys.stop - self.keys.start, TILE):
            here = slice(first, first + TILE)
            key_rows = slice(self.keys.start + first, self.keys.start + first + TILE)
            bias = joined([self.bias_ref[key_rows, span] for _, span in self.parts], 1)
            yield bias, self.raw[here], self.dprobs[here]

    def updated(self, stats, factor):
        scores, top = [], None
        for bias, raw, _ in self.tiles():
            scores.append(raw * factor + bias)
            top = scores[-1] if top is None else jnp.maximum(top, scores[-1])
        peak = jnp.max(top, axis=0, keepdims=True)
        if stats is not None:
            peak = jnp.maximum(peak, stats[0])
        weights, total, weighted = [], None, None
        for tile, (_, _, dprobs) in zip(scores, self.tiles()):
            weights.append(jnp.exp2(tile - peak))
            product = weights[-1] * dprobs
            total = weights[-1] if total is None else total + weights[-1]
            weighted = product if weighted is None else weighted + product
        total = jnp.sum(total, axis=0, keepdims=True)
        weighted = jnp.sum(weighted, axis=0, keepdims=True)
        if stats is not None:
            fade = jnp.exp2(stats[0] - peak)
            total = total + stats[1] * fade
            weighted = weighted + stats[2] * fade
        return (peak, total, weighted), weights

    def lowered(self, log_total, delta, factor, weights=None, inverse=None):
        probs, dscores = [], []
        for index, (bias, raw, dprobs) in enumerate(self.tiles()):
            if weights is None:
                tile = jnp.exp2(raw * factor + bias - log_total)
            else:
                tile = weights[index] * inverse
            probs.append(tile.astype(jnp.bfloat16))
            dscores.append((tile * (dprobs - delta)).astype(jnp.bfloat16))
        self.probs, self.dscores = joined(probs, 0), joined(dscores, 0)


def in_turn(units, make, handle, count):
    made = [make(unit) for unit in units[:count]]
    for index in range(len(units)):
        if index + count < len(units):
            made.append(make(units[index + count]))
        handle(made[index])
        made[index] = None


class GradSum:
    def __init__(self, acc_ref, rows):
        self.acc_ref, self.rows, self.waiting, self.seen = acc_ref, rows, {}, set()

    def add(self, unit):
        key = unit.keys.start, unit.keys.stop
        self.waiting.setdefault(key, []).append(unit)
        if len(self.waiting[key]) == 2:
            self.flush(key)

    def flush(self, key):
        units = self.waiting.pop(key)
        first, last = key
        for offset, lhs, rhs in (
            (0, joined([u.dscores for u in units], 1), joined([u.q for u in units], 0)),
            (self.rows, joined([u.probs for u in units], 1), joined([u.g for u in units], 0)),
        ):
            here = slice(offset + first, offset + last)
            term = times(lhs, rhs)
            self.acc_ref[here, :] = self.acc_ref[here, :] + term if key in self.seen else term
        self.seen.add(key)

    def finish(self):
        for key in list(self.waiting):
            self.flush(key)


def finals(stats):
    return stats[0] + jnp.log2(stats[1]), stats[2] / stats[1]


def stats_kernel(ins, outs, _, *, fill, chunk, per_kv, factor, step):
    q_ref, g_ref, own_seg_ref, kv_ref, kv_seg_ref = ins[:5]
    in_ref = ins[5] if step else None
    out_ref = outs[0]
    bias_ref = outs[1] if fill else ins[-1]
    rows = q_ref.shape[0]

    def run():
        if fill:
            fill_bias(bias_ref, own_seg_ref, kv_seg_ref, step)

        def handle(unit):
            source = in_ref
            if step == 0:
                source = out_ref if unit.keys.start > 0 else None
            stats = None if source is None else tuple(unit.row(source, part) for part in range(3))
            for part, value in enumerate(unit.updated(stats, factor)[0]):
                unit.put_row(out_ref, part, value)

        units = full_units(per_kv, rows) if step else own_units(per_kv, rows)
        in_turn(units, lambda unit: Unit(unit, chunk * per_kv, q_ref, g_ref, kv_ref, bias_ref), handle, AHEAD)

    if step == 0:
        run()
        return
    active, _ = activity(own_seg_ref, kv_seg_ref, step, rows)
    pl.when(active)(run)

    @pl.when(jnp.logical_not(active))
    def _():
        out_ref[...] = in_ref[...]


def far_kernel(ins, outs, scratch, *, fill, chunk, per_kv, factor, step):
    q_ref, g_ref, own_seg_ref, kv_ref, kv_seg_ref, in_ref = ins[:6]
    out_ref, kv_grad_ref, dq_ref = outs[:3]
    bias_ref = outs[3] if fill else ins[-1]
    kt_ref, acc_ref = scratch
    rows = q_ref.shape[0]
    half = rows // 2
    active, early = activity(own_seg_ref, kv_seg_ref, step, rows)
    log_total, delta = finals((in_ref[0], in_ref[1], in_ref[2]))
    out_ref[0] = log_total
    out_ref[1] = delta

    def run(units, keys):
        if fill:
            fill_bias(bias_ref, own_seg_ref, kv_seg_ref, step)
        kt_ref[...] = kv_ref[:rows, :].T
        if keys.start > 0:
            for offset in (0, rows):
                acc_ref[offset : offset + keys.start, :] = jnp.zeros((keys.start, HEAD_SIZE), jnp.float32)
        grads = GradSum(acc_ref, rows)

        def first(unit):
            stats = tuple(unit.row(in_ref, part) for part in range(3))
            stats, unit.weights = unit.updated(stats, factor)
            unit.finals = finals(stats)
            unit.inverse = 1.0 / stats[1]
            unit.put_row(out_ref, 0, unit.finals[0])
            unit.put_row(out_ref, 1, unit.finals[1])

        def second(unit):
            unit.lowered(*unit.finals, factor, unit.weights, unit.inverse)
            grads.add(unit)
            dq = times(kt_ref[:, unit.keys], unit.dscores)
            for (head, span), piece in zip(unit.parts, unit.split(dq)):
                dq_ref[head, :, span] = piece
                if span.stop < rows:
                    dq_ref[head, :, span.stop :] = jnp.zeros((HEAD_SIZE, rows - span.stop), jnp.float32)

        def both(unit):
            first(unit)
            second(unit)

        def make(unit):
            return Unit(unit, chunk * per_kv, q_ref, g_ref, kv_ref, bias_ref)

        if chunk % 2:
            made = []
            in_turn(units, make, lambda unit: (first(unit), made.append(unit)), AHEAD)
            for unit in made:
                second(unit)
        else:
            in_turn(units, make, both, AHEAD)
        grads.finish()
        kv_grad_ref[...] = acc_ref[...].astype(kv_grad_ref.dtype)

    @pl.when(active & jnp.logical_not(early))
    def _():
        run(late_units(per_kv, rows), slice(half, rows))

    @pl.when(active & early)
    def _():
        run(early_units(per_kv, rows), slice(0, rows))

    @pl.when(jnp.logical_not(active))
    def _():
        dq_ref[...] = jnp.zeros_like(dq_ref)
        kv_grad_ref[...] = jnp.zeros_like(kv_grad_ref)


def grads_kernel(ins, outs, scratch, *, early_own, chunk, per_kv, factor, scale, step):
    q_ref, g_ref, own_seg_ref, kv_ref, kv_seg_ref, in_ref, dq_in_ref, bias_ref = ins[:8]
    kv_grad_ref, dq_ref = outs[:2]
    kt_ref = scratch[0]
    rows = q_ref.shape[0]

    def make(unit):
        return Unit(unit, chunk * per_kv, q_ref, g_ref, kv_ref, bias_ref)

    def run():
        kt_ref[...] = kv_ref[:rows, :].T
        grads = GradSum(kv_grad_ref, rows)

        def handle(unit):
            unit.lowered(unit.row(in_ref, 0), unit.row(in_ref, 1), factor)
            grads.add(unit)
            head = unit.parts[0][0]
            dq_ref[head] = dq_in_ref[head] + times(kt_ref[:, unit.keys], unit.dscores)

        in_turn(full_units(per_kv, rows), make, handle, AHEAD)
        grads.finish()

    active, _ = activity(own_seg_ref, kv_seg_ref, step, rows)
    pl.when(active)(run)

    @pl.when(jnp.logical_not(active))
    def _():
        kv_grad_ref[...] = jnp.zeros_like(kv_grad_ref)
        dq_ref[...] = dq_in_ref[...]
        if early_own:
            own_kv_ref, own_bias_ref = ins[8:]
            own_run(
                (q_ref, g_ref, own_kv_ref, in_ref, dq_in_ref, own_bias_ref), outs[2:], scratch,
                chunk, per_kv, factor, scale,
            )


def own_run(ins, outs, scratch, chunk, per_kv, factor, scale):
    q_ref, g_ref, kv_ref, in_ref, dq_in_ref, bias_ref = ins
    kv_grad_ref, query_grad_ref = outs
    kt_ref, turned_ref, sems = scratch
    rows = q_ref.shape[0]
    half = rows // 2
    kt_ref[...] = kv_ref[:rows, :].T
    grads = GradSum(kv_grad_ref, rows)
    dq_now, copies = {}, []

    def send(head, count):
        here = slice(head * HEAD_SIZE, (head + count) * HEAD_SIZE)
        there = slice((chunk * per_kv + head) * HEAD_SIZE, (chunk * per_kv + head + count) * HEAD_SIZE)
        copies.append(
            pltpu.make_async_copy(turned_ref.at[:, here], query_grad_ref.at[:, there], sems.at[head // count])
        )
        copies[-1].start()

    def handle(unit):
        unit.lowered(unit.row(in_ref, 0), unit.row(in_ref, 1), factor)
        grads.add(unit)
        dq = times(kt_ref[:, unit.keys], unit.dscores)
        head = unit.parts[0][0]
        if unit.keys.start == 0:
            dq_now[head] = dq_in_ref[head] + dq
            return
        for (other, _), piece in zip(unit.parts, unit.split(dq)):
            total = dq_now.pop(other)
            for at, value in ((0, total[:, :half]), (half, total[:, half:] + piece)):
                turned_ref[at : at + half, other * HEAD_SIZE : (other + 1) * HEAD_SIZE] = (
                    (value * scale).astype(jnp.bfloat16).T
                )
        send(head, len(unit.parts))

    def make(unit):
        return Unit(unit, chunk * per_kv, q_ref, g_ref, kv_ref, bias_ref)

    in_turn(own_units(per_kv, rows), make, handle, AHEAD)
    grads.finish()
    for copy in copies:
        copy.wait()


def own_kernel(ins, outs, scratch, *, done_before, chunk, per_kv, factor, scale):
    q_ref, g_ref, own_seg_ref, kv_ref, kv_seg_ref, in_ref, dq_in_ref, bias_ref = ins[:8]

    def run():
        own_run(
            (q_ref, g_ref, kv_ref, in_ref, dq_in_ref, bias_ref), outs, scratch,
            chunk, per_kv, factor, scale,
        )

    if not done_before:
        run()
        return
    active, _ = activity(own_seg_ref, kv_seg_ref, 1, q_ref.shape[0])
    pl.when(active)(run)

    @pl.when(jnp.logical_not(active))
    def _():
        outs[0][...] = ins[8][...]


def finish_kernel(ins, outs, _, *, scale):
    own_ref, arrived_ref = ins
    rows = own_ref.shape[0] // 2
    for first, factor in ((0, scale), (rows, 1.0)):
        here = slice(first, first + rows)
        total = (own_ref[here, :] + arrived_ref[here, :].astype(jnp.float32)) * factor
        outs[0][here, :] = total.astype(jnp.bfloat16)


def place_kernel(mine_ref, other_ref, *refs, chunk, chunks):
    *out_refs, sems = refs[-3:]
    rows = out_refs[0].shape[0]
    core = lax.axis_index("kv")
    copies = []
    for place, ref in enumerate((mine_ref, other_ref)):
        first = ((1 - core if place else core) * chunks + chunk) * HEAD_SIZE
        columns = pl.ds(pl.multiple_of(first, HEAD_SIZE), HEAD_SIZE)
        for part, out_ref in enumerate(out_refs):
            copies.append(
                pltpu.make_async_copy(
                    ref.at[pl.ds(part * rows, rows), :], out_ref.at[:, columns], sems.at[place, part]
                )
            )
    for copy in copies:
        copy.start()
    for copy in copies:
        copy.wait()


def shards(queries, key_matrix, value_matrix, out_grad, segments):
    rows = queries.shape[0]
    heads = queries.shape[1] // HEAD_SIZE
    group_width = QUERY_HEADS // KEY_VALUE_HEADS
    chunks = max(heads // group_width, 1)
    per_kv = heads // chunks
    ctx = lax.axis_size("ctx")
    groups = lax.axis_size("groups")
    longest = rows * ctx // 2
    reach = min(ctx - 1, (longest - 1 + rows - 1) // rows)
    scale = HEAD_SIZE ** (-0.5)
    factor = scale * LOG2_E
    tail = number_rows(rows) * rows // HEAD_SIZE
    block_shapes = tuple(
        jax.ShapeDtypeStruct((2 * rows + (0 if chunk else tail), HEAD_SIZE), jnp.bfloat16)
        for chunk in range(chunks)
    )
    pairs = per_kv * rows * rows
    each = range(chunks)

    def first_of(kv_index):
        return kv_index * heads // group_width

    def up(step):
        route = []
        for group in range(groups):
            at = group * ctx
            beside = (group + 1) % groups * ctx
            route += [(at + i, beside + i) for i in range(step - 1)]
            route += [(at + i, at + i + 1) for i in range(step - 1, ctx - 1)]
            route.append((at + ctx - 1, at + step - 1))
        return route

    down = [
        (group * ctx + (i + 1) % ctx, group * ctx + i) for group in range(groups) for i in range(ctx)
    ]

    def moved(array, route):
        return lax.ppermute(array, ("groups", "ctx"), route)

    def call(body, operands, outs, scratch, name, micros, out_specs=None, into=(), after=()):
        count = len(operands)
        extra = [array for array, _ in into] + list(after)
        specs = [out_specs[index] for _, index in into] + [ANYWHERE] * len(after)

        def kernel(*refs):
            rest = refs[count + len(extra) :]
            body(refs[:count], rest[: len(outs)], rest[len(outs) :])

        return pl.pallas_call(
            kernel,
            out_shape=outs,
            in_specs=[WHOLE] * count + specs,
            out_specs=out_specs or (WHOLE,) * len(outs),
            scratch_shapes=scratch,
            input_output_aliases={count + place: index for place, (_, index) in enumerate(into)},
            compiler_params=pltpu.CompilerParams(vmem_limit_bytes=VMEM_LIMIT),
            cost_estimate=pl.CostEstimate(
                flops=int(1153e6 * micros * HINT), bytes_accessed=4 * pairs // rows, transcendentals=pairs
            ),
            name=name,
        )(*operands, *extra)

    own = pl.pallas_call(
        functools.partial(pack_kernel, first_of=first_of),
        out_shape=block_shapes,
        in_specs=[ANYWHERE] * 2,
        out_specs=(WHOLE,) * chunks,
        scratch_shapes=[pltpu.SemaphoreType.DMA((2 * chunks,))],
        compiler_params=pltpu.CompilerParams(vmem_limit_bytes=PACK_VMEM_LIMIT),
        cost_estimate=pl.CostEstimate(flops=0, bytes_accessed=4 * 1024 * 1024, transcendentals=0),
        name="pack",
    )(key_matrix, value_matrix)
    own = list(own)
    own[0] = pl.pallas_call(
        number_kernel,
        out_shape=block_shapes[0],
        in_specs=[WHOLE] * 2,
        out_specs=WHOLE,
        input_output_aliases={1: 0},
        compiler_params=pltpu.CompilerParams(vmem_limit_bytes=NUMBER_VMEM_LIMIT),
        name="number",
    )(segments.reshape(1, rows), own[0])

    rows_shape = jax.ShapeDtypeStruct(queries.shape, jnp.bfloat16)
    queries, out_grad = pl.pallas_call(
        load_kernel,
        out_shape=(rows_shape, rows_shape),
        in_specs=[ANYWHERE] * 3,
        out_specs=(WHOLE, WHOLE),
        scratch_shapes=[pltpu.SemaphoreType.DMA((2, LOAD_PIECES))],
        compiler_params=pltpu.CompilerParams(vmem_limit_bytes=LOAD_VMEM_LIMIT),
        name="load",
    )(queries, out_grad, own[0])

    turned = pltpu.VMEM((HEAD_SIZE, rows), jnp.bfloat16)
    total_sum = pltpu.VMEM((2 * rows, HEAD_SIZE), jnp.float32)
    bias_shape = jax.ShapeDtypeStruct((rows, rows), jnp.float32)
    stats_shape = jax.ShapeDtypeStruct((3, per_kv, rows), jnp.float32)
    finals_shape = jax.ShapeDtypeStruct((2, per_kv, rows), jnp.float32)
    dq_shape = jax.ShapeDtypeStruct((per_kv, HEAD_SIZE, rows), jnp.float32)
    kv_grad_shape = jax.ShapeDtypeStruct((2 * rows, HEAD_SIZE), jnp.float32)
    sent_shape = jax.ShapeDtypeStruct((2 * rows, HEAD_SIZE), jnp.bfloat16)
    common = {"per_kv": per_kv, "factor": factor}
    biases = [None] * (reach + 1)
    own = list(lax.optimization_barrier(tuple(own)))
    blocks = [[own[chunk], moved(own[chunk], up(1))] for chunk in each]

    def common_operands(chunk, step):
        return queries, out_grad, own[0], blocks[chunk][step], blocks[0][step]

    def with_bias(kernel, chunk, step, operands, outs, scratch, name, micros, after=()):
        fill = biases[step] is None
        body = functools.partial(kernel, fill=fill, chunk=chunk, step=step, **common)
        operands = common_operands(chunk, step) + operands
        if not fill:
            return call(body, operands + (biases[step],), outs, scratch, name, micros, after=after)
        *results, biases[step] = call(
            body, operands, outs + (bias_shape,), scratch, name, micros, after=after
        )
        return results

    stats, final_stats = [None] * chunks, [None] * chunks
    sums, dq = [None] * chunks, [None] * chunks
    for chunk in each:
        after = [blocks[chunk - 1][1]] if chunk else []
        (stats[chunk],) = with_bias(
            stats_kernel, chunk, 0, (), (stats_shape,), [], "stats_own", 0.8, after
        )
    for step in range(1, reach):
        for chunk in each:
            here, stats[chunk] = lax.optimization_barrier((blocks[chunk][step], stats[chunk]))
            blocks[chunk].append(moved(here, up(step + 1)))
        for chunk in each:
            (stats[chunk],) = with_bias(
                stats_kernel, chunk, step, (stats[chunk],), (stats_shape,), [], "stats", 1.1
            )
    before = [stats[-1]]
    for chunk in each:
        final_stats[chunk], sums[chunk], dq[chunk] = with_bias(
            far_kernel, chunk, reach, (stats[chunk],), (finals_shape, sent_shape, dq_shape),
            [turned, total_sum], "grads_far", 1.6, before,
        )
        before = [sums[chunk]]
    finished, returning, query_grad = [None] * chunks, [], []
    own_outs = (kv_grad_shape, jax.ShapeDtypeStruct(queries.shape, jnp.bfloat16))
    own_specs = (WHOLE, ANYWHERE)
    own_scratch = [
        turned,
        pltpu.VMEM((rows, per_kv * HEAD_SIZE), jnp.bfloat16),
        pltpu.SemaphoreType.DMA((per_kv // 2,)),
    ]

    def own_grads(chunk):
        done_before = finished[chunk] is not None
        body = functools.partial(own_kernel, done_before=done_before, chunk=chunk, scale=scale, **common)
        into = [(query_grad.pop(), 1)] if query_grad else []
        seen = 1 if done_before else 0
        finished[chunk], written = call(
            body,
            (queries, out_grad, own[0], blocks[chunk][0], blocks[0][seen])
            + (final_stats[chunk], dq[chunk], biases[0])
            + ((finished[chunk],) if done_before else ()),
            own_outs,
            own_scratch,
            "grads_own",
            1.8,
            out_specs=own_specs,
            into=into,
            after=[sums[chunk]],
        )
        query_grad.append(written)

    for step in range(reach - 1, 0, -1):
        mine = [None] * chunks
        arriving = [moved(sums[chunk], down) for chunk in each]
        for chunk in each:
            early_own = step == 1 and chunk == 0
            body = functools.partial(
                grads_kernel, early_own=early_own, chunk=chunk, step=step, scale=scale, **common
            )
            operands = common_operands(chunk, step) + (final_stats[chunk], dq[chunk], biases[step])
            outs, specs, scratch = (kv_grad_shape, dq_shape), (WHOLE, WHOLE), [turned]
            if early_own:
                operands += (blocks[chunk][0], biases[0])
                outs, specs, scratch = outs + own_outs, specs + own_specs, own_scratch
            mine[chunk], dq[chunk], *rest = call(
                body, operands, outs, scratch, "grads", 1.6, out_specs=specs, after=before
            )
            if early_own:
                finished[chunk] = rest[0]
                query_grad.append(rest[1])
            before = [mine[chunk]]
        arriving[0], mine[-1] = lax.optimization_barrier((arriving[0], mine[-1]))
        for chunk in each:
            here = arriving[chunk]
            if step == 1 and chunk:
                own_grads(chunk - 1)
                here, finished[chunk - 1] = lax.optimization_barrier((here, finished[chunk - 1]))
            sums[chunk] = (mine[chunk] + here.astype(jnp.float32)).astype(jnp.bfloat16)
            if step == 1:
                returning.append(moved(sums[chunk], down))
    if reach == 1:
        returning += [moved(sums[chunk], down) for chunk in each]
    for chunk in each if reach == 1 else each[-1:]:
        own_grads(chunk)

    returning[0], finished[-1] = lax.optimization_barrier((returning[0], finished[-1]))
    kv_swap = [(0, 1), (1, 0)]
    if chunks * lax.axis_size("kv") * HEAD_SIZE > key_matrix.shape[1]:
        key_scale = jnp.where(jnp.arange(2 * rows)[:, None] < rows, scale, 1.0).astype(jnp.float32)
        both = []
        for chunk in each:
            mine = (finished[chunk] + returning[chunk].astype(jnp.float32)).astype(jnp.bfloat16)
            other = lax.ppermute(mine, "kv", kv_swap).astype(jnp.float32)
            both.append(((mine.astype(jnp.float32) + other) * key_scale).astype(jnp.bfloat16))
        both = joined(both, 1)
        return query_grad[0], both[:rows], both[rows:]
    kv_grads, before = (), []
    for chunk in each:
        mine = call(
            functools.partial(finish_kernel, scale=scale),
            (finished[chunk], returning[chunk]),
            (sent_shape,),
            [],
            "finish",
            0.1,
            after=before,
        )[0]
        before = [mine]
        other = lax.ppermute(mine, "kv", kv_swap)
        kv_grads = pl.pallas_call(
            functools.partial(place_kernel, chunk=chunk, chunks=chunks),
            out_shape=(jax.ShapeDtypeStruct(key_matrix.shape, jnp.bfloat16),) * 2,
            in_specs=[WHOLE] * 2 + [ANYWHERE] * len(kv_grads),
            out_specs=(ANYWHERE,) * 2,
            scratch_shapes=[pltpu.SemaphoreType.DMA((2, 2))],
            input_output_aliases={2 + index: index for index in range(len(kv_grads))},
            compiler_params=pltpu.CompilerParams(vmem_limit_bytes=VMEM_LIMIT),
            name="place",
        )(mine, other, *kv_grads)
    return (query_grad[0], *kv_grads)


def solution(mesh):
    return jax.shard_map(
        shards,
        mesh=mesh,
        in_specs=(
            P(("groups", "ctx"), ("tp", "kv")),
            P(("groups", "ctx"), "tp"),
            P(("groups", "ctx"), "tp"),
            P(("groups", "ctx"), ("tp", "kv")),
            P(("groups", "ctx")),
        ),
        out_specs=(
            P(("groups", "ctx"), ("tp", "kv")),
            P(("groups", "ctx"), "tp"),
            P(("groups", "ctx"), "tp"),
        ),
        check_vma=False,
    )
```

time: 301 us -> 36.5 us (0.12)
  waiting for transfers between devices: 139 us -> 5.58 us
  matrix products: 40.5 us -> 0 us
  local copies, waits for them, and re-layouts: 35.2 us -> 0.67 us
  other arithmetic: 32.1 us -> 0.07 us
  blocking collectives: 23.5 us -> 0 us
  between operations: 15.7 us -> 0.98 us
  Pallas kernels: 0 us -> 11.6 us
  starting transfers between devices: 12.9 us -> 17 us
    ppermute x14 -> x10, waiting for transfers between devices: 133 us -> 5.58 us  [the longest x8 4.96 us: moved(): return lax.ppermute(array, ('groups', 'ctx'), route)]
    dot_general x28 -> x0, matrix products: 40.5 us -> none  [the longest x16 29 us: block_scores(): jnp.einsum('qgpd,kgd->gpqk', row_view, key_view, preferred_element_type=j...]
    all_gather x1 -> x0, blocking collectives: 23.5 us -> none  [shards(): seg_all = lax.all_gather(segments, 'ctx', axis=0, tiled=True)]
    add x20 -> x0, other arithmetic: 15.9 us -> none  [the longest x6 7.14 us: advance(): return (state_in[0] + query_term, state_in[1] + kv_term)]
    while x12 -> x0, local copies, waits for them, and re-layouts: 13.2 us -> none
    pallas_call x0 -> x17, Pallas kernels: none -> 11.6 us  [the longest x12 7.36 us: call(): pl.pallas_call(kernel, out_shape=outs, in_specs=[WHOLE] * count + specs,...]
    psum x1 -> x0, waiting for transfers between devices: 6.28 us -> none  [shards(): summed = lax.psum(grad_full.astype(jnp.bfloat16), 'kv').astype(jnp.float32)]
    dynamic_slice x11 -> x0, local copies, waits for them, and re-layouts: 5.19 us -> none  [the longest x7 4.89 us: key_mask(): k_seg = lax.dynamic_slice_in_dim(seg_all, k_first, key_count)]
  transfers between devices with their start and end apart: 15 -> 10, of which waited for: 12 -> 4; matrix products, arithmetic and copies ran while one was open for 3% -> 0% of each run, Pallas kernels for 0% -> 27%
where the time goes in v1:
time: 36.5 us; the launch traced here: 35.9 us
  starting transfers between devices  17 us (47%)
  Pallas kernels  11.6 us (32%)
  waiting for transfers between devices  5.58 us (15%)
  between operations  0.98 us (3%)
  local copies, waits for them, and re-layouts  0.67 us (2%)
    ppermute x8, starting transfers between devices, moved(): return lax.ppermute(array, ('groups', 'ctx'), route)  16.9 us
    pallas_call x12, Pallas kernels, call(): pl.pallas_call(kernel, out_shape=outs, in_specs=[WHOLE] * count + specs,...  7.36 us
    ppermute x8, waiting for transfers between devices, moved(): return lax.ppermute(array, ('groups', 'ctx'), route)  4.96 us
    pallas_call x1, Pallas kernels, shards(): pl.pallas_call(load_kernel, out_shape=(rows_shape, rows_shape), in_specs=...  1.73 us
    pallas_call x2, Pallas kernels, shards(): pl.pallas_call(functools.partial(place_kernel, chunk=chunk, chunks=chunks...  1.47 us
    pallas_call x1, Pallas kernels, shards(): pl.pallas_call(functools.partial(pack_kernel, first_of=first_of), out_sha...  0.99 us
  transfers between devices with their start and end apart: 10, of which 4 were waited for; matrix products, arithmetic and copies ran while one was open for 0% of the time, Pallas kernels for 27%

profile of v1, /device:TPU:0, one launch (start us, length us, event | category | flops | bytes accessed | tf_op | source)
XLA Modules:
  0.0 35.9 jit_solution(6260025260830144031)
XLA Ops:
  0.6 1.0 %pack.1 = (bf16[528,128]{1,0:T(8,128)(2,1)S(1)}, bf16[512,128]{1,0:T(8,128)(2,1)S(1)}) custom-call(bf16[256,512]{1,0:T(8,128)(2,1)} %k_ref.1, bf16[256,512]{1,0:T(8,128)(2,1)} %v_ref.1), custom_call_target="tpu_custom_call" | custom-call | bytes 4194304 | tf_op jit(solution)/shard_map/pack/pallas_call | solution.py:551
  1.6 0.0 copy-start
  1.6 0.7 %copy-done = s32[256]{0:T(256)S(1)} copy-done((s32[256]{0:T(256)S(1)}, s32[256]{0:T(256)}, u32[]{:S(2)}) %copy-start) | copy-done | bytes 1048
  2.4 3.1 %collective-permute-start.1 = (bf16[528,128]{1,0:T(8,128)(2,1)S(1)}, bf16[528,128]{1,0:T(8,128)(2,1)S(1)}, u32[]{:S(2)}, u32[]{:S(2)}) collective-permute-start(bf16[528,128]{1,0:T(8,128)(2,1)S(1)} %number.1.own_ref.refs_2_.refs_3_.refs_4_.refs_8_), channel_id=1, source_target_pairs={{0,4},{4,8},{8,12},{12,0},{16,20},{20,24},{24,28},{28,16},{1,5},{5... | collective-permute-start | bytes 405512 | tf_op jit(solution)/shard_map/ppermute | solution.py:526
  5.4 1.6 %collective-permute-start = (bf16[512,128]{1,0:T(8,128)(2,1)S(1)}, bf16[512,128]{1,0:T(8,128)(2,1)S(1)}, u32[]{:S(2)}, u32[]{:S(2)}) collective-permute-start(bf16[512,128]{1,0:T(8,128)(2,1)S(1)} %get-tuple-element.49.refs_3_), channel_id=1, source_target_pairs={{0,4},{4,8},{8,12},{12,0},{16,20},{20,24},{24,28},{28,16},{1,5},{5... | collective-permute-start | bytes 393224 | tf_op jit(solution)/shard_map/ppermute | solution.py:526
  7.0 1.7 %load.1 = (bf16[256,2048]{1,0:T(8,128)(2,1)S(1)}, bf16[256,2048]{1,0:T(8,128)(2,1)S(1)}) custom-call(bf16[256,2048]{1,0:T(8,128)(2,1)} %q_ref.1, bf16[256,2048]{1,0:T(8,128)(2,1)} %g_ref.1, bf16[528,128]{1,0:T(8,128)(2,1)S(1)} %number.1.own_ref.refs_2_.refs_3_.refs_4_.refs_8_), custom_call_target="tpu_custom_call" | custom-call | tf_op jit(solution)/shard_map/load/pallas_call | solution.py:573
  8.7 0.9 %stats_own.2 = (f32[3,8,256]{2,1,0:T(8,128)S(1)}, f32[256,256]{1,0:T(8,128)S(1)}) custom-call(bf16[256,2048]{1,0:T(8,128)(2,1)S(1)} %get-tuple-element.45.refs_0_, bf16[256,2048]{1,0:T(8,128)(2,1)S(1)} %get-tuple-element.46.refs_1_, bf16[528,128]{1,0:T(8,128)(2,1)S(1)} %number.1.own_ref.refs_2_.refs_3_.refs_4_.refs_8_, ...), custom_call_target="tpu_custom_call" | custom-call | flops 184480000 | bytes 8192 | tf_op jit(solution)/shard_map/stats_own/pallas_call | solution.py:537
  9.7 2.2 %collective-permute-done.1.refs_6_.refs_3_.refs_4_ = bf16[528,128]{1,0:T(8,128)(2,1)S(1)} collective-permute-done((bf16[528,128]{1,0:T(8,128)(2,1)S(1)}, bf16[528,128]{1,0:T(8,128)(2,1)S(1)}, u32[]{:S(2)}, u32[]{:S(2)}) %collective-permute-start.1) | collective-permute-done | bytes 135200 | tf_op jit(solution)/shard_map/ppermute | solution.py:526
  11.9 1.8 %collective-permute-start.3 = (bf16[528,128]{1,0:T(8,128)(2,1)S(1)}, bf16[528,128]{1,0:T(8,128)(2,1)S(1)}, u32[]{:S(2)}, u32[]{:S(2)}) collective-permute-start(bf16[528,128]{1,0:T(8,128)(2,1)S(1)} %collective-permute-done.1.refs_6_.refs_3_.refs_4_), channel_id=1, source_target_pairs={{0,16},{4,8},{8,12},{12,4},{16,0},{20,24},{24,28},{28,20},{1,17},{... | collective-permute-start | bytes 405512 | tf_op jit(solution)/shard_map/ppermute | solution.py:526
  13.6 0.8 %stats_own.3.refs_5_ = f32[3,8,256]{2,1,0:T(8,128)S(1)} custom-call(bf16[256,2048]{1,0:T(8,128)(2,1)S(1)} %get-tuple-element.45.refs_0_, bf16[256,2048]{1,0:T(8,128)(2,1)S(1)} %get-tuple-element.46.refs_1_, bf16[528,128]{1,0:T(8,128)(2,1)S(1)} %number.1.own_ref.refs_2_.refs_3_.refs_4_.refs_8_, bf16[512,128]{1,0:T(8,128)(2,1)S(1)} %get-tuple-element.49.refs_3_, ...), custom_call_target="tpu_custom_call" | custom-call | flops 184480000 | bytes 8192 | tf_op jit(solution)/shard_map/stats_own/pallas_call | solution.py:537
  14.5 1.2 %collective-permute-start.2 = (bf16[512,128]{1,0:T(8,128)(2,1)S(1)}, bf16[512,128]{1,0:T(8,128)(2,1)S(1)}, u32[]{:S(2)}, u32[]{:S(2)}) collective-permute-start(bf16[512,128]{1,0:T(8,128)(2,1)S(1)} %collective-permute-done.refs_3_), channel_id=1, source_target_pairs={{0,16},{4,8},{8,12},{12,4},{16,0},{20,24},{24,28},{28,20},{1,17},{... | collective-permute-start | bytes 393224 | tf_op jit(solution)/shard_map/ppermute | solution.py:526
  15.6 0.1 stats.2
  15.8 0.1 stats.3.refs_6_.refs_5_
  15.9 2.2 %collective-permute-done.3.refs_3_.refs_4_ = bf16[528,128]{1,0:T(8,128)(2,1)S(1)} collective-permute-done((bf16[528,128]{1,0:T(8,128)(2,1)S(1)}, bf16[528,128]{1,0:T(8,128)(2,1)S(1)}, u32[]{:S(2)}, u32[]{:S(2)}) %collective-permute-start.3) | collective-permute-done | bytes 135200 | tf_op jit(solution)/shard_map/ppermute | solution.py:526
  18.0 0.2 grads_far.2
  18.2 3.1 %collective-permute-start.4 = (bf16[512,128]{1,0:T(8,128)(2,1)S(1)}, bf16[512,128]{1,0:T(8,128)(2,1)S(1)}, u32[]{:S(2)}, u32[]{:S(2)}) collective-permute-start(bf16[512,128]{1,0:T(8,128)(2,1)S(1)} %get-tuple-element.59.refs_7_), channel_id=1, source_target_pairs={{4,0},{8,4},{12,8},{0,12},{20,16},{24,20},{28,24},{16,28},{5,1},{9... | collective-permute-start | bytes 393224 | tf_op jit(solution)/shard_map/ppermute | solution.py:526
  21.3 0.0 collective-permute-done.2.refs_3_
  21.3 0.2 grads_far.3
  21.5 1.5 %collective-permute-start.5 = (bf16[512,128]{1,0:T(8,128)(2,1)S(1)}, bf16[512,128]{1,0:T(8,128)(2,1)S(1)}, u32[]{:S(2)}, u32[]{:S(2)}) collective-permute-start(bf16[512,128]{1,0:T(8,128)(2,1)S(1)} %get-tuple-element.64.refs_10_), channel_id=1, source_target_pairs={{4,0},{8,4},{12,8},{0,12},{20,16},{24,20},{28,24},{16,28},{5,1},{9... | collective-permute-start | bytes 393224 | tf_op jit(solution)/shard_map/ppermute | solution.py:526
  23.0 2.3 %grads.2 = (f32[512,128]{1,0:T(8,128)S(1)}, f32[8,128,256]{2,1,0:T(8,128)S(1)}, f32[512,128]{1,0:T(8,128)S(1)}, bf16[256,2048]{1,0:T(8,128)(2,1)}) custom-call(bf16[256,2048]{1,0:T(8,128)(2,1)S(1)} %get-tuple-element.45.refs_0_, bf16[256,2048]{1,0:T(8,128)(2,1)S(1)} %get-tuple-element.46.refs_1_, ...), custom_call_target="tpu_custom_call" | custom-call | flops 368960000 | bytes 8192 | tf_op jit(solution)/shard_map/grads/pallas_call | solution.py:537
  25.3 0.4 %grads.3 = (f32[512,128]{1,0:T(8,128)S(1)}, f32[8,128,256]{2,1,0:T(8,128)S(1)}) custom-call(bf16[256,2048]{1,0:T(8,128)(2,1)S(1)} %get-tuple-element.45.refs_0_, bf16[256,2048]{1,0:T(8,128)(2,1)S(1)} %get-tuple-element.46.refs_1_, bf16[528,128]{1,0:T(8,128)(2,1)S(1)} %number.1.own_ref.refs_2_.refs_3_.refs_4_.refs_8_, ...), custom_call_target="tpu_custom_call" | custom-call | flops 368960000 | bytes 8192 | tf_op jit(solution)/shard_map/grads/pallas_call | solution.py:537
  25.7 2.6 %collective-permute-start.6 = (bf16[512,128]{1,0:T(8,128)(2,1)S(1)}, bf16[512,128]{1,0:T(8,128)(2,1)S(1)}, u32[]{:S(2)}, u32[]{:S(2)}) collective-permute-start(bf16[512,128]{1,0:T(8,128)(2,1)S(1)} %add_convert_fusion.1.refs_10_), channel_id=1, source_target_pairs={{4,0},{8,4},{12,8},{0,12},{20,16},{24,20},{28,24},{16,28},{5,1},{9... | collective-permute-start | bytes 393224 | tf_op jit(solution)/shard_map/ppermute | solution.py:526
  28.3 0.2 grads_own.2
  28.5 0.0 collective-permute-done.5
  28.5 2.2 %collective-permute-start.7 = (bf16[512,128]{1,0:T(8,128)(2,1)S(1)}, bf16[512,128]{1,0:T(8,128)(2,1)S(1)}, u32[]{:S(2)}, u32[]{:S(2)}) collective-permute-start(bf16[512,128]{1,0:T(8,128)(2,1)S(1)} %add_convert_fusion.refs_9_), channel_id=1, source_target_pairs={{4,0},{8,4},{12,8},{0,12},{20,16},{24,20},{28,24},{16,28},{5,1},{9... | collective-permute-start | bytes 393224 | tf_op jit(solution)/shard_map/ppermute | solution.py:526
  30.7 2.1 %grads_own.3 = (f32[512,128]{1,0:T(8,128)S(1)}, bf16[256,2048]{1,0:T(8,128)(2,1)}) custom-call(bf16[256,2048]{1,0:T(8,128)(2,1)S(1)} %get-tuple-element.45.refs_0_, bf16[256,2048]{1,0:T(8,128)(2,1)S(1)} %get-tuple-element.46.refs_1_, bf16[528,128]{1,0:T(8,128)(2,1)S(1)} %number.1.own_ref.refs_2_.refs_3_.refs_4_.refs_8_, ...), custom_call_target="tpu_custom_call", output_to_operand_aliasing={{1}: (8, {})} | custom-call | flops 415080000 | bytes 8192 | tf_op jit(solution)/shard_map/grads_own/pallas_call | solution.py:537
  32.9 0.1 collective-permute-start.9
  32.9 0.6 %collective-permute-done.7.refs_1_ = bf16[512,128]{1,0:T(8,128)(2,1)S(1)} collective-permute-done((bf16[512,128]{1,0:T(8,128)(2,1)S(1)}, bf16[512,128]{1,0:T(8,128)(2,1)S(1)}, u32[]{:S(2)}, u32[]{:S(2)}) %collective-permute-start.7) | collective-permute-done | bytes 131104 | tf_op jit(solution)/shard_map/ppermute | solution.py:526
  33.6 0.1 collective-permute-start.8
  33.7 0.6 %collective-permute-done.9.other_ref = bf16[512,128]{1,0:T(8,128)(2,1)S(1)} collective-permute-done((bf16[512,128]{1,0:T(8,128)(2,1)S(1)}, bf16[512,128]{1,0:T(8,128)(2,1)S(1)}, u32[]{:S(2)}, u32[]{:S(2)}) %collective-permute-start.9) | collective-permute-done | bytes 131104 | tf_op jit(solution)/shard_map/ppermute | solution.py:718
  34.3 0.7 %place.2 = (bf16[256,512]{1,0:T(8,128)(2,1)}, bf16[256,512]{1,0:T(8,128)(2,1)}) custom-call(bf16[512,128]{1,0:T(8,128)(2,1)S(1)} %finish.2.refs_2_.mine_ref, bf16[512,128]{1,0:T(8,128)(2,1)S(1)} %collective-permute-done.9.other_ref), custom_call_target="tpu_custom_call" | custom-call | tf_op jit(solution)/shard_map/place/pallas_call | solution.py:719
  35.0 0.7 %place.3 = (bf16[256,512]{1,0:T(8,128)(2,1)}, bf16[256,512]{1,0:T(8,128)(2,1)}) custom-call(bf16[512,128]{1,0:T(8,128)(2,1)S(1)} %finish.3.mine_ref, bf16[512,128]{1,0:T(8,128)(2,1)S(1)} %collective-permute-done.8.other_ref, bf16[256,512]{1,0:T(8,128)(2,1)} %get-tuple-element.81.refs_0_, ...), custom_call_target="tpu_custom_call", output_to_operand_aliasing={{0}: (2, {}), {1}: (3, {})} | custom-call | tf_op jit(solution)/shard_map/place/pallas_call | solution.py:719
  (9 shorter events, 0.2 us)
Async XLA Ops:
  1.6 0.7 %copy-start = (s32[256]{0:T(256)S(1)}, s32[256]{0:T(256)}, u32[]{:S(2)}) copy-start(s32[256]{0:T(256)} %param.9) | copy-start | bytes 3076
  2.4 9.5 %collective-permute-start.1 = (bf16[528,128]{1,0:T(8,128)(2,1)S(1)}, bf16[528,128]{1,0:T(8,128)(2,1)S(1)}, u32[]{:S(2)}, u32[]{:S(2)}) collective-permute-start(bf16[528,128]{1,0:T(8,128)(2,1)S(1)} %number.1.own_ref.refs_2_.refs_3_.refs_4_.refs_8_), channel_id=1, source_target_pairs={{0,4},{4,8},{8,12},{12,0},{16,20},{20,24},{24,28},{28,16},{1,5},{5... | collective-permute-start | bytes 405512 | tf_op jit(solution)/shard_map/ppermute | solution.py:526
  5.4 9.0 %collective-permute-start = (bf16[512,128]{1,0:T(8,128)(2,1)S(1)}, bf16[512,128]{1,0:T(8,128)(2,1)S(1)}, u32[]{:S(2)}, u32[]{:S(2)}) collective-permute-start(bf16[512,128]{1,0:T(8,128)(2,1)S(1)} %get-tuple-element.49.refs_3_), channel_id=1, source_target_pairs={{0,4},{4,8},{8,12},{12,0},{16,20},{20,24},{24,28},{28,16},{1,5},{5... | collective-permute-start | bytes 393224 | tf_op jit(solution)/shard_map/ppermute | solution.py:526
  11.9 6.2 %collective-permute-start.3 = (bf16[528,128]{1,0:T(8,128)(2,1)S(1)}, bf16[528,128]{1,0:T(8,128)(2,1)S(1)}, u32[]{:S(2)}, u32[]{:S(2)}) collective-permute-start(bf16[528,128]{1,0:T(8,128)(2,1)S(1)} %collective-permute-done.1.refs_6_.refs_3_.refs_4_), channel_id=1, source_target_pairs={{0,16},{4,8},{8,12},{12,4},{16,0},{20,24},{24,28},{28,20},{1,17},{... | collective-permute-start | bytes 405512 | tf_op jit(solution)/shard_map/ppermute | solution.py:526
  14.5 6.9 %collective-permute-start.2 = (bf16[512,128]{1,0:T(8,128)(2,1)S(1)}, bf16[512,128]{1,0:T(8,128)(2,1)S(1)}, u32[]{:S(2)}, u32[]{:S(2)}) collective-permute-start(bf16[512,128]{1,0:T(8,128)(2,1)S(1)} %collective-permute-done.refs_3_), channel_id=1, source_target_pairs={{0,16},{4,8},{8,12},{12,4},{16,0},{20,24},{24,28},{28,20},{1,17},{... | collective-permute-start | bytes 393224 | tf_op jit(solution)/shard_map/ppermute | solution.py:526
  18.2 7.4 %collective-permute-start.4 = (bf16[512,128]{1,0:T(8,128)(2,1)S(1)}, bf16[512,128]{1,0:T(8,128)(2,1)S(1)}, u32[]{:S(2)}, u32[]{:S(2)}) collective-permute-start(bf16[512,128]{1,0:T(8,128)(2,1)S(1)} %get-tuple-element.59.refs_7_), channel_id=1, source_target_pairs={{4,0},{8,4},{12,8},{0,12},{20,16},{24,20},{28,24},{16,28},{5,1},{9... | collective-permute-start | bytes 393224 | tf_op jit(solution)/shard_map/ppermute | solution.py:526
  21.5 6.9 %collective-permute-start.5 = (bf16[512,128]{1,0:T(8,128)(2,1)S(1)}, bf16[512,128]{1,0:T(8,128)(2,1)S(1)}, u32[]{:S(2)}, u32[]{:S(2)}) collective-permute-start(bf16[512,128]{1,0:T(8,128)(2,1)S(1)} %get-tuple-element.64.refs_10_), channel_id=1, source_target_pairs={{4,0},{8,4},{12,8},{0,12},{20,16},{24,20},{28,24},{16,28},{5,1},{9... | collective-permute-start | bytes 393224 | tf_op jit(solution)/shard_map/ppermute | solution.py:526
  25.7 7.1 %collective-permute-start.6 = (bf16[512,128]{1,0:T(8,128)(2,1)S(1)}, bf16[512,128]{1,0:T(8,128)(2,1)S(1)}, u32[]{:S(2)}, u32[]{:S(2)}) collective-permute-start(bf16[512,128]{1,0:T(8,128)(2,1)S(1)} %add_convert_fusion.1.refs_10_), channel_id=1, source_target_pairs={{4,0},{8,4},{12,8},{0,12},{20,16},{24,20},{28,24},{16,28},{5,1},{9... | collective-permute-start | bytes 393224 | tf_op jit(solution)/shard_map/ppermute | solution.py:526
  28.5 5.0 %collective-permute-start.7 = (bf16[512,128]{1,0:T(8,128)(2,1)S(1)}, bf16[512,128]{1,0:T(8,128)(2,1)S(1)}, u32[]{:S(2)}, u32[]{:S(2)}) collective-permute-start(bf16[512,128]{1,0:T(8,128)(2,1)S(1)} %add_convert_fusion.refs_9_), channel_id=1, source_target_pairs={{4,0},{8,4},{12,8},{0,12},{20,16},{24,20},{28,24},{16,28},{5,1},{9... | collective-permute-start | bytes 393224 | tf_op jit(solution)/shard_map/ppermute | solution.py:526
  32.9 1.4 %collective-permute-start.9 = (bf16[512,128]{1,0:T(8,128)(2,1)S(1)}, bf16[512,128]{1,0:T(8,128)(2,1)S(1)}, u32[]{:S(2)}, u32[]{:S(2)}) collective-permute-start(bf16[512,128]{1,0:T(8,128)(2,1)S(1)} %finish.2.refs_2_.mine_ref), channel_id=1, source_target_pairs={{0,1},{1,0},{2,3},{3,2},{4,5},{5,4},{6,7},{7,6},{8,9},{9,8},{10,11... | collective-permute-start | bytes 393224 | tf_op jit(solution)/shard_map/ppermute | solution.py:718
  33.6 1.4 %collective-permute-start.8 = (bf16[512,128]{1,0:T(8,128)(2,1)S(1)}, bf16[512,128]{1,0:T(8,128)(2,1)S(1)}, u32[]{:S(2)}, u32[]{:S(2)}) collective-permute-start(bf16[512,128]{1,0:T(8,128)(2,1)S(1)} %finish.3.mine_ref), channel_id=1, source_target_pairs={{0,1},{1,0},{2,3},{3,2},{4,5},{5,4},{6,7},{7,6},{8,9},{9,8},{10,11... | collective-permute-start | bytes 393224 | tf_op jit(solution)/shard_map/ppermute | solution.py:718

commit v2 on v1

--- a/solution.py
+++ b/solution.py
@@ -518,9 +518,8 @@
             route.append((at + ctx - 1, at + step - 1))
         return route
 
-    down = [
-        (group * ctx + (i + 1) % ctx, group * ctx + i) for group in range(groups) for i in range(ctx)
-    ]
+    def down(step):
+        return [(target, source) for source, target in up(step)]
 
     def moved(array, route):
         return lax.ppermute(array, ("groups", "ctx"), route)
@@ -660,7 +659,7 @@
 
     for step in range(reach - 1, 0, -1):
         mine = [None] * chunks
-        arriving = [moved(sums[chunk], down) for chunk in each]
+        arriving = [moved(sums[chunk], down(step + 1)) for chunk in each]
         for chunk in each:
             early_own = step == 1 and chunk == 0
             body = functools.partial(
@@ -686,9 +685,9 @@
                 here, finished[chunk - 1] = lax.optimization_barrier((here, finished[chunk - 1]))
             sums[chunk] = (mine[chunk] + here.astype(jnp.float32)).astype(jnp.bfloat16)
             if step == 1:
-                returning.append(moved(sums[chunk], down))
+                returning.append(moved(sums[chunk], down(1)))
     if reach == 1:
-        returning += [moved(sums[chunk], down) for chunk in each]
+        returning += [moved(sums[chunk], down(1)) for chunk in each]
     for chunk in each if reach == 1 else each[-1:]:
         own_grads(chunk)
 

time: 36.5 us -> 36 us (0.986); the launches traced: 35.9 us -> 35.9 us
  waiting for transfers between devices: 5.58 us -> 5.99 us
  starting transfers between devices: 17 us -> 16.6 us
    ppermute x8, starting transfers between devices: 16.9 us -> 16.3 us  [moved(): return lax.ppermute(array, ('groups', 'ctx'), route)]
  transfers between devices with their start and end apart: 10 -> 10, of which waited for: 4 -> 5; matrix products, arithmetic and copies ran while one was open for 0% -> 0% of each run, Pallas kernels for 27% -> 27%
where the time goes in v2:
time: 36 us; the launch traced here: 35.9 us
  starting transfers between devices  16.6 us (46%)
  Pallas kernels  11.6 us (32%)
  waiting for transfers between devices  5.99 us (17%)
  between operations  0.98 us (3%)
  local copies, waits for them, and re-layouts  0.67 us (2%)
    ppermute x8, starting transfers between devices, moved(): return lax.ppermute(array, ('groups', 'ctx'), route)  16.3 us
    pallas_call x12, Pallas kernels, call(): pl.pallas_call(kernel, out_shape=outs, in_specs=[WHOLE] * count + specs,...  7.36 us
    ppermute x8, waiting for transfers between devices, moved(): return lax.ppermute(array, ('groups', 'ctx'), route)  5.25 us
    pallas_call x1, Pallas kernels, shards(): pl.pallas_call(load_kernel, out_shape=(rows_shape, rows_shape), in_specs=...  1.73 us
    pallas_call x2, Pallas kernels, shards(): pl.pallas_call(functools.partial(place_kernel, chunk=chunk, chunks=chunks...  1.47 us
    pallas_call x1, Pallas kernels, shards(): pl.pallas_call(functools.partial(pack_kernel, first_of=first_of), out_sha...  0.99 us
    ppermute x2, waiting for transfers between devices, shards(): other = lax.ppermute(mine, 'kv', kv_swap)  0.74 us
  transfers between devices with their start and end apart: 10, of which 5 were waited for; matrix products, arithmetic and copies ran while one was open for 0% of the time, Pallas kernels for 27%

profile of v2, /device:TPU:0, one launch (start us, length us, event | category | flops | bytes accessed | tf_op | source)
XLA Modules:
  0.0 35.9 jit_solution(10611124986473829750)
XLA Ops:
  0.6 1.0 %pack.1 = (bf16[528,128]{1,0:T(8,128)(2,1)S(1)}, bf16[512,128]{1,0:T(8,128)(2,1)S(1)}) custom-call(bf16[256,512]{1,0:T(8,128)(2,1)} %k_ref.1, bf16[256,512]{1,0:T(8,128)(2,1)} %v_ref.1), custom_call_target="tpu_custom_call" | custom-call | bytes 4194304 | tf_op jit(solution)/shard_map/pack/pallas_call | solution.py:550
  1.6 0.0 copy-start
  1.6 0.7 %copy-done = s32[256]{0:T(256)S(1)} copy-done((s32[256]{0:T(256)S(1)}, s32[256]{0:T(256)}, u32[]{:S(2)}) %copy-start) | copy-done | bytes 1048
  2.4 3.1 %collective-permute-start.1 = (bf16[528,128]{1,0:T(8,128)(2,1)S(1)}, bf16[528,128]{1,0:T(8,128)(2,1)S(1)}, u32[]{:S(2)}, u32[]{:S(2)}) collective-permute-start(bf16[528,128]{1,0:T(8,128)(2,1)S(1)} %number.1.own_ref.refs_2_.refs_3_.refs_4_.refs_8_), channel_id=1, source_target_pairs={{0,4},{4,8},{8,12},{12,0},{16,20},{20,24},{24,28},{28,16},{1,5},{5... | collective-permute-start | bytes 405512 | tf_op jit(solution)/shard_map/ppermute | solution.py:525
  5.4 1.6 %collective-permute-start = (bf16[512,128]{1,0:T(8,128)(2,1)S(1)}, bf16[512,128]{1,0:T(8,128)(2,1)S(1)}, u32[]{:S(2)}, u32[]{:S(2)}) collective-permute-start(bf16[512,128]{1,0:T(8,128)(2,1)S(1)} %get-tuple-element.49.refs_3_), channel_id=1, source_target_pairs={{0,4},{4,8},{8,12},{12,0},{16,20},{20,24},{24,28},{28,16},{1,5},{5... | collective-permute-start | bytes 393224 | tf_op jit(solution)/shard_map/ppermute | solution.py:525
  7.0 1.7 %load.1 = (bf16[256,2048]{1,0:T(8,128)(2,1)S(1)}, bf16[256,2048]{1,0:T(8,128)(2,1)S(1)}) custom-call(bf16[256,2048]{1,0:T(8,128)(2,1)} %q_ref.1, bf16[256,2048]{1,0:T(8,128)(2,1)} %g_ref.1, bf16[528,128]{1,0:T(8,128)(2,1)S(1)} %number.1.own_ref.refs_2_.refs_3_.refs_4_.refs_8_), custom_call_target="tpu_custom_call" | custom-call | tf_op jit(solution)/shard_map/load/pallas_call | solution.py:572
  8.7 0.9 %stats_own.2 = (f32[3,8,256]{2,1,0:T(8,128)S(1)}, f32[256,256]{1,0:T(8,128)S(1)}) custom-call(bf16[256,2048]{1,0:T(8,128)(2,1)S(1)} %get-tuple-element.45.refs_0_, bf16[256,2048]{1,0:T(8,128)(2,1)S(1)} %get-tuple-element.46.refs_1_, bf16[528,128]{1,0:T(8,128)(2,1)S(1)} %number.1.own_ref.refs_2_.refs_3_.refs_4_.refs_8_, ...), custom_call_target="tpu_custom_call" | custom-call | flops 184480000 | bytes 8192 | tf_op jit(solution)/shard_map/stats_own/pallas_call | solution.py:536
  9.7 2.2 %collective-permute-done.1.refs_6_.refs_3_.refs_4_ = bf16[528,128]{1,0:T(8,128)(2,1)S(1)} collective-permute-done((bf16[528,128]{1,0:T(8,128)(2,1)S(1)}, bf16[528,128]{1,0:T(8,128)(2,1)S(1)}, u32[]{:S(2)}, u32[]{:S(2)}) %collective-permute-start.1) | collective-permute-done | bytes 135200 | tf_op jit(solution)/shard_map/ppermute | solution.py:525
  11.9 1.8 %collective-permute-start.3 = (bf16[528,128]{1,0:T(8,128)(2,1)S(1)}, bf16[528,128]{1,0:T(8,128)(2,1)S(1)}, u32[]{:S(2)}, u32[]{:S(2)}) collective-permute-start(bf16[528,128]{1,0:T(8,128)(2,1)S(1)} %collective-permute-done.1.refs_6_.refs_3_.refs_4_), channel_id=1, source_target_pairs={{0,16},{4,8},{8,12},{12,4},{16,0},{20,24},{24,28},{28,20},{1,17},{... | collective-permute-start | bytes 405512 | tf_op jit(solution)/shard_map/ppermute | solution.py:525
  13.6 0.8 %stats_own.3.refs_5_ = f32[3,8,256]{2,1,0:T(8,128)S(1)} custom-call(bf16[256,2048]{1,0:T(8,128)(2,1)S(1)} %get-tuple-element.45.refs_0_, bf16[256,2048]{1,0:T(8,128)(2,1)S(1)} %get-tuple-element.46.refs_1_, bf16[528,128]{1,0:T(8,128)(2,1)S(1)} %number.1.own_ref.refs_2_.refs_3_.refs_4_.refs_8_, bf16[512,128]{1,0:T(8,128)(2,1)S(1)} %get-tuple-element.49.refs_3_, ...), custom_call_target="tpu_custom_call" | custom-call | flops 184480000 | bytes 8192 | tf_op jit(solution)/shard_map/stats_own/pallas_call | solution.py:536
  14.5 0.0 collective-permute-done.refs_3_
  14.5 1.2 %collective-permute-start.2 = (bf16[512,128]{1,0:T(8,128)(2,1)S(1)}, bf16[512,128]{1,0:T(8,128)(2,1)S(1)}, u32[]{:S(2)}, u32[]{:S(2)}) collective-permute-start(bf16[512,128]{1,0:T(8,128)(2,1)S(1)} %collective-permute-done.refs_3_), channel_id=1, source_target_pairs={{0,16},{4,8},{8,12},{12,4},{16,0},{20,24},{24,28},{28,20},{1,17},{... | collective-permute-start | bytes 393224 | tf_op jit(solution)/shard_map/ppermute | solution.py:525
  15.6 0.1 stats.2
  15.8 0.1 stats.3.refs_6_.refs_5_
  15.9 2.1 %collective-permute-done.3.refs_3_.refs_4_ = bf16[528,128]{1,0:T(8,128)(2,1)S(1)} collective-permute-done((bf16[528,128]{1,0:T(8,128)(2,1)S(1)}, bf16[528,128]{1,0:T(8,128)(2,1)S(1)}, u32[]{:S(2)}, u32[]{:S(2)}) %collective-permute-start.3) | collective-permute-done | bytes 135200 | tf_op jit(solution)/shard_map/ppermute | solution.py:525
  18.0 0.2 grads_far.2
  18.2 2.1 %collective-permute-start.4 = (bf16[512,128]{1,0:T(8,128)(2,1)S(1)}, bf16[512,128]{1,0:T(8,128)(2,1)S(1)}, u32[]{:S(2)}, u32[]{:S(2)}) collective-permute-start(bf16[512,128]{1,0:T(8,128)(2,1)S(1)} %get-tuple-element.59.refs_7_), channel_id=1, source_target_pairs={{16,0},{8,4},{12,8},{4,12},{0,16},{24,20},{28,24},{20,28},{17,1},{... | collective-permute-start | bytes 393224 | tf_op jit(solution)/shard_map/ppermute | solution.py:525
  20.3 0.6 %collective-permute-done.2.refs_3_ = bf16[512,128]{1,0:T(8,128)(2,1)S(1)} collective-permute-done((bf16[512,128]{1,0:T(8,128)(2,1)S(1)}, bf16[512,128]{1,0:T(8,128)(2,1)S(1)}, u32[]{:S(2)}, u32[]{:S(2)}) %collective-permute-start.2) | collective-permute-done | bytes 131104 | tf_op jit(solution)/shard_map/ppermute | solution.py:525
  21.0 0.2 grads_far.3
  21.2 1.8 %collective-permute-start.5 = (bf16[512,128]{1,0:T(8,128)(2,1)S(1)}, bf16[512,128]{1,0:T(8,128)(2,1)S(1)}, u32[]{:S(2)}, u32[]{:S(2)}) collective-permute-start(bf16[512,128]{1,0:T(8,128)(2,1)S(1)} %get-tuple-element.64.refs_10_), channel_id=1, source_target_pairs={{16,0},{8,4},{12,8},{4,12},{0,16},{24,20},{28,24},{20,28},{17,1},{... | collective-permute-start | bytes 393224 | tf_op jit(solution)/shard_map/ppermute | solution.py:525
  22.9 2.3 %grads.2 = (f32[512,128]{1,0:T(8,128)S(1)}, f32[8,128,256]{2,1,0:T(8,128)S(1)}, f32[512,128]{1,0:T(8,128)S(1)}, bf16[256,2048]{1,0:T(8,128)(2,1)}) custom-call(bf16[256,2048]{1,0:T(8,128)(2,1)S(1)} %get-tuple-element.45.refs_0_, bf16[256,2048]{1,0:T(8,128)(2,1)S(1)} %get-tuple-element.46.refs_1_, ...), custom_call_target="tpu_custom_call" | custom-call | flops 368960000 | bytes 8192 | tf_op jit(solution)/shard_map/grads/pallas_call | solution.py:536
  25.2 0.4 %grads.3 = (f32[512,128]{1,0:T(8,128)S(1)}, f32[8,128,256]{2,1,0:T(8,128)S(1)}) custom-call(bf16[256,2048]{1,0:T(8,128)(2,1)S(1)} %get-tuple-element.45.refs_0_, bf16[256,2048]{1,0:T(8,128)(2,1)S(1)} %get-tuple-element.46.refs_1_, bf16[528,128]{1,0:T(8,128)(2,1)S(1)} %number.1.own_ref.refs_2_.refs_3_.refs_4_.refs_8_, ...), custom_call_target="tpu_custom_call" | custom-call | flops 368960000 | bytes 8192 | tf_op jit(solution)/shard_map/grads/pallas_call | solution.py:536
  25.7 2.3 %collective-permute-start.6 = (bf16[512,128]{1,0:T(8,128)(2,1)S(1)}, bf16[512,128]{1,0:T(8,128)(2,1)S(1)}, u32[]{:S(2)}, u32[]{:S(2)}) collective-permute-start(bf16[512,128]{1,0:T(8,128)(2,1)S(1)} %add_convert_fusion.1.refs_10_), channel_id=1, source_target_pairs={{4,0},{8,4},{12,8},{0,12},{20,16},{24,20},{28,24},{16,28},{5,1},{9... | collective-permute-start | bytes 393224 | tf_op jit(solution)/shard_map/ppermute | solution.py:525
  28.0 0.2 grads_own.2
  28.2 2.6 %collective-permute-start.7 = (bf16[512,128]{1,0:T(8,128)(2,1)S(1)}, bf16[512,128]{1,0:T(8,128)(2,1)S(1)}, u32[]{:S(2)}, u32[]{:S(2)}) collective-permute-start(bf16[512,128]{1,0:T(8,128)(2,1)S(1)} %add_convert_fusion.refs_9_), channel_id=1, source_target_pairs={{4,0},{8,4},{12,8},{0,12},{20,16},{24,20},{28,24},{16,28},{5,1},{9... | collective-permute-start | bytes 393224 | tf_op jit(solution)/shard_map/ppermute | solution.py:525
  30.7 2.1 %grads_own.3 = (f32[512,128]{1,0:T(8,128)S(1)}, bf16[256,2048]{1,0:T(8,128)(2,1)}) custom-call(bf16[256,2048]{1,0:T(8,128)(2,1)S(1)} %get-tuple-element.45.refs_0_, bf16[256,2048]{1,0:T(8,128)(2,1)S(1)} %get-tuple-element.46.refs_1_, bf16[528,128]{1,0:T(8,128)(2,1)S(1)} %number.1.own_ref.refs_2_.refs_3_.refs_4_.refs_8_, ...), custom_call_target="tpu_custom_call", output_to_operand_aliasing={{1}: (8, {})} | custom-call | flops 415080000 | bytes 8192 | tf_op jit(solution)/shard_map/grads_own/pallas_call | solution.py:536
  32.9 0.1 collective-permute-start.9
  33.0 0.3 collective-permute-done.7.refs_1_
  33.3 0.3 collective-permute-start.8
  33.6 0.7 %collective-permute-done.9.other_ref = bf16[512,128]{1,0:T(8,128)(2,1)S(1)} collective-permute-done((bf16[512,128]{1,0:T(8,128)(2,1)S(1)}, bf16[512,128]{1,0:T(8,128)(2,1)S(1)}, u32[]{:S(2)}, u32[]{:S(2)}) %collective-permute-start.9) | collective-permute-done | bytes 131104 | tf_op jit(solution)/shard_map/ppermute | solution.py:717
  34.3 0.7 %place.2 = (bf16[256,512]{1,0:T(8,128)(2,1)}, bf16[256,512]{1,0:T(8,128)(2,1)}) custom-call(bf16[512,128]{1,0:T(8,128)(2,1)S(1)} %finish.2.refs_2_.mine_ref, bf16[512,128]{1,0:T(8,128)(2,1)S(1)} %collective-permute-done.9.other_ref), custom_call_target="tpu_custom_call" | custom-call | tf_op jit(solution)/shard_map/place/pallas_call | solution.py:718
  35.0 0.7 %place.3 = (bf16[256,512]{1,0:T(8,128)(2,1)}, bf16[256,512]{1,0:T(8,128)(2,1)}) custom-call(bf16[512,128]{1,0:T(8,128)(2,1)S(1)} %finish.3.mine_ref, bf16[512,128]{1,0:T(8,128)(2,1)S(1)} %collective-permute-done.8.other_ref, bf16[256,512]{1,0:T(8,128)(2,1)} %get-tuple-element.81.refs_0_, ...), custom_call_target="tpu_custom_call", output_to_operand_aliasing={{0}: (2, {}), {1}: (3, {})} | custom-call | tf_op jit(solution)/shard_map/place/pallas_call | solution.py:718
  (9 shorter events, 0.2 us)
Async XLA Ops:
  1.6 0.7 %copy-start = (s32[256]{0:T(256)S(1)}, s32[256]{0:T(256)}, u32[]{:S(2)}) copy-start(s32[256]{0:T(256)} %param.9) | copy-start | bytes 3076
  2.4 9.5 %collective-permute-start.1 = (bf16[528,128]{1,0:T(8,128)(2,1)S(1)}, bf16[528,128]{1,0:T(8,128)(2,1)S(1)}, u32[]{:S(2)}, u32[]{:S(2)}) collective-permute-start(bf16[528,128]{1,0:T(8,128)(2,1)S(1)} %number.1.own_ref.refs_2_.refs_3_.refs_4_.refs_8_), channel_id=1, source_target_pairs={{0,4},{4,8},{8,12},{12,0},{16,20},{20,24},{24,28},{28,16},{1,5},{5... | collective-permute-start | bytes 405512 | tf_op jit(solution)/shard_map/ppermute | solution.py:525
  5.4 9.0 %collective-permute-start = (bf16[512,128]{1,0:T(8,128)(2,1)S(1)}, bf16[512,128]{1,0:T(8,128)(2,1)S(1)}, u32[]{:S(2)}, u32[]{:S(2)}) collective-permute-start(bf16[512,128]{1,0:T(8,128)(2,1)S(1)} %get-tuple-element.49.refs_3_), channel_id=1, source_target_pairs={{0,4},{4,8},{8,12},{12,0},{16,20},{20,24},{24,28},{28,16},{1,5},{5... | collective-permute-start | bytes 393224 | tf_op jit(solution)/shard_map/ppermute | solution.py:525
  11.9 6.2 %collective-permute-start.3 = (bf16[528,128]{1,0:T(8,128)(2,1)S(1)}, bf16[528,128]{1,0:T(8,128)(2,1)S(1)}, u32[]{:S(2)}, u32[]{:S(2)}) collective-permute-start(bf16[528,128]{1,0:T(8,128)(2,1)S(1)} %collective-permute-done.1.refs_6_.refs_3_.refs_4_), channel_id=1, source_target_pairs={{0,16},{4,8},{8,12},{12,4},{16,0},{20,24},{24,28},{28,20},{1,17},{... | collective-permute-start | bytes 405512 | tf_op jit(solution)/shard_map/ppermute | solution.py:525
  14.5 6.5 %collective-permute-start.2 = (bf16[512,128]{1,0:T(8,128)(2,1)S(1)}, bf16[512,128]{1,0:T(8,128)(2,1)S(1)}, u32[]{:S(2)}, u32[]{:S(2)}) collective-permute-start(bf16[512,128]{1,0:T(8,128)(2,1)S(1)} %collective-permute-done.refs_3_), channel_id=1, source_target_pairs={{0,16},{4,8},{8,12},{12,4},{16,0},{20,24},{24,28},{28,20},{1,17},{... | collective-permute-start | bytes 393224 | tf_op jit(solution)/shard_map/ppermute | solution.py:525
  18.2 7.4 %collective-permute-start.4 = (bf16[512,128]{1,0:T(8,128)(2,1)S(1)}, bf16[512,128]{1,0:T(8,128)(2,1)S(1)}, u32[]{:S(2)}, u32[]{:S(2)}) collective-permute-start(bf16[512,128]{1,0:T(8,128)(2,1)S(1)} %get-tuple-element.59.refs_7_), channel_id=1, source_target_pairs={{16,0},{8,4},{12,8},{4,12},{0,16},{24,20},{28,24},{20,28},{17,1},{... | collective-permute-start | bytes 393224 | tf_op jit(solution)/shard_map/ppermute | solution.py:525
  21.2 7.0 %collective-permute-start.5 = (bf16[512,128]{1,0:T(8,128)(2,1)S(1)}, bf16[512,128]{1,0:T(8,128)(2,1)S(1)}, u32[]{:S(2)}, u32[]{:S(2)}) collective-permute-start(bf16[512,128]{1,0:T(8,128)(2,1)S(1)} %get-tuple-element.64.refs_10_), channel_id=1, source_target_pairs={{16,0},{8,4},{12,8},{4,12},{0,16},{24,20},{28,24},{20,28},{17,1},{... | collective-permute-start | bytes 393224 | tf_op jit(solution)/shard_map/ppermute | solution.py:525
  25.7 7.2 %collective-permute-start.6 = (bf16[512,128]{1,0:T(8,128)(2,1)S(1)}, bf16[512,128]{1,0:T(8,128)(2,1)S(1)}, u32[]{:S(2)}, u32[]{:S(2)}) collective-permute-start(bf16[512,128]{1,0:T(8,128)(2,1)S(1)} %add_convert_fusion.1.refs_10_), channel_id=1, source_target_pairs={{4,0},{8,4},{12,8},{0,12},{20,16},{24,20},{28,24},{16,28},{5,1},{9... | collective-permute-start | bytes 393224 | tf_op jit(solution)/shard_map/ppermute | solution.py:525
  28.2 5.1 %collective-permute-start.7 = (bf16[512,128]{1,0:T(8,128)(2,1)S(1)}, bf16[512,128]{1,0:T(8,128)(2,1)S(1)}, u32[]{:S(2)}, u32[]{:S(2)}) collective-permute-start(bf16[512,128]{1,0:T(8,128)(2,1)S(1)} %add_convert_fusion.refs_9_), channel_id=1, source_target_pairs={{4,0},{8,4},{12,8},{0,12},{20,16},{24,20},{28,24},{16,28},{5,1},{9... | collective-permute-start | bytes 393224 | tf_op jit(solution)/shard_map/ppermute | solution.py:525
  32.9 1.4 %collective-permute-start.9 = (bf16[512,128]{1,0:T(8,128)(2,1)S(1)}, bf16[512,128]{1,0:T(8,128)(2,1)S(1)}, u32[]{:S(2)}, u32[]{:S(2)}) collective-permute-start(bf16[512,128]{1,0:T(8,128)(2,1)S(1)} %finish.2.refs_2_.mine_ref), channel_id=1, source_target_pairs={{0,1},{1,0},{2,3},{3,2},{4,5},{5,4},{6,7},{7,6},{8,9},{9,8},{10,11... | collective-permute-start | bytes 393224 | tf_op jit(solution)/shard_map/ppermute | solution.py:717
  33.3 1.7 %collective-permute-start.8 = (bf16[512,128]{1,0:T(8,128)(2,1)S(1)}, bf16[512,128]{1,0:T(8,128)(2,1)S(1)}, u32[]{:S(2)}, u32[]{:S(2)}) collective-permute-start(bf16[512,128]{1,0:T(8,128)(2,1)S(1)} %finish.3.mine_ref), channel_id=1, source_target_pairs={{0,1},{1,0},{2,3},{3,2},{4,5},{5,4},{6,7},{7,6},{8,9},{9,8},{10,11... | collective-permute-start | bytes 393224 | tf_op jit(solution)/shard_map/ppermute | solution.py:717

commit v3 on v2

--- a/solution.py
+++ b/solution.py
@@ -287,11 +287,11 @@
         out_ref[...] = in_ref[...]
 
 
-def far_kernel(ins, outs, scratch, *, fill, chunk, per_kv, factor, step):
+def far_kernel(ins, outs, scratch, *, early_own, fill, chunk, per_kv, factor, scale, step):
     q_ref, g_ref, own_seg_ref, kv_ref, kv_seg_ref, in_ref = ins[:6]
     out_ref, kv_grad_ref, dq_ref = outs[:3]
-    bias_ref = outs[3] if fill else ins[-1]
-    kt_ref, acc_ref = scratch
+    bias_ref = outs[-1] if fill else ins[-1]
+    kt_ref, acc_ref = scratch[:2]
     rows = q_ref.shape[0]
     half = rows // 2
     active, early = activity(own_seg_ref, kv_seg_ref, step, rows)
@@ -354,11 +354,21 @@
     def _():
         dq_ref[...] = jnp.zeros_like(dq_ref)
         kv_grad_ref[...] = jnp.zeros_like(kv_grad_ref)
-
-
-def grads_kernel(ins, outs, scratch, *, early_own, chunk, per_kv, factor, scale, step):
-    q_ref, g_ref, own_seg_ref, kv_ref, kv_seg_ref, in_ref, dq_in_ref, bias_ref = ins[:8]
-    kv_grad_ref, dq_ref = outs[:2]
+        if early_own:
+            own_kv_ref, near_seg_ref, own_bias_ref = ins[6:9]
+            near, _ = activity(own_seg_ref, near_seg_ref, 1, rows)
+
+            @pl.when(jnp.logical_not(near))
+            def _():
+                own_run(
+                    (q_ref, g_ref, own_kv_ref, out_ref, dq_ref, own_bias_ref), outs[3:5],
+                    (kt_ref, *scratch[2:]), chunk, per_kv, factor, scale,
+                )
+
+
+def grads_kernel(ins, outs, scratch, *, chunk, per_kv, factor, step):
+    q_ref, g_ref, own_seg_ref, kv_ref, kv_seg_ref, in_ref, dq_in_ref, bias_ref = ins
+    kv_grad_ref, dq_ref = outs
     kt_ref = scratch[0]
     rows = q_ref.shape[0]
 
@@ -385,12 +395,6 @@
     def _():
         kv_grad_ref[...] = jnp.zeros_like(kv_grad_ref)
         dq_ref[...] = dq_in_ref[...]
-        if early_own:
-            own_kv_ref, own_bias_ref = ins[8:]
-            own_run(
-                (q_ref, g_ref, own_kv_ref, in_ref, dq_in_ref, own_bias_ref), outs[2:], scratch,
-                chunk, per_kv, factor, scale,
-            )
 
 
 def own_run(ins, outs, scratch, chunk, per_kv, factor, scale):
@@ -595,14 +599,15 @@
     def common_operands(chunk, step):
         return queries, out_grad, own[0], blocks[chunk][step], blocks[0][step]
 
-    def with_bias(kernel, chunk, step, operands, outs, scratch, name, micros, after=()):
+    def with_bias(kernel, chunk, step, operands, outs, scratch, name, micros, after=(), specs=None, **options):
         fill = biases[step] is None
-        body = functools.partial(kernel, fill=fill, chunk=chunk, step=step, **common)
+        body = functools.partial(kernel, fill=fill, chunk=chunk, step=step, **options, **common)
         operands = common_operands(chunk, step) + operands
+        specs = specs or (WHOLE,) * len(outs)
         if not fill:
-            return call(body, operands + (biases[step],), outs, scratch, name, micros, after=after)
+            return call(body, operands + (biases[step],), outs, scratch, name, micros, specs, after=after)
         *results, biases[step] = call(
-            body, operands, outs + (bias_shape,), scratch, name, micros, after=after
+            body, operands, outs + (bias_shape,), scratch, name, micros, specs + (WHOLE,), after=after
         )
         return results
 
@@ -621,21 +626,38 @@
             (stats[chunk],) = with_bias(
                 stats_kernel, chunk, step, (stats[chunk],), (stats_shape,), [], "stats", 1.1
             )
-    before = [stats[-1]]
-    for chunk in each:
-        final_stats[chunk], sums[chunk], dq[chunk] = with_bias(
-            far_kernel, chunk, reach, (stats[chunk],), (finals_shape, sent_shape, dq_shape),
-            [turned, total_sum], "grads_far", 1.6, before,
-        )
-        before = [sums[chunk]]
     finished, returning, query_grad = [None] * chunks, [], []
     own_outs = (kv_grad_shape, jax.ShapeDtypeStruct(queries.shape, jnp.bfloat16))
     own_specs = (WHOLE, ANYWHERE)
-    own_scratch = [
-        turned,
+    written_scratch = [
         pltpu.VMEM((rows, per_kv * HEAD_SIZE), jnp.bfloat16),
         pltpu.SemaphoreType.DMA((per_kv // 2,)),
     ]
+    own_scratch = [turned] + written_scratch
+
+    def far_grads(chunk, before):
+        operands = (stats[chunk],)
+        outs, specs, scratch = (finals_shape, sent_shape, dq_shape), (WHOLE,) * 3, [turned, total_sum]
+        early_own = chunk == 0
+        if early_own:
+            operands += (own[chunk], blocks[0][1], biases[0])
+            outs, specs, scratch = outs + own_outs, specs + own_specs, scratch + written_scratch
+        final_stats[chunk], sums[chunk], dq[chunk], *rest = with_bias(
+            far_kernel, chunk, reach, operands, outs, scratch, "grads_far", 1.3, before, specs,
+            early_own=early_own, scale=scale,
+        )
+        if early_own:
+            finished[chunk] = rest[0]
+            query_grad.append(rest[1])
+        return [sums[chunk]]
+
+    def block_grads(chunk, step, before):
+        body = functools.partial(grads_kernel, chunk=chunk, step=step, **common)
+        operands = common_operands(chunk, step) + (final_stats[chunk], dq[chunk], biases[step])
+        mine[chunk], dq[chunk] = call(
+            body, operands, (kv_grad_shape, dq_shape), [turned], "grads", 1.6, after=before
+        )
+        return [mine[chunk]]
 
     def own_grads(chunk):
         done_before = finished[chunk] is not None
@@ -657,26 +679,18 @@
         )
         query_grad.append(written)
 
+    mine, arriving = [None] * chunks, [None] * chunks
+    before = [stats[-1]]
+    for chunk in each:
+        before = far_grads(chunk, before)
+        arriving[chunk] = moved(sums[chunk], down(reach))
+        if reach > 1:
+            before = block_grads(chunk, reach - 1, before)
     for step in range(reach - 1, 0, -1):
-        mine = [None] * chunks
-        arriving = [moved(sums[chunk], down(step + 1)) for chunk in each]
-        for chunk in each:
-            early_own = step == 1 and chunk == 0
-            body = functools.partial(
-                grads_kernel, early_own=early_own, chunk=chunk, step=step, scale=scale, **common
-            )
-            operands = common_operands(chunk, step) + (final_stats[chunk], dq[chunk], biases[step])
-            outs, specs, scratch = (kv_grad_shape, dq_shape), (WHOLE, WHOLE), [turned]
-            if early_own:
-                operands += (blocks[chunk][0], biases[0])
-                outs, specs, scratch = outs + own_outs, specs + own_specs, own_scratch
-            mine[chunk], dq[chunk], *rest = call(
-                body, operands, outs, scratch, "grads", 1.6, out_specs=specs, after=before
-            )
-            if early_own:
-                finished[chunk] = rest[0]
-                query_grad.append(rest[1])
-            before = [mine[chunk]]
+        if step + 1 < reach:
+            arriving = [moved(sums[chunk], down(step + 1)) for chunk in each]
+            for chunk in each:
+                before = block_grads(chunk, step, before)
         arriving[0], mine[-1] = lax.optimization_barrier((arriving[0], mine[-1]))
         for chunk in each:
             here = arriving[chunk]
@@ -687,7 +701,7 @@
             if step == 1:
                 returning.append(moved(sums[chunk], down(1)))
     if reach == 1:
-        returning += [moved(sums[chunk], down(1)) for chunk in each]
+        returning += arriving
     for chunk in each if reach == 1 else each[-1:]:
         own_grads(chunk)
 

time: 36 us -> 36.6 us (1.017)
  waiting for transfers between devices: 5.99 us -> 7.45 us
  starting transfers between devices: 16.6 us -> 15.8 us
    ppermute x8, waiting for transfers between devices: 5.25 us -> 6.72 us  [moved(): return lax.ppermute(array, ('groups', 'ctx'), route)]
    ppermute x8, starting transfers between devices: 16.3 us -> 15.4 us  [moved(): return lax.ppermute(array, ('groups', 'ctx'), route)]
where the time goes in v3:
time: 36.6 us
  starting transfers between devices  15.8 us (43%)
  Pallas kernels  11.7 us (32%)
  waiting for transfers between devices  7.45 us (20%)
  between operations  0.98 us (3%)
  local copies, waits for them, and re-layouts  0.67 us (2%)
    ppermute x8, starting transfers between devices, moved(): return lax.ppermute(array, ('groups', 'ctx'), route)  15.4 us
    pallas_call x12, Pallas kernels, call(): pl.pallas_call(kernel, out_shape=outs, in_specs=[WHOLE] * count + specs,...  7.43 us
    ppermute x8, waiting for transfers between devices, moved(): return lax.ppermute(array, ('groups', 'ctx'), route)  6.72 us
    pallas_call x1, Pallas kernels, shards(): pl.pallas_call(load_kernel, out_shape=(rows_shape, rows_shape), in_specs=...  1.73 us
    pallas_call x2, Pallas kernels, shards(): pl.pallas_call(functools.partial(place_kernel, chunk=chunk, chunks=chunks...  1.47 us
    pallas_call x1, Pallas kernels, shards(): pl.pallas_call(functools.partial(pack_kernel, first_of=first_of), out_sha...  0.99 us
  transfers between devices with their start and end apart: 10, of which 5 were waited for; matrix products, arithmetic and copies ran while one was open for 0% of the time, Pallas kernels for 27%

profile of v3, /device:TPU:0, one launch (start us, length us, event | category | flops | bytes accessed | tf_op | source)
XLA Modules:
  0.0 36.6 jit_solution(1744543878440213816)
XLA Ops:
  0.6 1.0 %pack.1 = (bf16[528,128]{1,0:T(8,128)(2,1)S(1)}, bf16[512,128]{1,0:T(8,128)(2,1)S(1)}) custom-call(bf16[256,512]{1,0:T(8,128)(2,1)} %k_ref.1, bf16[256,512]{1,0:T(8,128)(2,1)} %v_ref.1), custom_call_target="tpu_custom_call" | custom-call | bytes 4194304 | tf_op jit(solution)/shard_map/pack/pallas_call | solution.py:554
  1.6 0.0 copy-start
  1.6 0.7 %copy-done = s32[256]{0:T(256)S(1)} copy-done((s32[256]{0:T(256)S(1)}, s32[256]{0:T(256)}, u32[]{:S(2)}) %copy-start) | copy-done | bytes 1048
  2.4 3.1 %collective-permute-start.1 = (bf16[528,128]{1,0:T(8,128)(2,1)S(1)}, bf16[528,128]{1,0:T(8,128)(2,1)S(1)}, u32[]{:S(2)}, u32[]{:S(2)}) collective-permute-start(bf16[528,128]{1,0:T(8,128)(2,1)S(1)} %number.1.own_ref.refs_2_.refs_3_.refs_4_.refs_6_), channel_id=1, source_target_pairs={{0,4},{4,8},{8,12},{12,0},{16,20},{20,24},{24,28},{28,16},{1,5},{5... | collective-permute-start | bytes 405512 | tf_op jit(solution)/shard_map/ppermute | solution.py:529
  5.4 1.6 %collective-permute-start = (bf16[512,128]{1,0:T(8,128)(2,1)S(1)}, bf16[512,128]{1,0:T(8,128)(2,1)S(1)}, u32[]{:S(2)}, u32[]{:S(2)}) collective-permute-start(bf16[512,128]{1,0:T(8,128)(2,1)S(1)} %get-tuple-element.49.refs_3_), channel_id=1, source_target_pairs={{0,4},{4,8},{8,12},{12,0},{16,20},{20,24},{24,28},{28,16},{1,5},{5... | collective-permute-start | bytes 393224 | tf_op jit(solution)/shard_map/ppermute | solution.py:529
  7.0 1.7 %load.1 = (bf16[256,2048]{1,0:T(8,128)(2,1)S(1)}, bf16[256,2048]{1,0:T(8,128)(2,1)S(1)}) custom-call(bf16[256,2048]{1,0:T(8,128)(2,1)} %q_ref.1, bf16[256,2048]{1,0:T(8,128)(2,1)} %g_ref.1, bf16[528,128]{1,0:T(8,128)(2,1)S(1)} %number.1.own_ref.refs_2_.refs_3_.refs_4_.refs_6_), custom_call_target="tpu_custom_call" | custom-call | tf_op jit(solution)/shard_map/load/pallas_call | solution.py:576
  8.7 0.9 %stats_own.2 = (f32[3,8,256]{2,1,0:T(8,128)S(1)}, f32[256,256]{1,0:T(8,128)S(1)}) custom-call(bf16[256,2048]{1,0:T(8,128)(2,1)S(1)} %get-tuple-element.45.refs_0_, bf16[256,2048]{1,0:T(8,128)(2,1)S(1)} %get-tuple-element.46.refs_1_, bf16[528,128]{1,0:T(8,128)(2,1)S(1)} %number.1.own_ref.refs_2_.refs_3_.refs_4_.refs_6_, ...), custom_call_target="tpu_custom_call" | custom-call | flops 184480000 | bytes 8192 | tf_op jit(solution)/shard_map/stats_own/pallas_call | solution.py:540
  9.7 2.2 %collective-permute-done.1.refs_6_.refs_3_.refs_4_.refs_7_ = bf16[528,128]{1,0:T(8,128)(2,1)S(1)} collective-permute-done((bf16[528,128]{1,0:T(8,128)(2,1)S(1)}, bf16[528,128]{1,0:T(8,128)(2,1)S(1)}, u32[]{:S(2)}, u32[]{:S(2)}) %collective-permute-start.1) | collective-permute-done | bytes 135200 | tf_op jit(solution)/shard_map/ppermute | solution.py:529
  11.9 1.8 %collective-permute-start.3 = (bf16[528,128]{1,0:T(8,128)(2,1)S(1)}, bf16[528,128]{1,0:T(8,128)(2,1)S(1)}, u32[]{:S(2)}, u32[]{:S(2)}) collective-permute-start(bf16[528,128]{1,0:T(8,128)(2,1)S(1)} %collective-permute-done.1.refs_6_.refs_3_.refs_4_.refs_7_), channel_id=1, source_target_pairs={{0,16},{4,8},{8,12},{12,4},{16,0},{20,24},{24,28},{28,20},{1,17},{... | collective-permute-start | bytes 405512 | tf_op jit(solution)/shard_map/ppermute | solution.py:529
  13.6 0.8 %stats_own.3.refs_5_ = f32[3,8,256]{2,1,0:T(8,128)S(1)} custom-call(bf16[256,2048]{1,0:T(8,128)(2,1)S(1)} %get-tuple-element.45.refs_0_, bf16[256,2048]{1,0:T(8,128)(2,1)S(1)} %get-tuple-element.46.refs_1_, bf16[528,128]{1,0:T(8,128)(2,1)S(1)} %number.1.own_ref.refs_2_.refs_3_.refs_4_.refs_6_, bf16[512,128]{1,0:T(8,128)(2,1)S(1)} %get-tuple-element.49.refs_3_, ...), custom_call_target="tpu_custom_call" | custom-call | flops 184480000 | bytes 8192 | tf_op jit(solution)/shard_map/stats_own/pallas_call | solution.py:540
  14.5 1.2 %collective-permute-start.2 = (bf16[512,128]{1,0:T(8,128)(2,1)S(1)}, bf16[512,128]{1,0:T(8,128)(2,1)S(1)}, u32[]{:S(2)}, u32[]{:S(2)}) collective-permute-start(bf16[512,128]{1,0:T(8,128)(2,1)S(1)} %collective-permute-done.refs_3_), channel_id=1, source_target_pairs={{0,16},{4,8},{8,12},{12,4},{16,0},{20,24},{24,28},{28,20},{1,17},{... | collective-permute-start | bytes 393224 | tf_op jit(solution)/shard_map/ppermute | solution.py:529
  15.6 0.1 stats.2
  15.8 0.1 stats.3.refs_9_.refs_5_
  15.9 2.2 %collective-permute-done.3.refs_3_.refs_4_ = bf16[528,128]{1,0:T(8,128)(2,1)S(1)} collective-permute-done((bf16[528,128]{1,0:T(8,128)(2,1)S(1)}, bf16[528,128]{1,0:T(8,128)(2,1)S(1)}, u32[]{:S(2)}, u32[]{:S(2)}) %collective-permute-start.3) | collective-permute-done | bytes 135200 | tf_op jit(solution)/shard_map/ppermute | solution.py:529
  18.0 2.3 %grads_far.2 = (f32[2,8,256]{2,1,0:T(8,128)S(1)}, bf16[512,128]{1,0:T(8,128)(2,1)S(1)}, f32[8,128,256]{2,1,0:T(8,128)S(1)}, f32[512,128]{1,0:T(8,128)S(1)}, bf16...) custom-call(bf16[256,2048]{1,0:T(8,128)(2,1)S(1)} %get-tuple-element.45.refs_0_, ...), custom_call_target="tpu_custom_call" | custom-call | flops 299780000 | bytes 8192 | tf_op jit(solution)/shard_map/grads_far/pallas_call | solution.py:540
  20.4 1.9 %collective-permute-start.4 = (bf16[512,128]{1,0:T(8,128)(2,1)S(1)}, bf16[512,128]{1,0:T(8,128)(2,1)S(1)}, u32[]{:S(2)}, u32[]{:S(2)}) collective-permute-start(bf16[512,128]{1,0:T(8,128)(2,1)S(1)} %get-tuple-element.61.refs_8_), channel_id=1, source_target_pairs={{16,0},{8,4},{12,8},{4,12},{0,16},{24,20},{28,24},{20,28},{17,1},{... | collective-permute-start | bytes 393224 | tf_op jit(solution)/shard_map/ppermute | solution.py:529
  22.2 0.2 grads.2
  22.4 0.0 collective-permute-done.2.refs_3_
  22.4 0.2 grads_far.3
  22.7 0.3 collective-permute-start.5
  22.9 0.4 %grads.3 = (f32[512,128]{1,0:T(8,128)S(1)}, f32[8,128,256]{2,1,0:T(8,128)S(1)}) custom-call(bf16[256,2048]{1,0:T(8,128)(2,1)S(1)} %get-tuple-element.45.refs_0_, bf16[256,2048]{1,0:T(8,128)(2,1)S(1)} %get-tuple-element.46.refs_1_, bf16[528,128]{1,0:T(8,128)(2,1)S(1)} %number.1.own_ref.refs_2_.refs_3_.refs_4_.refs_6_, ...), custom_call_target="tpu_custom_call" | custom-call | flops 368960000 | bytes 8192 | tf_op jit(solution)/shard_map/grads/pallas_call | solution.py:540
  23.3 2.1 %collective-permute-done.4 = bf16[512,128]{1,0:T(8,128)(2,1)S(1)} collective-permute-done((bf16[512,128]{1,0:T(8,128)(2,1)S(1)}, bf16[512,128]{1,0:T(8,128)(2,1)S(1)}, u32[]{:S(2)}, u32[]{:S(2)}) %collective-permute-start.4) | collective-permute-done | bytes 131104 | tf_op jit(solution)/shard_map/ppermute | solution.py:529
  25.4 2.3 %collective-permute-start.6 = (bf16[512,128]{1,0:T(8,128)(2,1)S(1)}, bf16[512,128]{1,0:T(8,128)(2,1)S(1)}, u32[]{:S(2)}, u32[]{:S(2)}) collective-permute-start(bf16[512,128]{1,0:T(8,128)(2,1)S(1)} %add_convert_fusion.1.refs_10_), channel_id=1, source_target_pairs={{4,0},{8,4},{12,8},{0,12},{20,16},{24,20},{28,24},{16,28},{5,1},{9... | collective-permute-start | bytes 393224 | tf_op jit(solution)/shard_map/ppermute | solution.py:529
  27.7 0.2 grads_own.2
  27.9 3.5 %collective-permute-start.7 = (bf16[512,128]{1,0:T(8,128)(2,1)S(1)}, bf16[512,128]{1,0:T(8,128)(2,1)S(1)}, u32[]{:S(2)}, u32[]{:S(2)}) collective-permute-start(bf16[512,128]{1,0:T(8,128)(2,1)S(1)} %add_convert_fusion.refs_9_), channel_id=1, source_target_pairs={{4,0},{8,4},{12,8},{0,12},{20,16},{24,20},{28,24},{16,28},{5,1},{9... | collective-permute-start | bytes 393224 | tf_op jit(solution)/shard_map/ppermute | solution.py:529
  31.4 2.1 %grads_own.3 = (f32[512,128]{1,0:T(8,128)S(1)}, bf16[256,2048]{1,0:T(8,128)(2,1)}) custom-call(bf16[256,2048]{1,0:T(8,128)(2,1)S(1)} %get-tuple-element.45.refs_0_, bf16[256,2048]{1,0:T(8,128)(2,1)S(1)} %get-tuple-element.46.refs_1_, bf16[528,128]{1,0:T(8,128)(2,1)S(1)} %number.1.own_ref.refs_2_.refs_3_.refs_4_.refs_6_, ...), custom_call_target="tpu_custom_call", output_to_operand_aliasing={{1}: (8, {})} | custom-call | flops 415080000 | bytes 8192 | tf_op jit(solution)/shard_map/grads_own/pallas_call | solution.py:540
  33.5 0.1 collective-permute-start.9
  33.6 0.3 collective-permute-done.7.refs_1_
  34.0 0.3 collective-permute-start.8
  34.2 0.7 %collective-permute-done.9.other_ref = bf16[512,128]{1,0:T(8,128)(2,1)S(1)} collective-permute-done((bf16[512,128]{1,0:T(8,128)(2,1)S(1)}, bf16[512,128]{1,0:T(8,128)(2,1)S(1)}, u32[]{:S(2)}, u32[]{:S(2)}) %collective-permute-start.9) | collective-permute-done | bytes 131104 | tf_op jit(solution)/shard_map/ppermute | solution.py:731
  35.0 0.7 %place.2 = (bf16[256,512]{1,0:T(8,128)(2,1)}, bf16[256,512]{1,0:T(8,128)(2,1)}) custom-call(bf16[512,128]{1,0:T(8,128)(2,1)S(1)} %finish.2.refs_2_.mine_ref, bf16[512,128]{1,0:T(8,128)(2,1)S(1)} %collective-permute-done.9.other_ref), custom_call_target="tpu_custom_call" | custom-call | tf_op jit(solution)/shard_map/place/pallas_call | solution.py:732
  35.7 0.7 %place.3 = (bf16[256,512]{1,0:T(8,128)(2,1)}, bf16[256,512]{1,0:T(8,128)(2,1)}) custom-call(bf16[512,128]{1,0:T(8,128)(2,1)S(1)} %finish.3.mine_ref, bf16[512,128]{1,0:T(8,128)(2,1)S(1)} %collective-permute-done.8.other_ref, bf16[256,512]{1,0:T(8,128)(2,1)} %get-tuple-element.81.refs_0_, ...), custom_call_target="tpu_custom_call", output_to_operand_aliasing={{0}: (2, {}), {1}: (3, {})} | custom-call | tf_op jit(solution)/shard_map/place/pallas_call | solution.py:732
  (9 shorter events, 0.2 us)
Async XLA Ops:
  1.6 0.7 %copy-start = (s32[256]{0:T(256)S(1)}, s32[256]{0:T(256)}, u32[]{:S(2)}) copy-start(s32[256]{0:T(256)} %param.9) | copy-start | bytes 3076
  2.4 9.5 %collective-permute-start.1 = (bf16[528,128]{1,0:T(8,128)(2,1)S(1)}, bf16[528,128]{1,0:T(8,128)(2,1)S(1)}, u32[]{:S(2)}, u32[]{:S(2)}) collective-permute-start(bf16[528,128]{1,0:T(8,128)(2,1)S(1)} %number.1.own_ref.refs_2_.refs_3_.refs_4_.refs_6_), channel_id=1, source_target_pairs={{0,4},{4,8},{8,12},{12,0},{16,20},{20,24},{24,28},{28,16},{1,5},{5... | collective-permute-start | bytes 405512 | tf_op jit(solution)/shard_map/ppermute | solution.py:529
  5.4 9.0 %collective-permute-start = (bf16[512,128]{1,0:T(8,128)(2,1)S(1)}, bf16[512,128]{1,0:T(8,128)(2,1)S(1)}, u32[]{:S(2)}, u32[]{:S(2)}) collective-permute-start(bf16[512,128]{1,0:T(8,128)(2,1)S(1)} %get-tuple-element.49.refs_3_), channel_id=1, source_target_pairs={{0,4},{4,8},{8,12},{12,0},{16,20},{20,24},{24,28},{28,16},{1,5},{5... | collective-permute-start | bytes 393224 | tf_op jit(solution)/shard_map/ppermute | solution.py:529
  11.9 6.2 %collective-permute-start.3 = (bf16[528,128]{1,0:T(8,128)(2,1)S(1)}, bf16[528,128]{1,0:T(8,128)(2,1)S(1)}, u32[]{:S(2)}, u32[]{:S(2)}) collective-permute-start(bf16[528,128]{1,0:T(8,128)(2,1)S(1)} %collective-permute-done.1.refs_6_.refs_3_.refs_4_.refs_7_), channel_id=1, source_target_pairs={{0,16},{4,8},{8,12},{12,4},{16,0},{20,24},{24,28},{28,20},{1,17},{... | collective-permute-start | bytes 405512 | tf_op jit(solution)/shard_map/ppermute | solution.py:529
  14.5 8.0 %collective-permute-start.2 = (bf16[512,128]{1,0:T(8,128)(2,1)S(1)}, bf16[512,128]{1,0:T(8,128)(2,1)S(1)}, u32[]{:S(2)}, u32[]{:S(2)}) collective-permute-start(bf16[512,128]{1,0:T(8,128)(2,1)S(1)} %collective-permute-done.refs_3_), channel_id=1, source_target_pairs={{0,16},{4,8},{8,12},{12,4},{16,0},{20,24},{24,28},{28,20},{1,17},{... | collective-permute-start | bytes 393224 | tf_op jit(solution)/shard_map/ppermute | solution.py:529
  20.4 5.0 %collective-permute-start.4 = (bf16[512,128]{1,0:T(8,128)(2,1)S(1)}, bf16[512,128]{1,0:T(8,128)(2,1)S(1)}, u32[]{:S(2)}, u32[]{:S(2)}) collective-permute-start(bf16[512,128]{1,0:T(8,128)(2,1)S(1)} %get-tuple-element.61.refs_8_), channel_id=1, source_target_pairs={{16,0},{8,4},{12,8},{4,12},{0,16},{24,20},{28,24},{20,28},{17,1},{... | collective-permute-start | bytes 393224 | tf_op jit(solution)/shard_map/ppermute | solution.py:529
  22.7 5.2 %collective-permute-start.5 = (bf16[512,128]{1,0:T(8,128)(2,1)S(1)}, bf16[512,128]{1,0:T(8,128)(2,1)S(1)}, u32[]{:S(2)}, u32[]{:S(2)}) collective-permute-start(bf16[512,128]{1,0:T(8,128)(2,1)S(1)} %get-tuple-element.65.refs_8_), channel_id=1, source_target_pairs={{16,0},{8,4},{12,8},{4,12},{0,16},{24,20},{28,24},{20,28},{17,1},{... | collective-permute-start | bytes 393224 | tf_op jit(solution)/shard_map/ppermute | solution.py:529
  25.4 8.1 %collective-permute-start.6 = (bf16[512,128]{1,0:T(8,128)(2,1)S(1)}, bf16[512,128]{1,0:T(8,128)(2,1)S(1)}, u32[]{:S(2)}, u32[]{:S(2)}) collective-permute-start(bf16[512,128]{1,0:T(8,128)(2,1)S(1)} %add_convert_fusion.1.refs_10_), channel_id=1, source_target_pairs={{4,0},{8,4},{12,8},{0,12},{20,16},{24,20},{28,24},{16,28},{5,1},{9... | collective-permute-start | bytes 393224 | tf_op jit(solution)/shard_map/ppermute | solution.py:529
  27.9 6.0 %collective-permute-start.7 = (bf16[512,128]{1,0:T(8,128)(2,1)S(1)}, bf16[512,128]{1,0:T(8,128)(2,1)S(1)}, u32[]{:S(2)}, u32[]{:S(2)}) collective-permute-start(bf16[512,128]{1,0:T(8,128)(2,1)S(1)} %add_convert_fusion.refs_9_), channel_id=1, source_target_pairs={{4,0},{8,4},{12,8},{0,12},{20,16},{24,20},{28,24},{16,28},{5,1},{9... | collective-permute-start | bytes 393224 | tf_op jit(solution)/shard_map/ppermute | solution.py:529
  33.5 1.4 %collective-permute-start.9 = (bf16[512,128]{1,0:T(8,128)(2,1)S(1)}, bf16[512,128]{1,0:T(8,128)(2,1)S(1)}, u32[]{:S(2)}, u32[]{:S(2)}) collective-permute-start(bf16[512,128]{1,0:T(8,128)(2,1)S(1)} %finish.2.refs_2_.mine_ref), channel_id=1, source_target_pairs={{0,1},{1,0},{2,3},{3,2},{4,5},{5,4},{6,7},{7,6},{8,9},{9,8},{10,11... | collective-permute-start | bytes 393224 | tf_op jit(solution)/shard_map/ppermute | solution.py:731
  34.0 1.7 %collective-permute-start.8 = (bf16[512,128]{1,0:T(8,128)(2,1)S(1)}, bf16[512,128]{1,0:T(8,128)(2,1)S(1)}, u32[]{:S(2)}, u32[]{:S(2)}) collective-permute-start(bf16[512,128]{1,0:T(8,128)(2,1)S(1)} %finish.3.mine_ref), channel_id=1, source_target_pairs={{0,1},{1,0},{2,3},{3,2},{4,5},{5,4},{6,7},{7,6},{8,9},{9,8},{10,11... | collective-permute-start | bytes 393224 | tf_op jit(solution)/shard_map/ppermute | solution.py:731

commit v4 on v3

--- a/solution.py
+++ b/solution.py
@@ -113,8 +113,8 @@
     q_seg = segment_row(own_ref, rows)
     k_seg = segment_row(kv_ref, rows)
     reached = lax.axis_index("ctx") >= step
-    active = reached & (k_seg[0, rows - 1] >= q_seg[0, 0]) & (k_seg[0, 0] <= q_seg[0, rows - 1])
-    return active, k_seg[0, rows // 2 - 1] >= q_seg[0, 0]
+    first = q_seg[0, 0]
+    return reached & (k_seg[0, rows - 1] >= first), k_seg[0, rows // 2 - 1] >= first
 
 
 def full_units(per_kv, rows):
@@ -230,7 +230,7 @@
     def add(self, unit):
         key = unit.keys.start, unit.keys.stop
         self.waiting.setdefault(key, []).append(unit)
-        if len(self.waiting[key]) == 2:
+        if len(self.waiting[key]) == 4:
             self.flush(key)
 
     def flush(self, key):
@@ -366,9 +366,9 @@
                 )
 
 
-def grads_kernel(ins, outs, scratch, *, chunk, per_kv, factor, step):
-    q_ref, g_ref, own_seg_ref, kv_ref, kv_seg_ref, in_ref, dq_in_ref, bias_ref = ins
-    kv_grad_ref, dq_ref = outs
+def grads_kernel(ins, outs, scratch, *, early_own, chunk, per_kv, factor, scale, step):
+    q_ref, g_ref, own_seg_ref, kv_ref, kv_seg_ref, in_ref, dq_in_ref, bias_ref = ins[:8]
+    kv_grad_ref, dq_ref = outs[:2]
     kt_ref = scratch[0]
     rows = q_ref.shape[0]
 
@@ -395,6 +395,12 @@
     def _():
         kv_grad_ref[...] = jnp.zeros_like(kv_grad_ref)
         dq_ref[...] = dq_in_ref[...]
+        if early_own:
+            own_kv_ref, own_in_ref, own_dq_ref, own_bias_ref = ins[8:]
+            own_run(
+                (q_ref, g_ref, own_kv_ref, own_in_ref, own_dq_ref, own_bias_ref), outs[2:], scratch,
+                chunk + 1, per_kv, factor, scale,
+            )
 
 
 def own_run(ins, outs, scratch, chunk, per_kv, factor, scale):
@@ -652,11 +658,22 @@
         return [sums[chunk]]
 
     def block_grads(chunk, step, before):
-        body = functools.partial(grads_kernel, chunk=chunk, step=step, **common)
+        early_own = step == 1 and chunk == 0 and chunks > 1
+        body = functools.partial(
+            grads_kernel, early_own=early_own, chunk=chunk, step=step, scale=scale, **common
+        )
         operands = common_operands(chunk, step) + (final_stats[chunk], dq[chunk], biases[step])
-        mine[chunk], dq[chunk] = call(
-            body, operands, (kv_grad_shape, dq_shape), [turned], "grads", 1.6, after=before
-        )
+        outs, specs, scratch, into = (kv_grad_shape, dq_shape), (WHOLE,) * 2, [turned], []
+        if early_own:
+            operands += (own[chunk + 1], final_stats[chunk + 1], dq[chunk + 1], biases[0])
+            outs, specs, scratch = outs + own_outs, specs + own_specs, own_scratch
+            into = [(query_grad.pop(), 3)]
+        mine[chunk], dq[chunk], *rest = call(
+            body, operands, outs, scratch, "grads", 1.6, specs, into=into, after=before
+        )
+        if early_own:
+            finished[chunk + 1] = rest[0]
+            query_grad.append(rest[1])
         return [mine[chunk]]
 
     def own_grads(chunk):
@@ -679,18 +696,14 @@
         )
         query_grad.append(written)
 
-    mine, arriving = [None] * chunks, [None] * chunks
+    mine = [None] * chunks
     before = [stats[-1]]
     for chunk in each:
         before = far_grads(chunk, before)
-        arriving[chunk] = moved(sums[chunk], down(reach))
-        if reach > 1:
-            before = block_grads(chunk, reach - 1, before)
     for step in range(reach - 1, 0, -1):
-        if step + 1 < reach:
-            arriving = [moved(sums[chunk], down(step + 1)) for chunk in each]
-            for chunk in each:
-                before = block_grads(chunk, step, before)
+        arriving = [moved(sums[chunk], down(step + 1)) for chunk in each]
+        for chunk in each:
+            before = block_grads(chunk, step, before)
         arriving[0], mine[-1] = lax.optimization_barrier((arriving[0], mine[-1]))
         for chunk in each:
             here = arriving[chunk]
@@ -701,7 +714,7 @@
             if step == 1:
                 returning.append(moved(sums[chunk], down(1)))
     if reach == 1:
-        returning += arriving
+        returning += [moved(sums[chunk], down(1)) for chunk in each]
     for chunk in each if reach == 1 else each[-1:]:
         own_grads(chunk)
 

time: 36.6 us -> 35.9 us (0.981)
  starting transfers between devices: 15.8 us -> 14.9 us
    ppermute x8, starting transfers between devices: 15.4 us -> 14.8 us  [moved(): return lax.ppermute(array, ('groups', 'ctx'), route)]
  transfers between devices with their start and end apart: 10 -> 10, of which waited for: 5 -> 4; matrix products, arithmetic and copies ran while one was open for 0% -> 0% of each run, Pallas kernels for 27% -> 28%
where the time goes in v4:
time: 35.9 us; the launch traced here: 35.6 us
  starting transfers between devices  14.9 us (42%)
  Pallas kernels  11.8 us (33%)
  waiting for transfers between devices  7.18 us (20%)
  between operations  0.98 us (3%)
  local copies, waits for them, and re-layouts  0.67 us (2%)
    ppermute x8, starting transfers between devices, moved(): return lax.ppermute(array, ('groups', 'ctx'), route)  14.8 us
    pallas_call x12, Pallas kernels, call(): pl.pallas_call(kernel, out_shape=outs, in_specs=[WHOLE] * count + specs,...  7.56 us
    ppermute x8, waiting for transfers between devices, moved(): return lax.ppermute(array, ('groups', 'ctx'), route)  6.6 us
    pallas_call x1, Pallas kernels, shards(): pl.pallas_call(load_kernel, out_shape=(rows_shape, rows_shape), in_specs=...  1.73 us
    pallas_call x2, Pallas kernels, shards(): pl.pallas_call(functools.partial(place_kernel, chunk=chunk, chunks=chunks...  1.46 us
    pallas_call x1, Pallas kernels, shards(): pl.pallas_call(functools.partial(pack_kernel, first_of=first_of), out_sha...  0.99 us
  transfers between devices with their start and end apart: 10, of which 4 were waited for; matrix products, arithmetic and copies ran while one was open for 0% of the time, Pallas kernels for 28%

profile of v4, /device:TPU:0, one launch (start us, length us, event | category | flops | bytes accessed | tf_op | source)
XLA Modules:
  0.0 35.6 jit_solution(11966554231913344734)
XLA Ops:
  0.6 1.0 %pack.1 = (bf16[528,128]{1,0:T(8,128)(2,1)S(1)}, bf16[512,128]{1,0:T(8,128)(2,1)S(1)}) custom-call(bf16[256,512]{1,0:T(8,128)(2,1)} %k_ref.1, bf16[256,512]{1,0:T(8,128)(2,1)} %v_ref.1), custom_call_target="tpu_custom_call" | custom-call | bytes 4194304 | tf_op jit(solution)/shard_map/pack/pallas_call | solution.py:560
  1.6 0.0 copy-start
  1.6 0.7 %copy-done = s32[256]{0:T(256)S(1)} copy-done((s32[256]{0:T(256)S(1)}, s32[256]{0:T(256)}, u32[]{:S(2)}) %copy-start) | copy-done | bytes 1048
  2.4 3.1 %collective-permute-start = (bf16[528,128]{1,0:T(8,128)(2,1)S(1)}, bf16[528,128]{1,0:T(8,128)(2,1)S(1)}, u32[]{:S(2)}, u32[]{:S(2)}) collective-permute-start(bf16[528,128]{1,0:T(8,128)(2,1)S(1)} %number.1.own_ref.refs_2_.refs_3_.refs_4_.refs_6_), channel_id=1, source_target_pairs={{0,4},{4,8},{8,12},{12,0},{16,20},{20,24},{24,28},{28,16},{1,5},{5... | collective-permute-start | bytes 405512 | tf_op jit(solution)/shard_map/ppermute | solution.py:535
  5.4 1.6 %collective-permute-start.1 = (bf16[512,128]{1,0:T(8,128)(2,1)S(1)}, bf16[512,128]{1,0:T(8,128)(2,1)S(1)}, u32[]{:S(2)}, u32[]{:S(2)}) collective-permute-start(bf16[512,128]{1,0:T(8,128)(2,1)S(1)} %get-tuple-element.51.refs_3_.refs_8_), channel_id=1, source_target_pairs={{0,4},{4,8},{8,12},{12,0},{16,20},{20,24},{24,28},{28,16},{1,5},{5... | collective-permute-start | bytes 393224 | tf_op jit(solution)/shard_map/ppermute | solution.py:535
  7.0 1.7 %load.1 = (bf16[256,2048]{1,0:T(8,128)(2,1)S(1)}, bf16[256,2048]{1,0:T(8,128)(2,1)S(1)}) custom-call(bf16[256,2048]{1,0:T(8,128)(2,1)} %q_ref.1, bf16[256,2048]{1,0:T(8,128)(2,1)} %g_ref.1, bf16[528,128]{1,0:T(8,128)(2,1)S(1)} %number.1.own_ref.refs_2_.refs_3_.refs_4_.refs_6_), custom_call_target="tpu_custom_call" | custom-call | tf_op jit(solution)/shard_map/load/pallas_call | solution.py:582
  8.7 0.9 %stats_own.2 = (f32[3,8,256]{2,1,0:T(8,128)S(1)}, f32[256,256]{1,0:T(8,128)S(1)}) custom-call(bf16[256,2048]{1,0:T(8,128)(2,1)S(1)} %get-tuple-element.47.refs_0_, bf16[256,2048]{1,0:T(8,128)(2,1)S(1)} %get-tuple-element.48.refs_1_, bf16[528,128]{1,0:T(8,128)(2,1)S(1)} %number.1.own_ref.refs_2_.refs_3_.refs_4_.refs_6_, ...), custom_call_target="tpu_custom_call" | custom-call | flops 184480000 | bytes 8192 | tf_op jit(solution)/shard_map/stats_own/pallas_call | solution.py:546
  9.7 2.2 %collective-permute-done.refs_6_.refs_3_.refs_4_.refs_7_ = bf16[528,128]{1,0:T(8,128)(2,1)S(1)} collective-permute-done((bf16[528,128]{1,0:T(8,128)(2,1)S(1)}, bf16[528,128]{1,0:T(8,128)(2,1)S(1)}, u32[]{:S(2)}, u32[]{:S(2)}) %collective-permute-start) | collective-permute-done | bytes 135200 | tf_op jit(solution)/shard_map/ppermute | solution.py:535
  11.9 1.8 %collective-permute-start.3 = (bf16[528,128]{1,0:T(8,128)(2,1)S(1)}, bf16[528,128]{1,0:T(8,128)(2,1)S(1)}, u32[]{:S(2)}, u32[]{:S(2)}) collective-permute-start(bf16[528,128]{1,0:T(8,128)(2,1)S(1)} %collective-permute-done.refs_6_.refs_3_.refs_4_.refs_7_), channel_id=1, source_target_pairs={{0,16},{4,8},{8,12},{12,4},{16,0},{20,24},{24,28},{28,20},{1,17},{... | collective-permute-start | bytes 405512 | tf_op jit(solution)/shard_map/ppermute | solution.py:535
  13.6 0.8 %stats_own.3.refs_5_ = f32[3,8,256]{2,1,0:T(8,128)S(1)} custom-call(bf16[256,2048]{1,0:T(8,128)(2,1)S(1)} %get-tuple-element.47.refs_0_, bf16[256,2048]{1,0:T(8,128)(2,1)S(1)} %get-tuple-element.48.refs_1_, bf16[528,128]{1,0:T(8,128)(2,1)S(1)} %number.1.own_ref.refs_2_.refs_3_.refs_4_.refs_6_, bf16[512,128]{1,0:T(8,128)(2,1)S(1)} %get-tuple-element.51.refs_3_.refs_8_, ...), custom_call_target="tpu_custom_call" | custom-call | flops 184480000 | bytes 8192 | tf_op jit(solution)/shard_map/stats_own/pallas_call | solution.py:546
  14.5 0.0 collective-permute-done.1.refs_3_
  14.5 1.2 %collective-permute-start.2 = (bf16[512,128]{1,0:T(8,128)(2,1)S(1)}, bf16[512,128]{1,0:T(8,128)(2,1)S(1)}, u32[]{:S(2)}, u32[]{:S(2)}) collective-permute-start(bf16[512,128]{1,0:T(8,128)(2,1)S(1)} %collective-permute-done.1.refs_3_), channel_id=1, source_target_pairs={{0,16},{4,8},{8,12},{12,4},{16,0},{20,24},{24,28},{28,20},{1,17},{... | collective-permute-start | bytes 393224 | tf_op jit(solution)/shard_map/ppermute | solution.py:535
  15.6 0.1 stats.2
  15.7 0.1 stats.3.refs_9_.refs_5_
  15.9 2.2 %collective-permute-done.3.refs_3_.refs_4_ = bf16[528,128]{1,0:T(8,128)(2,1)S(1)} collective-permute-done((bf16[528,128]{1,0:T(8,128)(2,1)S(1)}, bf16[528,128]{1,0:T(8,128)(2,1)S(1)}, u32[]{:S(2)}, u32[]{:S(2)}) %collective-permute-start.3) | collective-permute-done | bytes 135200 | tf_op jit(solution)/shard_map/ppermute | solution.py:535
  18.0 2.3 %grads_far.2 = (f32[2,8,256]{2,1,0:T(8,128)S(1)}, bf16[512,128]{1,0:T(8,128)(2,1)S(1)}, f32[8,128,256]{2,1,0:T(8,128)S(1)}, f32[512,128]{1,0:T(8,128)S(1)}, bf16...) custom-call(bf16[256,2048]{1,0:T(8,128)(2,1)S(1)} %get-tuple-element.47.refs_0_, ...), custom_call_target="tpu_custom_call" | custom-call | flops 299780000 | bytes 8192 | tf_op jit(solution)/shard_map/grads_far/pallas_call | solution.py:546
  20.4 1.9 %collective-permute-start.4 = (bf16[512,128]{1,0:T(8,128)(2,1)S(1)}, bf16[512,128]{1,0:T(8,128)(2,1)S(1)}, u32[]{:S(2)}, u32[]{:S(2)}) collective-permute-start(bf16[512,128]{1,0:T(8,128)(2,1)S(1)} %get-tuple-element.61.refs_7_), channel_id=1, source_target_pairs={{16,0},{8,4},{12,8},{4,12},{0,16},{24,20},{28,24},{20,28},{17,1},{... | collective-permute-start | bytes 393224 | tf_op jit(solution)/shard_map/ppermute | solution.py:535
  22.3 0.2 grads_far.3
  22.5 0.3 collective-permute-start.5
  22.7 2.5 %grads.2 = (f32[512,128]{1,0:T(8,128)S(1)}, f32[8,128,256]{2,1,0:T(8,128)S(1)}, f32[512,128]{1,0:T(8,128)S(1)}, bf16[256,2048]{1,0:T(8,128)(2,1)}) custom-call(bf16[256,2048]{1,0:T(8,128)(2,1)S(1)} %get-tuple-element.47.refs_0_, bf16[256,2048]{1,0:T(8,128)(2,1)S(1)} %get-tuple-element.48.refs_1_, ...), custom_call_target="tpu_custom_call", output_to_operand_aliasing={{3}: (12, {})} | custom-call | flops 368960000 | bytes 8192 | tf_op jit(solution)/shard_map/grads/pallas_call | solution.py:546
  25.2 0.2 grads.3
  25.4 0.0 collective-permute-done.4
  25.4 2.3 %collective-permute-start.6 = (bf16[512,128]{1,0:T(8,128)(2,1)S(1)}, bf16[512,128]{1,0:T(8,128)(2,1)S(1)}, u32[]{:S(2)}, u32[]{:S(2)}) collective-permute-start(bf16[512,128]{1,0:T(8,128)(2,1)S(1)} %add_convert_fusion.1.refs_10_), channel_id=1, source_target_pairs={{4,0},{8,4},{12,8},{0,12},{20,16},{24,20},{28,24},{16,28},{5,1},{9... | collective-permute-start | bytes 393224 | tf_op jit(solution)/shard_map/ppermute | solution.py:535
  27.8 0.2 grads_own.2
  28.0 2.7 %collective-permute-start.7 = (bf16[512,128]{1,0:T(8,128)(2,1)S(1)}, bf16[512,128]{1,0:T(8,128)(2,1)S(1)}, u32[]{:S(2)}, u32[]{:S(2)}) collective-permute-start(bf16[512,128]{1,0:T(8,128)(2,1)S(1)} %add_convert_fusion.refs_10_), channel_id=1, source_target_pairs={{4,0},{8,4},{12,8},{0,12},{20,16},{24,20},{28,24},{16,28},{5,1},{9... | collective-permute-start | bytes 393224 | tf_op jit(solution)/shard_map/ppermute | solution.py:535
  30.7 0.2 grads_own.3
  30.9 0.1 collective-permute-start.9
  31.0 2.2 %collective-permute-done.7.refs_1_ = bf16[512,128]{1,0:T(8,128)(2,1)S(1)} collective-permute-done((bf16[512,128]{1,0:T(8,128)(2,1)S(1)}, bf16[512,128]{1,0:T(8,128)(2,1)S(1)}, u32[]{:S(2)}, u32[]{:S(2)}) %collective-permute-start.7) | collective-permute-done | bytes 131104 | tf_op jit(solution)/shard_map/ppermute | solution.py:535
  33.3 0.1 collective-permute-start.8
  33.4 0.7 %place.2 = (bf16[256,512]{1,0:T(8,128)(2,1)}, bf16[256,512]{1,0:T(8,128)(2,1)}) custom-call(bf16[512,128]{1,0:T(8,128)(2,1)S(1)} %finish.2.refs_2_.mine_ref, bf16[512,128]{1,0:T(8,128)(2,1)S(1)} %collective-permute-done.9.other_ref), custom_call_target="tpu_custom_call" | custom-call | tf_op jit(solution)/shard_map/place/pallas_call | solution.py:745
  34.1 0.6 %collective-permute-done.8.other_ref = bf16[512,128]{1,0:T(8,128)(2,1)S(1)} collective-permute-done((bf16[512,128]{1,0:T(8,128)(2,1)S(1)}, bf16[512,128]{1,0:T(8,128)(2,1)S(1)}, u32[]{:S(2)}, u32[]{:S(2)}) %collective-permute-start.8) | collective-permute-done | bytes 131104 | tf_op jit(solution)/shard_map/ppermute | solution.py:744
  34.7 0.7 %place.3 = (bf16[256,512]{1,0:T(8,128)(2,1)}, bf16[256,512]{1,0:T(8,128)(2,1)}) custom-call(bf16[512,128]{1,0:T(8,128)(2,1)S(1)} %finish.3.mine_ref, bf16[512,128]{1,0:T(8,128)(2,1)S(1)} %collective-permute-done.8.other_ref, bf16[256,512]{1,0:T(8,128)(2,1)} %get-tuple-element.85.refs_0_, ...), custom_call_target="tpu_custom_call", output_to_operand_aliasing={{0}: (2, {}), {1}: (3, {})} | custom-call | tf_op jit(solution)/shard_map/place/pallas_call | solution.py:745
  (9 shorter events, 0.2 us)
Async XLA Ops:
  1.6 0.7 %copy-start = (s32[256]{0:T(256)S(1)}, s32[256]{0:T(256)}, u32[]{:S(2)}) copy-start(s32[256]{0:T(256)} %param.9) | copy-start | bytes 3076
  2.4 9.5 %collective-permute-start = (bf16[528,128]{1,0:T(8,128)(2,1)S(1)}, bf16[528,128]{1,0:T(8,128)(2,1)S(1)}, u32[]{:S(2)}, u32[]{:S(2)}) collective-permute-start(bf16[528,128]{1,0:T(8,128)(2,1)S(1)} %number.1.own_ref.refs_2_.refs_3_.refs_4_.refs_6_), channel_id=1, source_target_pairs={{0,4},{4,8},{8,12},{12,0},{16,20},{20,24},{24,28},{28,16},{1,5},{5... | collective-permute-start | bytes 405512 | tf_op jit(solution)/shard_map/ppermute | solution.py:535
  5.4 9.0 %collective-permute-start.1 = (bf16[512,128]{1,0:T(8,128)(2,1)S(1)}, bf16[512,128]{1,0:T(8,128)(2,1)S(1)}, u32[]{:S(2)}, u32[]{:S(2)}) collective-permute-start(bf16[512,128]{1,0:T(8,128)(2,1)S(1)} %get-tuple-element.51.refs_3_.refs_8_), channel_id=1, source_target_pairs={{0,4},{4,8},{8,12},{12,0},{16,20},{20,24},{24,28},{28,16},{1,5},{5... | collective-permute-start | bytes 393224 | tf_op jit(solution)/shard_map/ppermute | solution.py:535
  11.9 6.2 %collective-permute-start.3 = (bf16[528,128]{1,0:T(8,128)(2,1)S(1)}, bf16[528,128]{1,0:T(8,128)(2,1)S(1)}, u32[]{:S(2)}, u32[]{:S(2)}) collective-permute-start(bf16[528,128]{1,0:T(8,128)(2,1)S(1)} %collective-permute-done.refs_6_.refs_3_.refs_4_.refs_7_), channel_id=1, source_target_pairs={{0,16},{4,8},{8,12},{12,4},{16,0},{20,24},{24,28},{28,20},{1,17},{... | collective-permute-start | bytes 405512 | tf_op jit(solution)/shard_map/ppermute | solution.py:535
  14.5 7.8 %collective-permute-start.2 = (bf16[512,128]{1,0:T(8,128)(2,1)S(1)}, bf16[512,128]{1,0:T(8,128)(2,1)S(1)}, u32[]{:S(2)}, u32[]{:S(2)}) collective-permute-start(bf16[512,128]{1,0:T(8,128)(2,1)S(1)} %collective-permute-done.1.refs_3_), channel_id=1, source_target_pairs={{0,16},{4,8},{8,12},{12,4},{16,0},{20,24},{24,28},{28,20},{1,17},{... | collective-permute-start | bytes 393224 | tf_op jit(solution)/shard_map/ppermute | solution.py:535
  20.4 5.0 %collective-permute-start.4 = (bf16[512,128]{1,0:T(8,128)(2,1)S(1)}, bf16[512,128]{1,0:T(8,128)(2,1)S(1)}, u32[]{:S(2)}, u32[]{:S(2)}) collective-permute-start(bf16[512,128]{1,0:T(8,128)(2,1)S(1)} %get-tuple-element.61.refs_7_), channel_id=1, source_target_pairs={{16,0},{8,4},{12,8},{4,12},{0,16},{24,20},{28,24},{20,28},{17,1},{... | collective-permute-start | bytes 393224 | tf_op jit(solution)/shard_map/ppermute | solution.py:535
  22.5 5.5 %collective-permute-start.5 = (bf16[512,128]{1,0:T(8,128)(2,1)S(1)}, bf16[512,128]{1,0:T(8,128)(2,1)S(1)}, u32[]{:S(2)}, u32[]{:S(2)}) collective-permute-start(bf16[512,128]{1,0:T(8,128)(2,1)S(1)} %get-tuple-element.67.refs_13_), channel_id=1, source_target_pairs={{16,0},{8,4},{12,8},{4,12},{0,16},{24,20},{28,24},{20,28},{17,1},{... | collective-permute-start | bytes 393224 | tf_op jit(solution)/shard_map/ppermute | solution.py:535
  25.4 5.5 %collective-permute-start.6 = (bf16[512,128]{1,0:T(8,128)(2,1)S(1)}, bf16[512,128]{1,0:T(8,128)(2,1)S(1)}, u32[]{:S(2)}, u32[]{:S(2)}) collective-permute-start(bf16[512,128]{1,0:T(8,128)(2,1)S(1)} %add_convert_fusion.1.refs_10_), channel_id=1, source_target_pairs={{4,0},{8,4},{12,8},{0,12},{20,16},{24,20},{28,24},{16,28},{5,1},{9... | collective-permute-start | bytes 393224 | tf_op jit(solution)/shard_map/ppermute | solution.py:535
  28.0 5.2 %collective-permute-start.7 = (bf16[512,128]{1,0:T(8,128)(2,1)S(1)}, bf16[512,128]{1,0:T(8,128)(2,1)S(1)}, u32[]{:S(2)}, u32[]{:S(2)}) collective-permute-start(bf16[512,128]{1,0:T(8,128)(2,1)S(1)} %add_convert_fusion.refs_10_), channel_id=1, source_target_pairs={{4,0},{8,4},{12,8},{0,12},{20,16},{24,20},{28,24},{16,28},{5,1},{9... | collective-permute-start | bytes 393224 | tf_op jit(solution)/shard_map/ppermute | solution.py:535
  30.9 2.4 %collective-permute-start.9 = (bf16[512,128]{1,0:T(8,128)(2,1)S(1)}, bf16[512,128]{1,0:T(8,128)(2,1)S(1)}, u32[]{:S(2)}, u32[]{:S(2)}) collective-permute-start(bf16[512,128]{1,0:T(8,128)(2,1)S(1)} %finish.2.refs_2_.mine_ref), channel_id=1, source_target_pairs={{0,1},{1,0},{2,3},{3,2},{4,5},{5,4},{6,7},{7,6},{8,9},{9,8},{10,11... | collective-permute-start | bytes 393224 | tf_op jit(solution)/shard_map/ppermute | solution.py:744
  33.3 1.4 %collective-permute-start.8 = (bf16[512,128]{1,0:T(8,128)(2,1)S(1)}, bf16[512,128]{1,0:T(8,128)(2,1)S(1)}, u32[]{:S(2)}, u32[]{:S(2)}) collective-permute-start(bf16[512,128]{1,0:T(8,128)(2,1)S(1)} %finish.3.mine_ref), channel_id=1, source_target_pairs={{0,1},{1,0},{2,3},{3,2},{4,5},{5,4},{6,7},{7,6},{8,9},{9,8},{10,11... | collective-permute-start | bytes 393224 | tf_op jit(solution)/shard_map/ppermute | solution.py:744

commit v5 on v3

--- a/solution.py
+++ b/solution.py
@@ -113,8 +113,8 @@
     q_seg = segment_row(own_ref, rows)
     k_seg = segment_row(kv_ref, rows)
     reached = lax.axis_index("ctx") >= step
-    active = reached & (k_seg[0, rows - 1] >= q_seg[0, 0]) & (k_seg[0, 0] <= q_seg[0, rows - 1])
-    return active, k_seg[0, rows // 2 - 1] >= q_seg[0, 0]
+    first = q_seg[0, 0]
+    return reached & (k_seg[0, rows - 1] >= first), k_seg[0, rows // 2 - 1] >= first
 
 
 def full_units(per_kv, rows):
@@ -230,7 +230,7 @@
     def add(self, unit):
         key = unit.keys.start, unit.keys.stop
         self.waiting.setdefault(key, []).append(unit)
-        if len(self.waiting[key]) == 2:
+        if len(self.waiting[key]) == 4:
             self.flush(key)
 
     def flush(self, key):
@@ -254,11 +254,11 @@
     return stats[0] + jnp.log2(stats[1]), stats[2] / stats[1]
 
 
-def stats_kernel(ins, outs, _, *, fill, chunk, per_kv, factor, step):
+def stats_kernel(ins, outs, scratch, *, early_own, fill, chunk, per_kv, factor, scale, step):
     q_ref, g_ref, own_seg_ref, kv_ref, kv_seg_ref = ins[:5]
     in_ref = ins[5] if step else None
     out_ref = outs[0]
-    bias_ref = outs[1] if fill else ins[-1]
+    bias_ref = outs[-1] if fill else ins[-1]
     rows = q_ref.shape[0]
 
     def run():
@@ -276,8 +276,21 @@
         units = full_units(per_kv, rows) if step else own_units(per_kv, rows)
         in_turn(units, lambda unit: Unit(unit, chunk * per_kv, q_ref, g_ref, kv_ref, bias_ref), handle, AHEAD)
 
+    def own_early():
+        near_seg_ref, own_kv_ref, stats_ref, own_bias_ref = ins[-5:-1]
+        final_ref = scratch[0]
+        for part, value in enumerate(finals((stats_ref[0], stats_ref[1], stats_ref[2]))):
+            final_ref[part] = value
+        own_run(
+            (q_ref, g_ref, own_kv_ref, final_ref, None, own_bias_ref), outs[1:3], scratch[1:],
+            early_own, per_kv, factor, scale,
+        )
+
     if step == 0:
         run()
+        if early_own is not None:
+            near, _ = activity(own_seg_ref, ins[-5], 1, rows)
+            pl.when(jnp.logical_not(near))(own_early)
         return
     active, _ = activity(own_seg_ref, kv_seg_ref, step, rows)
     pl.when(active)(run)
@@ -285,9 +298,11 @@
     @pl.when(jnp.logical_not(active))
     def _():
         out_ref[...] = in_ref[...]
-
-
-def far_kernel(ins, outs, scratch, *, early_own, fill, chunk, per_kv, factor, scale, step):
+        if early_own is not None:
+            own_early()
+
+
+def far_kernel(ins, outs, scratch, *, fill, chunk, per_kv, factor, step):
     q_ref, g_ref, own_seg_ref, kv_ref, kv_seg_ref, in_ref = ins[:6]
     out_ref, kv_grad_ref, dq_ref = outs[:3]
     bias_ref = outs[-1] if fill else ins[-1]
@@ -354,16 +369,6 @@
     def _():
         dq_ref[...] = jnp.zeros_like(dq_ref)
         kv_grad_ref[...] = jnp.zeros_like(kv_grad_ref)
-        if early_own:
-            own_kv_ref, near_seg_ref, own_bias_ref = ins[6:9]
-            near, _ = activity(own_seg_ref, near_seg_ref, 1, rows)
-
-            @pl.when(jnp.logical_not(near))
-            def _():
-                own_run(
-                    (q_ref, g_ref, own_kv_ref, out_ref, dq_ref, own_bias_ref), outs[3:5],
-                    (kt_ref, *scratch[2:]), chunk, per_kv, factor, scale,
-                )
 
 
 def grads_kernel(ins, outs, scratch, *, chunk, per_kv, factor, step):
@@ -421,7 +426,7 @@
         dq = times(kt_ref[:, unit.keys], unit.dscores)
         head = unit.parts[0][0]
         if unit.keys.start == 0:
-            dq_now[head] = dq_in_ref[head] + dq
+            dq_now[head] = dq if dq_in_ref is None else dq_in_ref[head] + dq
             return
         for (other, _), piece in zip(unit.parts, unit.split(dq)):
             total = dq_now.pop(other)
@@ -599,56 +604,63 @@
     def common_operands(chunk, step):
         return queries, out_grad, own[0], blocks[chunk][step], blocks[0][step]
 
-    def with_bias(kernel, chunk, step, operands, outs, scratch, name, micros, after=(), specs=None, **options):
+    def with_bias(
+        kernel, chunk, step, operands, outs, scratch, name, micros, after=(), specs=None, into=(), **options
+    ):
         fill = biases[step] is None
         body = functools.partial(kernel, fill=fill, chunk=chunk, step=step, **options, **common)
         operands = common_operands(chunk, step) + operands
         specs = specs or (WHOLE,) * len(outs)
         if not fill:
-            return call(body, operands + (biases[step],), outs, scratch, name, micros, specs, after=after)
+            return call(body, operands + (biases[step],), outs, scratch, name, micros, specs, into, after)
         *results, biases[step] = call(
-            body, operands, outs + (bias_shape,), scratch, name, micros, specs + (WHOLE,), after=after
+            body, operands, outs + (bias_shape,), scratch, name, micros, specs + (WHOLE,), into, after
         )
         return results
 
     stats, final_stats = [None] * chunks, [None] * chunks
     sums, dq = [None] * chunks, [None] * chunks
+    finished, returning, query_grad = [None] * chunks, [], []
+    own_outs = (kv_grad_shape, jax.ShapeDtypeStruct(queries.shape, jnp.bfloat16))
+    own_specs = (WHOLE, ANYWHERE)
+    own_scratch = [
+        turned,
+        pltpu.VMEM((rows, per_kv * HEAD_SIZE), jnp.bfloat16),
+        pltpu.SemaphoreType.DMA((per_kv // 2,)),
+    ]
+
+    def block_stats(chunk, step, early_own=None, after=()):
+        operands = () if step == 0 else (stats[chunk],)
+        outs, specs, scratch, into = (stats_shape,), (WHOLE,), [], []
+        if early_own is not None:
+            operands += (blocks[0][1], own[early_own], stats[early_own], biases[0])
+            outs, specs = outs + own_outs, specs + own_specs
+            scratch = [pltpu.VMEM(finals_shape.shape, jnp.float32)] + own_scratch
+            into = [(query_grad.pop(), 2)] if query_grad else []
+        stats[chunk], *rest = with_bias(
+            stats_kernel, chunk, step, operands, outs, scratch, "stats" if step else "stats_own", 1.0,
+            after, specs, into, early_own=early_own, scale=scale,
+        )
+        if early_own is not None:
+            finished[early_own] = rest[0]
+            query_grad.append(rest[1])
+
+    early = chunks > 1 and reach > 1
     for chunk in each:
         after = [blocks[chunk - 1][1]] if chunk else []
-        (stats[chunk],) = with_bias(
-            stats_kernel, chunk, 0, (), (stats_shape,), [], "stats_own", 0.8, after
-        )
+        block_stats(chunk, 0, 0 if early and chunk == 1 else None, after)
     for step in range(1, reach):
         for chunk in each:
             here, stats[chunk] = lax.optimization_barrier((blocks[chunk][step], stats[chunk]))
             blocks[chunk].append(moved(here, up(step + 1)))
         for chunk in each:
-            (stats[chunk],) = with_bias(
-                stats_kernel, chunk, step, (stats[chunk],), (stats_shape,), [], "stats", 1.1
-            )
-    finished, returning, query_grad = [None] * chunks, [], []
-    own_outs = (kv_grad_shape, jax.ShapeDtypeStruct(queries.shape, jnp.bfloat16))
-    own_specs = (WHOLE, ANYWHERE)
-    written_scratch = [
-        pltpu.VMEM((rows, per_kv * HEAD_SIZE), jnp.bfloat16),
-        pltpu.SemaphoreType.DMA((per_kv // 2,)),
-    ]
-    own_scratch = [turned] + written_scratch
+            block_stats(chunk, step, 1 if early and step == 1 and chunk == 1 else None)
 
     def far_grads(chunk, before):
-        operands = (stats[chunk],)
-        outs, specs, scratch = (finals_shape, sent_shape, dq_shape), (WHOLE,) * 3, [turned, total_sum]
-        early_own = chunk == 0
-        if early_own:
-            operands += (own[chunk], blocks[0][1], biases[0])
-            outs, specs, scratch = outs + own_outs, specs + own_specs, scratch + written_scratch
-        final_stats[chunk], sums[chunk], dq[chunk], *rest = with_bias(
-            far_kernel, chunk, reach, operands, outs, scratch, "grads_far", 1.3, before, specs,
-            early_own=early_own, scale=scale,
-        )
-        if early_own:
-            finished[chunk] = rest[0]
-            query_grad.append(rest[1])
+        final_stats[chunk], sums[chunk], dq[chunk] = with_bias(
+            far_kernel, chunk, reach, (stats[chunk],), (finals_shape, sent_shape, dq_shape),
+            [turned, total_sum], "grads_far", 1.3, before,
+        )
         return [sums[chunk]]
 
     def block_grads(chunk, step, before):
@@ -679,18 +691,14 @@
         )
         query_grad.append(written)
 
-    mine, arriving = [None] * chunks, [None] * chunks
+    mine = [None] * chunks
     before = [stats[-1]]
     for chunk in each:
         before = far_grads(chunk, before)
-        arriving[chunk] = moved(sums[chunk], down(reach))
-        if reach > 1:
-            before = block_grads(chunk, reach - 1, before)
     for step in range(reach - 1, 0, -1):
-        if step + 1 < reach:
-            arriving = [moved(sums[chunk], down(step + 1)) for chunk in each]
-            for chunk in each:
-                before = block_grads(chunk, step, before)
+        arriving = [moved(sums[chunk], down(step + 1)) for chunk in each]
+        for chunk in each:
+            before = block_grads(chunk, step, before)
         arriving[0], mine[-1] = lax.optimization_barrier((arriving[0], mine[-1]))
         for chunk in each:
             here = arriving[chunk]
@@ -701,7 +709,7 @@
             if step == 1:
                 returning.append(moved(sums[chunk], down(1)))
     if reach == 1:
-        returning += arriving
+        returning += [moved(sums[chunk], down(1)) for chunk in each]
     for chunk in each if reach == 1 else each[-1:]:
         own_grads(chunk)
 

time: 36.6 us -> 35.9 us (0.981)
  starting transfers between devices: 15.8 us -> 13.1 us
  waiting for transfers between devices: 7.45 us -> 9.07 us
    ppermute x8, starting transfers between devices: 15.4 us -> 13 us  [moved(): return lax.ppermute(array, ('groups', 'ctx'), route)]
    ppermute x8, waiting for transfers between devices: 6.72 us -> 8.49 us  [moved(): return lax.ppermute(array, ('groups', 'ctx'), route)]
  transfers between devices with their start and end apart: 10 -> 10, of which waited for: 5 -> 6; matrix products, arithmetic and copies ran while one was open for 0% -> 0% of each run, Pallas kernels for 27% -> 28%
where the time goes in v5:
time: 35.9 us; the launch traced here: 35.7 us
  starting transfers between devices  13.1 us (36%)
  Pallas kernels  11.8 us (33%)
  waiting for transfers between devices  9.07 us (25%)
  between operations  0.98 us (3%)
  local copies, waits for them, and re-layouts  0.67 us (2%)
    ppermute x8, starting transfers between devices, moved(): return lax.ppermute(array, ('groups', 'ctx'), route)  13 us
    ppermute x8, waiting for transfers between devices, moved(): return lax.ppermute(array, ('groups', 'ctx'), route)  8.49 us
    pallas_call x12, Pallas kernels, call(): pl.pallas_call(kernel, out_shape=outs, in_specs=[WHOLE] * count + specs,...  7.55 us
    pallas_call x1, Pallas kernels, shards(): pl.pallas_call(load_kernel, out_shape=(rows_shape, rows_shape), in_specs=...  1.73 us
    pallas_call x2, Pallas kernels, shards(): pl.pallas_call(functools.partial(place_kernel, chunk=chunk, chunks=chunks...  1.46 us
    pallas_call x1, Pallas kernels, shards(): pl.pallas_call(functools.partial(pack_kernel, first_of=first_of), out_sha...  0.99 us
  transfers between devices with their start and end apart: 10, of which 6 were waited for; matrix products, arithmetic and copies ran while one was open for 0% of the time, Pallas kernels for 28%

profile of v5, /device:TPU:0, one launch (start us, length us, event | category | flops | bytes accessed | tf_op | source)
XLA Modules:
  0.0 35.7 jit_solution(17808067611975077343)
XLA Ops:
  0.6 1.0 %pack.1 = (bf16[528,128]{1,0:T(8,128)(2,1)S(1)}, bf16[512,128]{1,0:T(8,128)(2,1)S(1)}) custom-call(bf16[256,512]{1,0:T(8,128)(2,1)} %k_ref.1, bf16[256,512]{1,0:T(8,128)(2,1)} %v_ref.1), custom_call_target="tpu_custom_call" | custom-call | bytes 4194304 | tf_op jit(solution)/shard_map/pack/pallas_call | solution.py:559
  1.6 0.0 copy-start
  1.6 0.7 %copy-done = s32[256]{0:T(256)S(1)} copy-done((s32[256]{0:T(256)S(1)}, s32[256]{0:T(256)}, u32[]{:S(2)}) %copy-start) | copy-done | bytes 1048
  2.4 3.1 %collective-permute-start = (bf16[528,128]{1,0:T(8,128)(2,1)S(1)}, bf16[528,128]{1,0:T(8,128)(2,1)S(1)}, u32[]{:S(2)}, u32[]{:S(2)}) collective-permute-start(bf16[528,128]{1,0:T(8,128)(2,1)S(1)} %number.1.own_ref.refs_2_.refs_3_.refs_4_.refs_6_), channel_id=1, source_target_pairs={{0,4},{4,8},{8,12},{12,0},{16,20},{20,24},{24,28},{28,16},{1,5},{5... | collective-permute-start | bytes 405512 | tf_op jit(solution)/shard_map/ppermute | solution.py:534
  5.4 1.6 %collective-permute-start.1 = (bf16[512,128]{1,0:T(8,128)(2,1)S(1)}, bf16[512,128]{1,0:T(8,128)(2,1)S(1)}, u32[]{:S(2)}, u32[]{:S(2)}) collective-permute-start(bf16[512,128]{1,0:T(8,128)(2,1)S(1)} %get-tuple-element.53.refs_3_.refs_7_), channel_id=1, source_target_pairs={{0,4},{4,8},{8,12},{12,0},{16,20},{20,24},{24,28},{28,16},{1,5},{5... | collective-permute-start | bytes 393224 | tf_op jit(solution)/shard_map/ppermute | solution.py:534
  7.0 1.7 %load.1 = (bf16[256,2048]{1,0:T(8,128)(2,1)S(1)}, bf16[256,2048]{1,0:T(8,128)(2,1)S(1)}) custom-call(bf16[256,2048]{1,0:T(8,128)(2,1)} %q_ref.1, bf16[256,2048]{1,0:T(8,128)(2,1)} %g_ref.1, bf16[528,128]{1,0:T(8,128)(2,1)S(1)} %number.1.own_ref.refs_2_.refs_3_.refs_4_.refs_6_), custom_call_target="tpu_custom_call" | custom-call | tf_op jit(solution)/shard_map/load/pallas_call | solution.py:581
  8.7 0.9 %stats_own.2 = (f32[3,8,256]{2,1,0:T(8,128)S(1)}, f32[256,256]{1,0:T(8,128)S(1)}) custom-call(bf16[256,2048]{1,0:T(8,128)(2,1)S(1)} %get-tuple-element.49.refs_0_, bf16[256,2048]{1,0:T(8,128)(2,1)S(1)} %get-tuple-element.50.refs_1_, bf16[528,128]{1,0:T(8,128)(2,1)S(1)} %number.1.own_ref.refs_2_.refs_3_.refs_4_.refs_6_, ...), custom_call_target="tpu_custom_call" | custom-call | flops 230600000 | bytes 8192 | tf_op jit(solution)/shard_map/stats_own/pallas_call | solution.py:545
  9.7 2.2 %collective-permute-done.refs_5_.refs_10_.refs_3_.refs_4_.refs_6_ = bf16[528,128]{1,0:T(8,128)(2,1)S(1)} collective-permute-done((bf16[528,128]{1,0:T(8,128)(2,1)S(1)}, bf16[528,128]{1,0:T(8,128)(2,1)S(1)}, u32[]{:S(2)}, u32[]{:S(2)}) %collective-permute-start) | collective-permute-done | bytes 135200 | tf_op jit(solution)/shard_map/ppermute | solution.py:534
  11.9 1.8 %collective-permute-start.3 = (bf16[528,128]{1,0:T(8,128)(2,1)S(1)}, bf16[528,128]{1,0:T(8,128)(2,1)S(1)}, u32[]{:S(2)}, u32[]{:S(2)}) collective-permute-start(bf16[528,128]{1,0:T(8,128)(2,1)S(1)} %collective-permute-done.refs_5_.refs_10_.refs_3_.refs_4_.refs_6_), channel_id=1, source_target_pairs={{0,16},{4,8},{8,12},{12,4},{16,0},{20,24},{24,28},{28,20},{1,17},{... | collective-permute-start | bytes 405512 | tf_op jit(solution)/shard_map/ppermute | solution.py:534
  13.6 2.9 %stats_own.3 = (f32[3,8,256]{2,1,0:T(8,128)S(1)}, f32[512,128]{1,0:T(8,128)S(1)}, bf16[256,2048]{1,0:T(8,128)(2,1)}) custom-call(bf16[256,2048]{1,0:T(8,128)(2,1)S(1)} %get-tuple-element.49.refs_0_, bf16[256,2048]{1,0:T(8,128)(2,1)S(1)} %get-tuple-element.50.refs_1_, bf16[528,128]{1,0:T(8,128)(2,1)S(1)} %number.1.own_ref.refs_2_.refs_3_.refs_4_.refs_6_, ...), custom_call_target="tpu_custom_call" | custom-call | flops 230600000 | bytes 8192 | tf_op jit(solution)/shard_map/stats_own/pallas_call | solution.py:545
  16.6 0.3 collective-permute-start.2
  16.9 0.1 stats.2
  17.0 2.2 %stats.3 = (f32[3,8,256]{2,1,0:T(8,128)S(1)}, f32[512,128]{1,0:T(8,128)S(1)}, bf16[256,2048]{1,0:T(8,128)(2,1)}) custom-call(bf16[256,2048]{1,0:T(8,128)(2,1)S(1)} %get-tuple-element.49.refs_0_, bf16[256,2048]{1,0:T(8,128)(2,1)S(1)} %get-tuple-element.50.refs_1_, ...), custom_call_target="tpu_custom_call", output_to_operand_aliasing={{2}: (11, {})} | custom-call | flops 230600000 | bytes 8192 | tf_op jit(solution)/shard_map/stats/pallas_call | solution.py:545
  19.2 0.2 grads_far.2
  19.4 1.8 %collective-permute-start.4 = (bf16[512,128]{1,0:T(8,128)(2,1)S(1)}, bf16[512,128]{1,0:T(8,128)(2,1)S(1)}, u32[]{:S(2)}, u32[]{:S(2)}) collective-permute-start(bf16[512,128]{1,0:T(8,128)(2,1)S(1)} %get-tuple-element.66.refs_7_), channel_id=1, source_target_pairs={{16,0},{8,4},{12,8},{4,12},{0,16},{24,20},{28,24},{20,28},{17,1},{... | collective-permute-start | bytes 393224 | tf_op jit(solution)/shard_map/ppermute | solution.py:534
  21.3 1.7 %collective-permute-done.2.refs_3_ = bf16[512,128]{1,0:T(8,128)(2,1)S(1)} collective-permute-done((bf16[512,128]{1,0:T(8,128)(2,1)S(1)}, bf16[512,128]{1,0:T(8,128)(2,1)S(1)}, u32[]{:S(2)}, u32[]{:S(2)}) %collective-permute-start.2) | collective-permute-done | bytes 131104 | tf_op jit(solution)/shard_map/ppermute | solution.py:534
  23.0 0.2 grads_far.3
  23.2 0.1 collective-permute-start.5
  23.3 0.4 %grads.2 = (f32[512,128]{1,0:T(8,128)S(1)}, f32[8,128,256]{2,1,0:T(8,128)S(1)}) custom-call(bf16[256,2048]{1,0:T(8,128)(2,1)S(1)} %get-tuple-element.49.refs_0_, bf16[256,2048]{1,0:T(8,128)(2,1)S(1)} %get-tuple-element.50.refs_1_, bf16[528,128]{1,0:T(8,128)(2,1)S(1)} %number.1.own_ref.refs_2_.refs_3_.refs_4_.refs_6_, ...), custom_call_target="tpu_custom_call" | custom-call | flops 368960000 | bytes 8192 | tf_op jit(solution)/shard_map/grads/pallas_call | solution.py:545
  23.6 0.2 grads.3
  23.9 1.7 %collective-permute-done.4 = bf16[512,128]{1,0:T(8,128)(2,1)S(1)} collective-permute-done((bf16[512,128]{1,0:T(8,128)(2,1)S(1)}, bf16[512,128]{1,0:T(8,128)(2,1)S(1)}, u32[]{:S(2)}, u32[]{:S(2)}) %collective-permute-start.4) | collective-permute-done | bytes 131104 | tf_op jit(solution)/shard_map/ppermute | solution.py:534
  25.6 1.8 %collective-permute-start.6 = (bf16[512,128]{1,0:T(8,128)(2,1)S(1)}, bf16[512,128]{1,0:T(8,128)(2,1)S(1)}, u32[]{:S(2)}, u32[]{:S(2)}) collective-permute-start(bf16[512,128]{1,0:T(8,128)(2,1)S(1)} %add_convert_fusion.1.refs_10_), channel_id=1, source_target_pairs={{4,0},{8,4},{12,8},{0,12},{20,16},{24,20},{28,24},{16,28},{5,1},{9... | collective-permute-start | bytes 393224 | tf_op jit(solution)/shard_map/ppermute | solution.py:534
  27.4 0.2 grads_own.2
  27.6 0.6 %collective-permute-done.5 = bf16[512,128]{1,0:T(8,128)(2,1)S(1)} collective-permute-done((bf16[512,128]{1,0:T(8,128)(2,1)S(1)}, bf16[512,128]{1,0:T(8,128)(2,1)S(1)}, u32[]{:S(2)}, u32[]{:S(2)}) %collective-permute-start.5) | collective-permute-done | bytes 131104 | tf_op jit(solution)/shard_map/ppermute | solution.py:534
  28.3 2.6 %collective-permute-start.7 = (bf16[512,128]{1,0:T(8,128)(2,1)S(1)}, bf16[512,128]{1,0:T(8,128)(2,1)S(1)}, u32[]{:S(2)}, u32[]{:S(2)}) collective-permute-start(bf16[512,128]{1,0:T(8,128)(2,1)S(1)} %add_convert_fusion.refs_10_), channel_id=1, source_target_pairs={{4,0},{8,4},{12,8},{0,12},{20,16},{24,20},{28,24},{16,28},{5,1},{9... | collective-permute-start | bytes 393224 | tf_op jit(solution)/shard_map/ppermute | solution.py:534
  30.8 0.2 grads_own.3
  31.0 0.1 collective-permute-start.9
  31.1 2.2 %collective-permute-done.7.refs_1_ = bf16[512,128]{1,0:T(8,128)(2,1)S(1)} collective-permute-done((bf16[512,128]{1,0:T(8,128)(2,1)S(1)}, bf16[512,128]{1,0:T(8,128)(2,1)S(1)}, u32[]{:S(2)}, u32[]{:S(2)}) %collective-permute-start.7) | collective-permute-done | bytes 131104 | tf_op jit(solution)/shard_map/ppermute | solution.py:534
  33.4 0.1 collective-permute-start.8
  33.5 0.7 %place.2 = (bf16[256,512]{1,0:T(8,128)(2,1)}, bf16[256,512]{1,0:T(8,128)(2,1)}) custom-call(bf16[512,128]{1,0:T(8,128)(2,1)S(1)} %finish.2.refs_2_.mine_ref, bf16[512,128]{1,0:T(8,128)(2,1)S(1)} %collective-permute-done.9.other_ref), custom_call_target="tpu_custom_call" | custom-call | tf_op jit(solution)/shard_map/place/pallas_call | solution.py:740
  34.2 0.6 %collective-permute-done.8.other_ref = bf16[512,128]{1,0:T(8,128)(2,1)S(1)} collective-permute-done((bf16[512,128]{1,0:T(8,128)(2,1)S(1)}, bf16[512,128]{1,0:T(8,128)(2,1)S(1)}, u32[]{:S(2)}, u32[]{:S(2)}) %collective-permute-start.8) | collective-permute-done | bytes 131104 | tf_op jit(solution)/shard_map/ppermute | solution.py:739
  34.8 0.7 %place.3 = (bf16[256,512]{1,0:T(8,128)(2,1)}, bf16[256,512]{1,0:T(8,128)(2,1)}) custom-call(bf16[512,128]{1,0:T(8,128)(2,1)S(1)} %finish.3.mine_ref, bf16[512,128]{1,0:T(8,128)(2,1)S(1)} %collective-permute-done.8.other_ref, bf16[256,512]{1,0:T(8,128)(2,1)} %get-tuple-element.89.refs_0_, ...), custom_call_target="tpu_custom_call", output_to_operand_aliasing={{0}: (2, {}), {1}: (3, {})} | custom-call | tf_op jit(solution)/shard_map/place/pallas_call | solution.py:740
  (9 shorter events, 0.2 us)
Async XLA Ops:
  1.6 0.7 %copy-start = (s32[256]{0:T(256)S(1)}, s32[256]{0:T(256)}, u32[]{:S(2)}) copy-start(s32[256]{0:T(256)} %param.9) | copy-start | bytes 3076
  2.4 9.5 %collective-permute-start = (bf16[528,128]{1,0:T(8,128)(2,1)S(1)}, bf16[528,128]{1,0:T(8,128)(2,1)S(1)}, u32[]{:S(2)}, u32[]{:S(2)}) collective-permute-start(bf16[528,128]{1,0:T(8,128)(2,1)S(1)} %number.1.own_ref.refs_2_.refs_3_.refs_4_.refs_6_), channel_id=1, source_target_pairs={{0,4},{4,8},{8,12},{12,0},{16,20},{20,24},{24,28},{28,16},{1,5},{5... | collective-permute-start | bytes 405512 | tf_op jit(solution)/shard_map/ppermute | solution.py:534
  5.4 11.1 %collective-permute-start.1 = (bf16[512,128]{1,0:T(8,128)(2,1)S(1)}, bf16[512,128]{1,0:T(8,128)(2,1)S(1)}, u32[]{:S(2)}, u32[]{:S(2)}) collective-permute-start(bf16[512,128]{1,0:T(8,128)(2,1)S(1)} %get-tuple-element.53.refs_3_.refs_7_), channel_id=1, source_target_pairs={{0,4},{4,8},{8,12},{12,0},{16,20},{20,24},{24,28},{28,16},{1,5},{5... | collective-permute-start | bytes 393224 | tf_op jit(solution)/shard_map/ppermute | solution.py:534
  11.9 7.3 %collective-permute-start.3 = (bf16[528,128]{1,0:T(8,128)(2,1)S(1)}, bf16[528,128]{1,0:T(8,128)(2,1)S(1)}, u32[]{:S(2)}, u32[]{:S(2)}) collective-permute-start(bf16[528,128]{1,0:T(8,128)(2,1)S(1)} %collective-permute-done.refs_5_.refs_10_.refs_3_.refs_4_.refs_6_), channel_id=1, source_target_pairs={{0,16},{4,8},{8,12},{12,4},{16,0},{20,24},{24,28},{28,20},{1,17},{... | collective-permute-start | bytes 405512 | tf_op jit(solution)/shard_map/ppermute | solution.py:534
  16.6 6.4 %collective-permute-start.2 = (bf16[512,128]{1,0:T(8,128)(2,1)S(1)}, bf16[512,128]{1,0:T(8,128)(2,1)S(1)}, u32[]{:S(2)}, u32[]{:S(2)}) collective-permute-start(bf16[512,128]{1,0:T(8,128)(2,1)S(1)} %collective-permute-done.1.refs_3_), channel_id=1, source_target_pairs={{0,16},{4,8},{8,12},{12,4},{16,0},{20,24},{24,28},{28,20},{1,17},{... | collective-permute-start | bytes 393224 | tf_op jit(solution)/shard_map/ppermute | solution.py:534
  19.4 6.2 %collective-permute-start.4 = (bf16[512,128]{1,0:T(8,128)(2,1)S(1)}, bf16[512,128]{1,0:T(8,128)(2,1)S(1)}, u32[]{:S(2)}, u32[]{:S(2)}) collective-permute-start(bf16[512,128]{1,0:T(8,128)(2,1)S(1)} %get-tuple-element.66.refs_7_), channel_id=1, source_target_pairs={{16,0},{8,4},{12,8},{4,12},{0,16},{24,20},{28,24},{20,28},{17,1},{... | collective-permute-start | bytes 393224 | tf_op jit(solution)/shard_map/ppermute | solution.py:534
  23.2 5.0 %collective-permute-start.5 = (bf16[512,128]{1,0:T(8,128)(2,1)S(1)}, bf16[512,128]{1,0:T(8,128)(2,1)S(1)}, u32[]{:S(2)}, u32[]{:S(2)}) collective-permute-start(bf16[512,128]{1,0:T(8,128)(2,1)S(1)} %get-tuple-element.71.refs_8_), channel_id=1, source_target_pairs={{16,0},{8,4},{12,8},{4,12},{0,16},{24,20},{28,24},{20,28},{17,1},{... | collective-permute-start | bytes 393224 | tf_op jit(solution)/shard_map/ppermute | solution.py:534
  25.6 5.4 %collective-permute-start.6 = (bf16[512,128]{1,0:T(8,128)(2,1)S(1)}, bf16[512,128]{1,0:T(8,128)(2,1)S(1)}, u32[]{:S(2)}, u32[]{:S(2)}) collective-permute-start(bf16[512,128]{1,0:T(8,128)(2,1)S(1)} %add_convert_fusion.1.refs_10_), channel_id=1, source_target_pairs={{4,0},{8,4},{12,8},{0,12},{20,16},{24,20},{28,24},{16,28},{5,1},{9... | collective-permute-start | bytes 393224 | tf_op jit(solution)/shard_map/ppermute | solution.py:534
  28.3 5.1 %collective-permute-start.7 = (bf16[512,128]{1,0:T(8,128)(2,1)S(1)}, bf16[512,128]{1,0:T(8,128)(2,1)S(1)}, u32[]{:S(2)}, u32[]{:S(2)}) collective-permute-start(bf16[512,128]{1,0:T(8,128)(2,1)S(1)} %add_convert_fusion.refs_10_), channel_id=1, source_target_pairs={{4,0},{8,4},{12,8},{0,12},{20,16},{24,20},{28,24},{16,28},{5,1},{9... | collective-permute-start | bytes 393224 | tf_op jit(solution)/shard_map/ppermute | solution.py:534
  31.0 2.4 %collective-permute-start.9 = (bf16[512,128]{1,0:T(8,128)(2,1)S(1)}, bf16[512,128]{1,0:T(8,128)(2,1)S(1)}, u32[]{:S(2)}, u32[]{:S(2)}) collective-permute-start(bf16[512,128]{1,0:T(8,128)(2,1)S(1)} %finish.2.refs_2_.mine_ref), channel_id=1, source_target_pairs={{0,1},{1,0},{2,3},{3,2},{4,5},{5,4},{6,7},{7,6},{8,9},{9,8},{10,11... | collective-permute-start | bytes 393224 | tf_op jit(solution)/shard_map/ppermute | solution.py:739
  33.4 1.4 %collective-permute-start.8 = (bf16[512,128]{1,0:T(8,128)(2,1)S(1)}, bf16[512,128]{1,0:T(8,128)(2,1)S(1)}, u32[]{:S(2)}, u32[]{:S(2)}) collective-permute-start(bf16[512,128]{1,0:T(8,128)(2,1)S(1)} %finish.3.mine_ref), channel_id=1, source_target_pairs={{0,1},{1,0},{2,3},{3,2},{4,5},{5,4},{6,7},{7,6},{8,9},{9,8},{10,11... | collective-permute-start | bytes 393224 | tf_op jit(solution)/shard_map/ppermute | solution.py:739

commit v6 on v5

--- a/solution.py
+++ b/solution.py
@@ -282,7 +282,7 @@
         for part, value in enumerate(finals((stats_ref[0], stats_ref[1], stats_ref[2]))):
             final_ref[part] = value
         own_run(
-            (q_ref, g_ref, own_kv_ref, final_ref, None, own_bias_ref), outs[1:3], scratch[1:],
+            (q_ref, g_ref, own_kv_ref, final_ref, (), own_bias_ref), outs[1:3], scratch[1:],
             early_own, per_kv, factor, scale,
         )
 
@@ -372,7 +372,7 @@
 
 
 def grads_kernel(ins, outs, scratch, *, chunk, per_kv, factor, step):
-    q_ref, g_ref, own_seg_ref, kv_ref, kv_seg_ref, in_ref, dq_in_ref, bias_ref = ins
+    q_ref, g_ref, own_seg_ref, kv_ref, kv_seg_ref, in_ref, *dq_in_refs, bias_ref = ins
     kv_grad_ref, dq_ref = outs
     kt_ref = scratch[0]
     rows = q_ref.shape[0]
@@ -388,7 +388,8 @@
             unit.lowered(unit.row(in_ref, 0), unit.row(in_ref, 1), factor)
             grads.add(unit)
             head = unit.parts[0][0]
-            dq_ref[head] = dq_in_ref[head] + times(kt_ref[:, unit.keys], unit.dscores)
+            dq = times(kt_ref[:, unit.keys], unit.dscores)
+            dq_ref[head] = dq_in_refs[0][head] + dq if dq_in_refs else dq
 
         in_turn(full_units(per_kv, rows), make, handle, AHEAD)
         grads.finish()
@@ -399,11 +400,11 @@
     @pl.when(jnp.logical_not(active))
     def _():
         kv_grad_ref[...] = jnp.zeros_like(kv_grad_ref)
-        dq_ref[...] = dq_in_ref[...]
+        dq_ref[...] = dq_in_refs[0][...] if dq_in_refs else jnp.zeros_like(dq_ref)
 
 
 def own_run(ins, outs, scratch, chunk, per_kv, factor, scale):
-    q_ref, g_ref, kv_ref, in_ref, dq_in_ref, bias_ref = ins
+    q_ref, g_ref, kv_ref, in_ref, dq_in_refs, bias_ref = ins
     kv_grad_ref, query_grad_ref = outs
     kt_ref, turned_ref, sems = scratch
     rows = q_ref.shape[0]
@@ -426,7 +427,9 @@
         dq = times(kt_ref[:, unit.keys], unit.dscores)
         head = unit.parts[0][0]
         if unit.keys.start == 0:
-            dq_now[head] = dq if dq_in_ref is None else dq_in_ref[head] + dq
+            for ref in dq_in_refs:
+                dq = dq + ref[head]
+            dq_now[head] = dq
             return
         for (other, _), piece in zip(unit.parts, unit.split(dq)):
             total = dq_now.pop(other)
@@ -445,12 +448,13 @@
         copy.wait()
 
 
-def own_kernel(ins, outs, scratch, *, done_before, chunk, per_kv, factor, scale):
-    q_ref, g_ref, own_seg_ref, kv_ref, kv_seg_ref, in_ref, dq_in_ref, bias_ref = ins[:8]
+def own_kernel(ins, outs, scratch, *, terms, done_before, chunk, per_kv, factor, scale):
+    q_ref, g_ref, own_seg_ref, kv_ref, kv_seg_ref, in_ref = ins[:6]
+    dq_in_refs, bias_ref = ins[6 : 6 + terms], ins[6 + terms]
 
     def run():
         own_run(
-            (q_ref, g_ref, kv_ref, in_ref, dq_in_ref, bias_ref), outs, scratch,
+            (q_ref, g_ref, kv_ref, in_ref, dq_in_refs, bias_ref), outs, scratch,
             chunk, per_kv, factor, scale,
         )
 
@@ -462,7 +466,7 @@
 
     @pl.when(jnp.logical_not(active))
     def _():
-        outs[0][...] = ins[8][...]
+        outs[0][...] = ins[7 + terms][...]
 
 
 def finish_kernel(ins, outs, _, *, scale):
@@ -533,7 +537,7 @@
     def moved(array, route):
         return lax.ppermute(array, ("groups", "ctx"), route)
 
-    def call(body, operands, outs, scratch, name, micros, out_specs=None, into=(), after=()):
+    def call(body, operands, outs, scratch, name, micros, out_specs=None, into=(), after=(), same=()):
         count = len(operands)
         extra = [array for array, _ in into] + list(after)
         specs = [out_specs[index] for _, index in into] + [ANYWHERE] * len(after)
@@ -548,7 +552,7 @@
             in_specs=[WHOLE] * count + specs,
             out_specs=out_specs or (WHOLE,) * len(outs),
             scratch_shapes=scratch,
-            input_output_aliases={count + place: index for place, (_, index) in enumerate(into)},
+            input_output_aliases={count + place: index for place, (_, index) in enumerate(into)} | dict(same),
             compiler_params=pltpu.CompilerParams(vmem_limit_bytes=VMEM_LIMIT),
             cost_estimate=pl.CostEstimate(
                 flops=int(1153e6 * micros * HINT), bytes_accessed=4 * pairs // rows, transcendentals=pairs
@@ -657,7 +661,7 @@
             block_stats(chunk, step, 1 if early and step == 1 and chunk == 1 else None)
 
     def far_grads(chunk, before):
-        final_stats[chunk], sums[chunk], dq[chunk] = with_bias(
+        final_stats[chunk], sums[chunk], *dq[chunk] = with_bias(
             far_kernel, chunk, reach, (stats[chunk],), (finals_shape, sent_shape, dq_shape),
             [turned, total_sum], "grads_far", 1.3, before,
         )
@@ -665,21 +669,25 @@
 
     def block_grads(chunk, step, before):
         body = functools.partial(grads_kernel, chunk=chunk, step=step, **common)
-        operands = common_operands(chunk, step) + (final_stats[chunk], dq[chunk], biases[step])
-        mine[chunk], dq[chunk] = call(
+        so_far = tuple(dq[chunk]) if step > 1 else ()
+        operands = common_operands(chunk, step) + (final_stats[chunk],) + so_far + (biases[step],)
+        mine[chunk], term = call(
             body, operands, (kv_grad_shape, dq_shape), [turned], "grads", 1.6, after=before
         )
+        dq[chunk] = [term] if step > 1 else dq[chunk] + [term]
         return [mine[chunk]]
 
     def own_grads(chunk):
         done_before = finished[chunk] is not None
-        body = functools.partial(own_kernel, done_before=done_before, chunk=chunk, scale=scale, **common)
+        body = functools.partial(
+            own_kernel, terms=len(dq[chunk]), done_before=done_before, chunk=chunk, scale=scale, **common
+        )
         into = [(query_grad.pop(), 1)] if query_grad else []
         seen = 1 if done_before else 0
         finished[chunk], written = call(
             body,
             (queries, out_grad, own[0], blocks[chunk][0], blocks[0][seen])
-            + (final_stats[chunk], dq[chunk], biases[0])
+            + (final_stats[chunk], *dq[chunk], biases[0])
             + ((finished[chunk],) if done_before else ()),
             own_outs,
             own_scratch,

time: 35.9 us -> 36 us (level)
  no operation moved by 1% of the time
where the time goes in v6:
time: 36 us; the launch traced here: 35.6 us
  starting transfers between devices  13.3 us (37%)
  Pallas kernels  11.8 us (33%)
  waiting for transfers between devices  8.81 us (24%)
  between operations  0.98 us (3%)
  local copies, waits for them, and re-layouts  0.67 us (2%)
    ppermute x8, starting transfers between devices, moved(): return lax.ppermute(array, ('groups', 'ctx'), route)  13.2 us
    ppermute x8, waiting for transfers between devices, moved(): return lax.ppermute(array, ('groups', 'ctx'), route)  8.23 us
    pallas_call x12, Pallas kernels, call(): pl.pallas_call(kernel, out_shape=outs, in_specs=[WHOLE] * count + specs,...  7.54 us
    pallas_call x1, Pallas kernels, shards(): pl.pallas_call(load_kernel, out_shape=(rows_shape, rows_shape), in_specs=...  1.73 us
    pallas_call x2, Pallas kernels, shards(): pl.pallas_call(functools.partial(place_kernel, chunk=chunk, chunks=chunks...  1.46 us
    pallas_call x1, Pallas kernels, shards(): pl.pallas_call(functools.partial(pack_kernel, first_of=first_of), out_sha...  0.99 us
  transfers between devices with their start and end apart: 10, of which 6 were waited for; matrix products, arithmetic and copies ran while one was open for 0% of the time, Pallas kernels for 28%

profile of v6, /device:TPU:0, one launch (start us, length us, event | category | flops | bytes accessed | tf_op | source)
XLA Modules:
  0.0 35.6 jit_solution(15369527284500929286)
XLA Ops:
  0.6 1.0 %pack.1 = (bf16[528,128]{1,0:T(8,128)(2,1)S(1)}, bf16[512,128]{1,0:T(8,128)(2,1)S(1)}) custom-call(bf16[256,512]{1,0:T(8,128)(2,1)} %k_ref.1, bf16[256,512]{1,0:T(8,128)(2,1)} %v_ref.1), custom_call_target="tpu_custom_call" | custom-call | bytes 4194304 | tf_op jit(solution)/shard_map/pack/pallas_call | solution.py:563
  1.6 0.0 copy-start
  1.6 0.7 %copy-done = s32[256]{0:T(256)S(1)} copy-done((s32[256]{0:T(256)S(1)}, s32[256]{0:T(256)}, u32[]{:S(2)}) %copy-start) | copy-done | bytes 1048
  2.4 3.1 %collective-permute-start = (bf16[528,128]{1,0:T(8,128)(2,1)S(1)}, bf16[528,128]{1,0:T(8,128)(2,1)S(1)}, u32[]{:S(2)}, u32[]{:S(2)}) collective-permute-start(bf16[528,128]{1,0:T(8,128)(2,1)S(1)} %number.1.own_ref.refs_2_.refs_3_.refs_4_.refs_6_), channel_id=1, source_target_pairs={{0,4},{4,8},{8,12},{12,0},{16,20},{20,24},{24,28},{28,16},{1,5},{5... | collective-permute-start | bytes 405512 | tf_op jit(solution)/shard_map/ppermute | solution.py:538
  5.4 1.6 %collective-permute-start.1 = (bf16[512,128]{1,0:T(8,128)(2,1)S(1)}, bf16[512,128]{1,0:T(8,128)(2,1)S(1)}, u32[]{:S(2)}, u32[]{:S(2)}) collective-permute-start(bf16[512,128]{1,0:T(8,128)(2,1)S(1)} %get-tuple-element.53.refs_3_.refs_7_), channel_id=1, source_target_pairs={{0,4},{4,8},{8,12},{12,0},{16,20},{20,24},{24,28},{28,16},{1,5},{5... | collective-permute-start | bytes 393224 | tf_op jit(solution)/shard_map/ppermute | solution.py:538
  7.0 1.7 %load.1 = (bf16[256,2048]{1,0:T(8,128)(2,1)S(1)}, bf16[256,2048]{1,0:T(8,128)(2,1)S(1)}) custom-call(bf16[256,2048]{1,0:T(8,128)(2,1)} %q_ref.1, bf16[256,2048]{1,0:T(8,128)(2,1)} %g_ref.1, bf16[528,128]{1,0:T(8,128)(2,1)S(1)} %number.1.own_ref.refs_2_.refs_3_.refs_4_.refs_6_), custom_call_target="tpu_custom_call" | custom-call | tf_op jit(solution)/shard_map/load/pallas_call | solution.py:585
  8.7 0.9 %stats_own.2 = (f32[3,8,256]{2,1,0:T(8,128)S(1)}, f32[256,256]{1,0:T(8,128)S(1)}) custom-call(bf16[256,2048]{1,0:T(8,128)(2,1)S(1)} %get-tuple-element.49.refs_0_, bf16[256,2048]{1,0:T(8,128)(2,1)S(1)} %get-tuple-element.50.refs_1_, bf16[528,128]{1,0:T(8,128)(2,1)S(1)} %number.1.own_ref.refs_2_.refs_3_.refs_4_.refs_6_, ...), custom_call_target="tpu_custom_call" | custom-call | flops 230600000 | bytes 8192 | tf_op jit(solution)/shard_map/stats_own/pallas_call | solution.py:549
  9.7 2.2 %collective-permute-done.refs_5_.refs_10_.refs_3_.refs_4_.refs_6_ = bf16[528,128]{1,0:T(8,128)(2,1)S(1)} collective-permute-done((bf16[528,128]{1,0:T(8,128)(2,1)S(1)}, bf16[528,128]{1,0:T(8,128)(2,1)S(1)}, u32[]{:S(2)}, u32[]{:S(2)}) %collective-permute-start) | collective-permute-done | bytes 135200 | tf_op jit(solution)/shard_map/ppermute | solution.py:538
  11.9 1.8 %collective-permute-start.3 = (bf16[528,128]{1,0:T(8,128)(2,1)S(1)}, bf16[528,128]{1,0:T(8,128)(2,1)S(1)}, u32[]{:S(2)}, u32[]{:S(2)}) collective-permute-start(bf16[528,128]{1,0:T(8,128)(2,1)S(1)} %collective-permute-done.refs_5_.refs_10_.refs_3_.refs_4_.refs_6_), channel_id=1, source_target_pairs={{0,16},{4,8},{8,12},{12,4},{16,0},{20,24},{24,28},{28,20},{1,17},{... | collective-permute-start | bytes 405512 | tf_op jit(solution)/shard_map/ppermute | solution.py:538
  13.6 2.9 %stats_own.3 = (f32[3,8,256]{2,1,0:T(8,128)S(1)}, f32[512,128]{1,0:T(8,128)S(1)}, bf16[256,2048]{1,0:T(8,128)(2,1)}) custom-call(bf16[256,2048]{1,0:T(8,128)(2,1)S(1)} %get-tuple-element.49.refs_0_, bf16[256,2048]{1,0:T(8,128)(2,1)S(1)} %get-tuple-element.50.refs_1_, bf16[528,128]{1,0:T(8,128)(2,1)S(1)} %number.1.own_ref.refs_2_.refs_3_.refs_4_.refs_6_, ...), custom_call_target="tpu_custom_call" | custom-call | flops 230600000 | bytes 8192 | tf_op jit(solution)/shard_map/stats_own/pallas_call | solution.py:549
  16.6 0.3 collective-permute-start.2
  16.9 0.1 stats.2
  17.0 2.2 %stats.3 = (f32[3,8,256]{2,1,0:T(8,128)S(1)}, f32[512,128]{1,0:T(8,128)S(1)}, bf16[256,2048]{1,0:T(8,128)(2,1)}) custom-call(bf16[256,2048]{1,0:T(8,128)(2,1)S(1)} %get-tuple-element.49.refs_0_, bf16[256,2048]{1,0:T(8,128)(2,1)S(1)} %get-tuple-element.50.refs_1_, ...), custom_call_target="tpu_custom_call", output_to_operand_aliasing={{2}: (11, {})} | custom-call | flops 230600000 | bytes 8192 | tf_op jit(solution)/shard_map/stats/pallas_call | solution.py:549
  19.2 0.2 grads_far.2
  19.4 1.8 %collective-permute-start.4 = (bf16[512,128]{1,0:T(8,128)(2,1)S(1)}, bf16[512,128]{1,0:T(8,128)(2,1)S(1)}, u32[]{:S(2)}, u32[]{:S(2)}) collective-permute-start(bf16[512,128]{1,0:T(8,128)(2,1)S(1)} %get-tuple-element.66.refs_7_), channel_id=1, source_target_pairs={{16,0},{8,4},{12,8},{4,12},{0,16},{24,20},{28,24},{20,28},{17,1},{... | collective-permute-start | bytes 393224 | tf_op jit(solution)/shard_map/ppermute | solution.py:538
  21.3 1.7 %collective-permute-done.2.refs_3_ = bf16[512,128]{1,0:T(8,128)(2,1)S(1)} collective-permute-done((bf16[512,128]{1,0:T(8,128)(2,1)S(1)}, bf16[512,128]{1,0:T(8,128)(2,1)S(1)}, u32[]{:S(2)}, u32[]{:S(2)}) %collective-permute-start.2) | collective-permute-done | bytes 131104 | tf_op jit(solution)/shard_map/ppermute | solution.py:538
  23.0 0.2 grads_far.3
  23.2 0.1 collective-permute-start.5
  23.3 0.4 %grads.2 = (f32[512,128]{1,0:T(8,128)S(1)}, f32[8,128,256]{2,1,0:T(8,128)S(1)}) custom-call(bf16[256,2048]{1,0:T(8,128)(2,1)S(1)} %get-tuple-element.49.refs_0_, bf16[256,2048]{1,0:T(8,128)(2,1)S(1)} %get-tuple-element.50.refs_1_, bf16[528,128]{1,0:T(8,128)(2,1)S(1)} %number.1.own_ref.refs_2_.refs_3_.refs_4_.refs_6_, ...), custom_call_target="tpu_custom_call" | custom-call | flops 368960000 | bytes 8192 | tf_op jit(solution)/shard_map/grads/pallas_call | solution.py:549
  23.7 0.2 grads.3
  23.9 1.7 %collective-permute-done.4 = bf16[512,128]{1,0:T(8,128)(2,1)S(1)} collective-permute-done((bf16[512,128]{1,0:T(8,128)(2,1)S(1)}, bf16[512,128]{1,0:T(8,128)(2,1)S(1)}, u32[]{:S(2)}, u32[]{:S(2)}) %collective-permute-start.4) | collective-permute-done | bytes 131104 | tf_op jit(solution)/shard_map/ppermute | solution.py:538
  25.6 2.1 %collective-permute-start.6 = (bf16[512,128]{1,0:T(8,128)(2,1)S(1)}, bf16[512,128]{1,0:T(8,128)(2,1)S(1)}, u32[]{:S(2)}, u32[]{:S(2)}) collective-permute-start(bf16[512,128]{1,0:T(8,128)(2,1)S(1)} %add_convert_fusion.1.refs_11_), channel_id=1, source_target_pairs={{4,0},{8,4},{12,8},{0,12},{20,16},{24,20},{28,24},{16,28},{5,1},{9... | collective-permute-start | bytes 393224 | tf_op jit(solution)/shard_map/ppermute | solution.py:538
  27.8 0.2 grads_own.2
  27.9 0.3 collective-permute-done.5
  28.3 2.5 %collective-permute-start.7 = (bf16[512,128]{1,0:T(8,128)(2,1)S(1)}, bf16[512,128]{1,0:T(8,128)(2,1)S(1)}, u32[]{:S(2)}, u32[]{:S(2)}) collective-permute-start(bf16[512,128]{1,0:T(8,128)(2,1)S(1)} %add_convert_fusion.refs_11_), channel_id=1, source_target_pairs={{4,0},{8,4},{12,8},{0,12},{20,16},{24,20},{28,24},{16,28},{5,1},{9... | collective-permute-start | bytes 393224 | tf_op jit(solution)/shard_map/ppermute | solution.py:538
  30.7 0.2 grads_own.3
  30.9 0.1 collective-permute-start.9
  31.0 2.3 %collective-permute-done.7.refs_1_ = bf16[512,128]{1,0:T(8,128)(2,1)S(1)} collective-permute-done((bf16[512,128]{1,0:T(8,128)(2,1)S(1)}, bf16[512,128]{1,0:T(8,128)(2,1)S(1)}, u32[]{:S(2)}, u32[]{:S(2)}) %collective-permute-start.7) | collective-permute-done | bytes 131104 | tf_op jit(solution)/shard_map/ppermute | solution.py:538
  33.3 0.1 collective-permute-start.8
  33.4 0.7 %place.2 = (bf16[256,512]{1,0:T(8,128)(2,1)}, bf16[256,512]{1,0:T(8,128)(2,1)}) custom-call(bf16[512,128]{1,0:T(8,128)(2,1)S(1)} %finish.2.refs_2_.mine_ref, bf16[512,128]{1,0:T(8,128)(2,1)S(1)} %collective-permute-done.9.other_ref), custom_call_target="tpu_custom_call" | custom-call | tf_op jit(solution)/shard_map/place/pallas_call | solution.py:748
  34.2 0.6 %collective-permute-done.8.other_ref = bf16[512,128]{1,0:T(8,128)(2,1)S(1)} collective-permute-done((bf16[512,128]{1,0:T(8,128)(2,1)S(1)}, bf16[512,128]{1,0:T(8,128)(2,1)S(1)}, u32[]{:S(2)}, u32[]{:S(2)}) %collective-permute-start.8) | collective-permute-done | bytes 131104 | tf_op jit(solution)/shard_map/ppermute | solution.py:747
  34.7 0.7 %place.3 = (bf16[256,512]{1,0:T(8,128)(2,1)}, bf16[256,512]{1,0:T(8,128)(2,1)}) custom-call(bf16[512,128]{1,0:T(8,128)(2,1)S(1)} %finish.3.mine_ref, bf16[512,128]{1,0:T(8,128)(2,1)S(1)} %collective-permute-done.8.other_ref, bf16[256,512]{1,0:T(8,128)(2,1)} %get-tuple-element.89.refs_0_, ...), custom_call_target="tpu_custom_call", output_to_operand_aliasing={{0}: (2, {}), {1}: (3, {})} | custom-call | tf_op jit(solution)/shard_map/place/pallas_call | solution.py:748
  (9 shorter events, 0.2 us)
Async XLA Ops:
  1.6 0.7 %copy-start = (s32[256]{0:T(256)S(1)}, s32[256]{0:T(256)}, u32[]{:S(2)}) copy-start(s32[256]{0:T(256)} %param.9) | copy-start | bytes 3076
  2.4 9.5 %collective-permute-start = (bf16[528,128]{1,0:T(8,128)(2,1)S(1)}, bf16[528,128]{1,0:T(8,128)(2,1)S(1)}, u32[]{:S(2)}, u32[]{:S(2)}) collective-permute-start(bf16[528,128]{1,0:T(8,128)(2,1)S(1)} %number.1.own_ref.refs_2_.refs_3_.refs_4_.refs_6_), channel_id=1, source_target_pairs={{0,4},{4,8},{8,12},{12,0},{16,20},{20,24},{24,28},{28,16},{1,5},{5... | collective-permute-start | bytes 405512 | tf_op jit(solution)/shard_map/ppermute | solution.py:538
  5.4 11.1 %collective-permute-start.1 = (bf16[512,128]{1,0:T(8,128)(2,1)S(1)}, bf16[512,128]{1,0:T(8,128)(2,1)S(1)}, u32[]{:S(2)}, u32[]{:S(2)}) collective-permute-start(bf16[512,128]{1,0:T(8,128)(2,1)S(1)} %get-tuple-element.53.refs_3_.refs_7_), channel_id=1, source_target_pairs={{0,4},{4,8},{8,12},{12,0},{16,20},{20,24},{24,28},{28,16},{1,5},{5... | collective-permute-start | bytes 393224 | tf_op jit(solution)/shard_map/ppermute | solution.py:538
  11.9 7.4 %collective-permute-start.3 = (bf16[528,128]{1,0:T(8,128)(2,1)S(1)}, bf16[528,128]{1,0:T(8,128)(2,1)S(1)}, u32[]{:S(2)}, u32[]{:S(2)}) collective-permute-start(bf16[528,128]{1,0:T(8,128)(2,1)S(1)} %collective-permute-done.refs_5_.refs_10_.refs_3_.refs_4_.refs_6_), channel_id=1, source_target_pairs={{0,16},{4,8},{8,12},{12,4},{16,0},{20,24},{24,28},{28,20},{1,17},{... | collective-permute-start | bytes 405512 | tf_op jit(solution)/shard_map/ppermute | solution.py:538
  16.6 6.4 %collective-permute-start.2 = (bf16[512,128]{1,0:T(8,128)(2,1)S(1)}, bf16[512,128]{1,0:T(8,128)(2,1)S(1)}, u32[]{:S(2)}, u32[]{:S(2)}) collective-permute-start(bf16[512,128]{1,0:T(8,128)(2,1)S(1)} %collective-permute-done.1.refs_3_), channel_id=1, source_target_pairs={{0,16},{4,8},{8,12},{12,4},{16,0},{20,24},{24,28},{28,20},{1,17},{... | collective-permute-start | bytes 393224 | tf_op jit(solution)/shard_map/ppermute | solution.py:538
  19.4 6.1 %collective-permute-start.4 = (bf16[512,128]{1,0:T(8,128)(2,1)S(1)}, bf16[512,128]{1,0:T(8,128)(2,1)S(1)}, u32[]{:S(2)}, u32[]{:S(2)}) collective-permute-start(bf16[512,128]{1,0:T(8,128)(2,1)S(1)} %get-tuple-element.66.refs_7_), channel_id=1, source_target_pairs={{16,0},{8,4},{12,8},{4,12},{0,16},{24,20},{28,24},{20,28},{17,1},{... | collective-permute-start | bytes 393224 | tf_op jit(solution)/shard_map/ppermute | solution.py:538
  23.2 5.0 %collective-permute-start.5 = (bf16[512,128]{1,0:T(8,128)(2,1)S(1)}, bf16[512,128]{1,0:T(8,128)(2,1)S(1)}, u32[]{:S(2)}, u32[]{:S(2)}) collective-permute-start(bf16[512,128]{1,0:T(8,128)(2,1)S(1)} %get-tuple-element.70.refs_7_), channel_id=1, source_target_pairs={{16,0},{8,4},{12,8},{4,12},{0,16},{24,20},{28,24},{20,28},{17,1},{... | collective-permute-start | bytes 393224 | tf_op jit(solution)/shard_map/ppermute | solution.py:538
  25.6 5.3 %collective-permute-start.6 = (bf16[512,128]{1,0:T(8,128)(2,1)S(1)}, bf16[512,128]{1,0:T(8,128)(2,1)S(1)}, u32[]{:S(2)}, u32[]{:S(2)}) collective-permute-start(bf16[512,128]{1,0:T(8,128)(2,1)S(1)} %add_convert_fusion.1.refs_11_), channel_id=1, source_target_pairs={{4,0},{8,4},{12,8},{0,12},{20,16},{24,20},{28,24},{16,28},{5,1},{9... | collective-permute-start | bytes 393224 | tf_op jit(solution)/shard_map/ppermute | solution.py:538
  28.3 5.0 %collective-permute-start.7 = (bf16[512,128]{1,0:T(8,128)(2,1)S(1)}, bf16[512,128]{1,0:T(8,128)(2,1)S(1)}, u32[]{:S(2)}, u32[]{:S(2)}) collective-permute-start(bf16[512,128]{1,0:T(8,128)(2,1)S(1)} %add_convert_fusion.refs_11_), channel_id=1, source_target_pairs={{4,0},{8,4},{12,8},{0,12},{20,16},{24,20},{28,24},{16,28},{5,1},{9... | collective-permute-start | bytes 393224 | tf_op jit(solution)/shard_map/ppermute | solution.py:538
  30.9 2.5 %collective-permute-start.9 = (bf16[512,128]{1,0:T(8,128)(2,1)S(1)}, bf16[512,128]{1,0:T(8,128)(2,1)S(1)}, u32[]{:S(2)}, u32[]{:S(2)}) collective-permute-start(bf16[512,128]{1,0:T(8,128)(2,1)S(1)} %finish.2.refs_2_.mine_ref), channel_id=1, source_target_pairs={{0,1},{1,0},{2,3},{3,2},{4,5},{5,4},{6,7},{7,6},{8,9},{9,8},{10,11... | collective-permute-start | bytes 393224 | tf_op jit(solution)/shard_map/ppermute | solution.py:747
  33.3 1.4 %collective-permute-start.8 = (bf16[512,128]{1,0:T(8,128)(2,1)S(1)}, bf16[512,128]{1,0:T(8,128)(2,1)S(1)}, u32[]{:S(2)}, u32[]{:S(2)}) collective-permute-start(bf16[512,128]{1,0:T(8,128)(2,1)S(1)} %finish.3.mine_ref), channel_id=1, source_target_pairs={{0,1},{1,0},{2,3},{3,2},{4,5},{5,4},{6,7},{7,6},{8,9},{9,8},{10,11... | collective-permute-start | bytes 393224 | tf_op jit(solution)/shard_map/ppermute | solution.py:747
